TPU v7x, 32 devices: a whole 2x2x4 slice. The times are simulated.
32 devices in a mesh: tm: 4 (over z), height: 2 (over x), width: 4 (over y, core).
Axes of the slice: x: 2, y: 2, z: 4, core: 2. Of those that a mesh axis runs over, the one named last changes fastest.
Arguments:
- video_in: bfloat16 [16, 16, 6144], P('tm', 'height', 'width'), may hold values from -24 to 24
- gain_first: float32 [96], replicated, may hold values from 0.5 to 2
- gain_second: float32 [192], replicated, may hold values from 0.5 to 2
- conv_first: bfloat16 [3, 3, 3, 96, 192], replicated, may hold values from -0.125 to 0.125
- conv_second: bfloat16 [3, 3, 3, 192, 192], replicated, may hold values from -0.078125 to 0.078125
- shortcut: bfloat16 [96, 192], replicated, may hold values from -0.625 to 0.625
- downscale_weight: bfloat16 [3, 3, 192, 192], replicated, may hold values from -0.15625 to 0.15625
Outputs:
- encoded: bfloat16 [16, 8, 6144], P('tm', 'height', 'width')
All inputs are finite; a program needn't handle non-finite values.
Results may differ from a plain program's by a relative error of at most 0.0054.
Values may be sent and summed in bfloat16 or wider, within the bound.
No kernel may reach another device: no remote copies, remote signals or barrier semaphores. Data moves between devices by JAX's collectives and lax.ppermute only.
A program may use at most 64 MiB of HBM per device.

v0:
```python
import jax
import jax.numpy as jnp
from jax import lax
from jax.sharding import PartitionSpec as P

epsilon = 1e-06


def shifted(value, axis, by):
    devices = lax.axis_size(axis)
    pairs = [(i, i + by) for i in range(devices) if 0 <= i + by < devices]
    return lax.ppermute(value, axis, pairs)


def padded(block, sides, width):
    for axis, dim in sides:
        count = lax.axis_size(axis)
        forward = [(i, i + 1) for i in range(count - 1)]
        backward = [(target, source) for source, target in forward]
        low = lax.ppermute(
            lax.slice_in_dim(block, block.shape[dim] - width, None, axis=dim), axis, forward
        )
        high = lax.ppermute(lax.slice_in_dim(block, 0, width, axis=dim), axis, backward)
        block = jnp.concatenate([low, block, high], axis=dim)
    return block


def activate(feature_values, gain):
    feature_values = feature_values.astype(jnp.float32)
    meansq = jnp.mean(feature_values * feature_values, axis=-1, keepdims=True)
    normed = feature_values * lax.rsqrt(meansq + epsilon) * gain
    return jax.nn.silu(normed).astype(jnp.bfloat16)


def convolve(border_filled, filter_weight):
    frames = border_filled.shape[0] - 2
    rows = border_filled.shape[1] - 2
    cols = border_filled.shape[2] - 2
    c_in = border_filled.shape[3]
    c_out = filter_weight.shape[4]
    total = jnp.zeros((frames * rows * cols, c_out), jnp.float32)
    for depth_tap in range(3):
        for row_tap in range(3):
            window_slab = border_filled[depth_tap : depth_tap + frames, row_tap : row_tap + rows]
            stacked = jnp.concatenate(
                [window_slab[:, :, col_tap : col_tap + cols] for col_tap in range(3)], axis=-1
            )
            total = total + jnp.dot(
                stacked.reshape(-1, 3 * c_in),
                filter_weight[depth_tap, row_tap].reshape(3 * c_in, c_out),
                preferred_element_type=jnp.float32,
            )
    return total.reshape(frames, rows, cols, c_out)


def halve_spatial(border_filled, filter_weight):
    frames = border_filled.shape[0]
    out_rows = (border_filled.shape[1] - 1) // 2
    out_cols = (border_filled.shape[2] - 1) // 2
    chans = border_filled.shape[3]
    total = jnp.zeros((frames * out_rows * out_cols, filter_weight.shape[3]), jnp.float32)
    for row_tap in range(3):
        stacked = jnp.concatenate(
            [
                border_filled[
                    :, row_tap : row_tap + 2 * out_rows : 2, col_tap : col_tap + 2 * out_cols : 2
                ]
                for col_tap in range(3)
            ],
            axis=-1,
        )
        total = total + jnp.dot(
            stacked.reshape(-1, 3 * chans),
            filter_weight[row_tap].reshape(3 * chans, filter_weight.shape[3]),
            preferred_element_type=jnp.float32,
        )
    return total.reshape(frames, out_rows, out_cols, filter_weight.shape[3])


def local(video_in, gain_first, gain_second, conv_first, conv_second, shortcut, downscale_weight):
    frames, rows, merged_cols = video_in.shape
    c_in = gain_first.shape[0]
    c_out = gain_second.shape[0]
    cols = merged_cols // c_in
    field = video_in.reshape(frames, rows, cols, c_in)
    first = activate(field, gain_first)
    earlier = shifted(first[frames - 2 :], "tm", 1)
    framed = jnp.concatenate([earlier, first], axis=0)
    border_filled = padded(framed, (("height", 1), ("width", 2)), 1)
    hidden = convolve(border_filled, conv_first)
    second = activate(hidden, gain_second)
    earlier_mid = shifted(second[frames - 2 :], "tm", 1)
    framed_mid = jnp.concatenate([earlier_mid, second], axis=0)
    padded_mid = padded(framed_mid, (("height", 1), ("width", 2)), 1)
    branch = convolve(padded_mid, conv_second)
    skip_term = jnp.dot(
        field.reshape(-1, c_in), shortcut, preferred_element_type=jnp.float32
    ).reshape(frames, rows, cols, c_out)
    merged = (branch + skip_term).astype(jnp.bfloat16)
    next_col = shifted(merged[:, :, :1], "width", -1)
    widened = jnp.concatenate([merged, next_col], axis=2)
    next_row = shifted(widened[:, :1], "height", -1)
    border_filled_output = jnp.concatenate([widened, next_row], axis=1)
    block_output = halve_spatial(border_filled_output, downscale_weight)
    return block_output.astype(jnp.bfloat16).reshape(frames, rows // 2, cols // 2 * c_out)


def solution(mesh):
    placed = (P("tm", "height", "width"), P(), P(), P(), P(), P(), P())
    return jax.shard_map(
        local, mesh=mesh, in_specs=placed, out_specs=P("tm", "height", "width"), check_vma=False
    )
```

profile of v0, /device:TPU:0, one launch (start us, length us, event | category | flops | bytes accessed | tf_op | source)
XLA Modules:
  0.0 78.9 jit_solution(9033494974139563480)
XLA Ops:
  0.0 1.1 %reshape.106 = bf16[4,8,16,96]{3,2,1,0:T(8,128)(2,1)S(1)} reshape(bf16[4,8,1536]{2,1,0:T(8,128)(2,1)} %param.7) | data formatting | bytes 196608 | tf_op jit(solution)/shard_map/reshape | solution.py:85
  1.2 0.8 %fusion.13 = bf16[4,8,16,96]{3,2,1,0:T(8,128)(2,1)S(1)} fusion(bf16[4,8,16,96]{3,2,1,0:T(8,128)(2,1)S(1)} %reshape.106, f32[96]{0:T(128)} %param.8, f32[4,8,16]{2,1,0:T(8,128)S(1)} %add_rsqrt_fusion), kind=kLoop, calls=%fused_computation.66 | loop fusion | flops 393216 | bytes 199040 | tf_op jit(solution)/shard_map/convert_element_type | solution.py:32
  2.1 4.9 %collective-permute-start = (bf16[2,8,16,96]{3,2,1,0:T(8,128)(2,1)S(1)}, bf16[2,8,16,96]{3,2,1,0:T(8,128)(2,1)S(1)}, u32[]{:S(2)}, u32[]{:S(2)}) collective-permute-start(bf16[2,8,16,96]{3,2,1,0:T(8,128)(2,1)S(1)} %slice.522), channel_id=1, source_target_pairs={{0,8},{8,16},{16,24},{1,9},{9,17},{17,25},{2,10},{10,18},{18,26},{... | collective-permute-start | bytes 147464 | tf_op jit(solution)/shard_map/ppermute | solution.py:12
  7.0 1.5 %fusion.19 = (bf16[1,1,3,96,192]{4,3,2,1,0:T(8,128)(2,1)S(1)}, bf16[1,1,3,96,192]{4,3,2,1,0:T(8,128)(2,1)S(1)}, bf16[1,1,3,96,192]{4,3,2,1,0:T(8,128)(2,1)S(1)},...) fusion(bf16[3,3,3,96,192]{4,3,2,1,0:T(8,128)(2,1)} %param.10), kind=kLoop, calls=%fused_computation.93 | loop fusion | bytes 1990656 | tf_op jit(solution)/shard_map/slice | solution.py:50
  8.9 3.4 %collective-permute-start.1 = (bf16[6,1,16,96]{3,2,1,0:T(8,128)(2,1)S(1)}, bf16[6,1,16,96]{3,2,1,0:T(8,128)(2,1)S(1)}, u32[]{:S(2)}, u32[]{:S(2)}) collective-permute-start(bf16[6,1,16,96]{3,2,1,0:T(8,128)(2,1)S(1)} %get-tuple-element.90), channel_id=1, source_target_pairs={{0,4},{1,5},{2,6},{3,7},{8,12},{9,13},{10,14},{11,15},{16,20},{17,... | collective-permute-start | bytes 55304 | tf_op jit(solution)/shard_map/ppermute | solution.py:20
  12.3 1.3 %collective-permute-start.2 = (bf16[6,1,16,96]{3,2,1,0:T(8,128)(2,1)S(1)}, bf16[6,1,16,96]{3,2,1,0:T(8,128)(2,1)S(1)}, u32[]{:S(2)}, u32[]{:S(2)}) collective-permute-start(bf16[6,1,16,96]{3,2,1,0:T(8,128)(2,1)S(1)} %get-tuple-element.91), channel_id=1, source_target_pairs={{4,0},{5,1},{6,2},{7,3},{12,8},{13,9},{14,10},{15,11},{20,16},{21,... | collective-permute-start | bytes 55304 | tf_op jit(solution)/shard_map/ppermute | solution.py:23
  13.8 4.2 %collective-permute-done.2 = bf16[6,1,16,96]{3,2,1,0:T(8,128)(2,1)S(1)} collective-permute-done((bf16[6,1,16,96]{3,2,1,0:T(8,128)(2,1)S(1)}, bf16[6,1,16,96]{3,2,1,0:T(8,128)(2,1)S(1)}, u32[]{:S(2)}, u32[]{:S(2)}) %collective-permute-start.2) | collective-permute-done | bytes 18464 | tf_op jit(solution)/shard_map/ppermute | solution.py:23
  18.1 1.3 %collective-permute-start.3 = (bf16[6,10,1,96]{3,2,1,0:T(2,128)(2,1)S(1)}, bf16[6,10,1,96]{3,2,1,0:T(2,128)(2,1)S(1)}, u32[]{:S(2)}, u32[]{:S(2)}) collective-permute-start(bf16[6,10,1,96]{3,2,1,0:T(2,128)(2,1)S(1)} %get-tuple-element.80), channel_id=1, source_target_pairs={{0,1},{1,2},{2,3},{4,5},{5,6},{6,7},{8,9},{9,10},{10,11},{12,13},{... | collective-permute-start | bytes 34568 | tf_op jit(solution)/shard_map/ppermute | solution.py:20
  19.4 1.3 %collective-permute-start.4 = (bf16[6,10,1,96]{3,2,1,0:T(2,128)(2,1)S(1)}, bf16[6,10,1,96]{3,2,1,0:T(2,128)(2,1)S(1)}, u32[]{:S(2)}, u32[]{:S(2)}) collective-permute-start(bf16[6,10,1,96]{3,2,1,0:T(2,128)(2,1)S(1)} %get-tuple-element.81), channel_id=1, source_target_pairs={{1,0},{2,1},{3,2},{5,4},{6,5},{7,6},{9,8},{10,9},{11,10},{13,12},{... | collective-permute-start | bytes 34568 | tf_op jit(solution)/shard_map/ppermute | solution.py:23
  20.9 3.3 %collective-permute-done.4 = bf16[6,10,1,96]{3,2,1,0:T(2,128)(2,1)S(1)} collective-permute-done((bf16[6,10,1,96]{3,2,1,0:T(2,128)(2,1)S(1)}, bf16[6,10,1,96]{3,2,1,0:T(2,128)(2,1)S(1)}, u32[]{:S(2)}, u32[]{:S(2)}) %collective-permute-start.4) | collective-permute-done | bytes 11552 | tf_op jit(solution)/shard_map/ppermute | solution.py:23
  29.4 1.1 %multiply_reduce_fusion = (f32[512]{0:T(512)S(1)}, f32[512,192]{0,1:T(8,128)}) fusion(f32[512,192]{0,1:T(8,128)S(1)} %convolution_add_fusion.2, bf16[512,288]{1,0:T(8,128)(2,1)S(1)} %bitcast.104, bf16[288,192]{1,0:T(8,128)(2,1)S(1)} %bitcast.128), kind=kOutput, calls=%fused_computation.54 | convolution fusion | flops 56917504 | bytes 1193984 | tf_op jit(solution)/shard_map/dot_general | solution.py:48
  30.5 1.2 %copy.9 = f32[512,192]{1,0:T(8,128)S(1)} copy(f32[512,192]{0,1:T(8,128)} %get-tuple-element.95) | data formatting | bytes 786432 | tf_op jit(solution)/shard_map/add | solution.py:48
  32.0 4.3 %collective-permute-start.5 = (bf16[2,8,16,192]{3,2,1,0:T(8,128)(2,1)S(1)}, bf16[2,8,16,192]{3,2,1,0:T(8,128)(2,1)S(1)}, u32[]{:S(2)}, u32[]{:S(2)}) collective-permute-start(bf16[2,8,16,192]{3,2,1,0:T(8,128)(2,1)S(1)} %slice.549), channel_id=1, source_target_pairs={{0,8},{8,16},{16,24},{1,9},{9,17},{17,25},{2,10},{10,18},{18,26},{... | collective-permute-start | bytes 294920 | tf_op jit(solution)/shard_map/ppermute | solution.py:12
  36.5 2.3 %collective-permute-done.5 = bf16[2,8,16,192]{3,2,1,0:T(8,128)(2,1)S(1)} collective-permute-done((bf16[2,8,16,192]{3,2,1,0:T(8,128)(2,1)S(1)}, bf16[2,8,16,192]{3,2,1,0:T(8,128)(2,1)S(1)}, u32[]{:S(2)}, u32[]{:S(2)}) %collective-permute-start.5) | collective-permute-done | bytes 98336 | tf_op jit(solution)/shard_map/ppermute | solution.py:12
  38.8 1.6 %collective-permute-start.6 = (bf16[6,1,16,192]{3,2,1,0:T(8,128)(2,1)S(1)}, bf16[6,1,16,192]{3,2,1,0:T(8,128)(2,1)S(1)}, u32[]{:S(2)}, u32[]{:S(2)}) collective-permute-start(bf16[6,1,16,192]{3,2,1,0:T(8,128)(2,1)S(1)} %get-tuple-element.56), channel_id=1, source_target_pairs={{0,4},{1,5},{2,6},{3,7},{8,12},{9,13},{10,14},{11,15},{16,20},{17,... | collective-permute-start | bytes 110600 | tf_op jit(solution)/shard_map/ppermute | solution.py:20
  40.5 1.3 %collective-permute-start.7 = (bf16[6,1,16,192]{3,2,1,0:T(8,128)(2,1)S(1)}, bf16[6,1,16,192]{3,2,1,0:T(8,128)(2,1)S(1)}, u32[]{:S(2)}, u32[]{:S(2)}) collective-permute-start(bf16[6,1,16,192]{3,2,1,0:T(8,128)(2,1)S(1)} %get-tuple-element.57), channel_id=1, source_target_pairs={{4,0},{5,1},{6,2},{7,3},{12,8},{13,9},{14,10},{15,11},{20,16},{21,... | collective-permute-start | bytes 110600 | tf_op jit(solution)/shard_map/ppermute | solution.py:23
  42.2 4.3 %collective-permute-done.7 = bf16[6,1,16,192]{3,2,1,0:T(8,128)(2,1)S(1)} collective-permute-done((bf16[6,1,16,192]{3,2,1,0:T(8,128)(2,1)S(1)}, bf16[6,1,16,192]{3,2,1,0:T(8,128)(2,1)S(1)}, u32[]{:S(2)}, u32[]{:S(2)}) %collective-permute-start.7) | collective-permute-done | bytes 36896 | tf_op jit(solution)/shard_map/ppermute | solution.py:23
  46.9 2.2 %collective-permute-start.8 = (bf16[6,10,1,192]{3,2,1,0:T(2,128)(2,1)S(1)}, bf16[6,10,1,192]{3,2,1,0:T(2,128)(2,1)S(1)}, u32[]{:S(2)}, u32[]{:S(2)}) collective-permute-start(bf16[6,10,1,192]{3,2,1,0:T(2,128)(2,1)S(1)} %get-tuple-element.46), channel_id=1, source_target_pairs={{0,1},{1,2},{2,3},{4,5},{5,6},{6,7},{8,9},{9,10},{10,11},{12,13},{... | collective-permute-start | bytes 69128 | tf_op jit(solution)/shard_map/ppermute | solution.py:20
  49.1 1.5 %collective-permute-start.9 = (bf16[6,10,1,192]{3,2,1,0:T(2,128)(2,1)S(1)}, bf16[6,10,1,192]{3,2,1,0:T(2,128)(2,1)S(1)}, u32[]{:S(2)}, u32[]{:S(2)}) collective-permute-start(bf16[6,10,1,192]{3,2,1,0:T(2,128)(2,1)S(1)} %get-tuple-element.47), channel_id=1, source_target_pairs={{1,0},{2,1},{3,2},{5,4},{6,5},{7,6},{9,8},{10,9},{11,10},{13,12},{... | collective-permute-start | bytes 69128 | tf_op jit(solution)/shard_map/ppermute | solution.py:23
  50.7 3.3 %collective-permute-done.9 = bf16[6,10,1,192]{3,2,1,0:T(2,128)(2,1)S(1)} collective-permute-done((bf16[6,10,1,192]{3,2,1,0:T(2,128)(2,1)S(1)}, bf16[6,10,1,192]{3,2,1,0:T(2,128)(2,1)S(1)}, u32[]{:S(2)}, u32[]{:S(2)}) %collective-permute-start.9) | collective-permute-done | bytes 23072 | tf_op jit(solution)/shard_map/ppermute | solution.py:23
  54.0 0.5 maximum_maximum_fusion
  58.3 0.4 pad_maximum_fusion.8
  61.2 1.3 %collective-permute-start.10 = (bf16[4,8,1,192]{3,2,1,0:T(2,128)(2,1)S(1)}, bf16[4,8,1,192]{3,2,1,0:T(2,128)(2,1)S(1)}, u32[]{:S(2)}, u32[]{:S(2)}) collective-permute-start(bf16[4,8,1,192]{3,2,1,0:T(2,128)(2,1)S(1)} %slice.576), channel_id=1, source_target_pairs={{1,0},{2,1},{3,2},{5,4},{6,5},{7,6},{9,8},{10,9},{11,10},{13,12},{... | collective-permute-start | bytes 36872 | tf_op jit(solution)/shard_map/ppermute | solution.py:12
  63.0 3.7 %collective-permute-done.10 = bf16[4,8,1,192]{3,2,1,0:T(2,128)(2,1)S(1)} collective-permute-done((bf16[4,8,1,192]{3,2,1,0:T(2,128)(2,1)S(1)}, bf16[4,8,1,192]{3,2,1,0:T(2,128)(2,1)S(1)}, u32[]{:S(2)}, u32[]{:S(2)}) %collective-permute-start.10) | collective-permute-done | bytes 12320 | tf_op jit(solution)/shard_map/ppermute | solution.py:12
  67.2 0.5 slice.511
  67.7 1.3 %collective-permute-start.11 = (bf16[4,1,17,192]{3,2,1,0:T(8,128)(2,1)S(1)}, bf16[4,1,17,192]{3,2,1,0:T(8,128)(2,1)S(1)}, u32[]{:S(2)}, u32[]{:S(2)}) collective-permute-start(bf16[4,1,17,192]{3,2,1,0:T(8,128)(2,1)S(1)} %fusion.16), channel_id=1, source_target_pairs={{4,0},{5,1},{6,2},{7,3},{12,8},{13,9},{14,10},{15,11},{20,16},{21,... | collective-permute-start | bytes 78344 | tf_op jit(solution)/shard_map/ppermute | solution.py:12
  69.4 4.3 %collective-permute-done.11 = bf16[4,1,17,192]{3,2,1,0:T(8,128)(2,1)S(1)} collective-permute-done((bf16[4,1,17,192]{3,2,1,0:T(8,128)(2,1)S(1)}, bf16[4,1,17,192]{3,2,1,0:T(8,128)(2,1)S(1)}, u32[]{:S(2)}, u32[]{:S(2)}) %collective-permute-start.11) | collective-permute-done | bytes 26144 | tf_op jit(solution)/shard_map/ppermute | solution.py:12
  73.8 0.6 slice.518
  74.4 0.6 slice.519
  75.0 0.8 %slice.520 = bf16[4,4,8,192]{3,2,1,0:T(8,128)(2,1)S(1)} slice(bf16[4,9,17,192]{3,2,1,0:T(8,128)(2,1)S(1)} %pad_maximum_fusion.12), slice={[0:4:1], [2:9:2], [2:17:2], [0:192:1]} | slice | bytes 98304 | tf_op jit(solution)/shard_map/slice | solution.py:65
  76.7 0.5 slice.516
  78.1 0.7 convert_element_type.24
  (86 shorter events, 16.8 us)
Async XLA Ops:
  0.0 60.9 %copy-start = (bf16[96,192]{1,0:T(8,128)(2,1)S(1)}, bf16[96,192]{1,0:T(8,128)(2,1)}, u32[]{:S(2)}) copy-start(bf16[96,192]{1,0:T(8,128)(2,1)} %param.12) | copy-start | bytes 110596
  2.1 6.8 %collective-permute-start = (bf16[2,8,16,96]{3,2,1,0:T(8,128)(2,1)S(1)}, bf16[2,8,16,96]{3,2,1,0:T(8,128)(2,1)S(1)}, u32[]{:S(2)}, u32[]{:S(2)}) collective-permute-start(bf16[2,8,16,96]{3,2,1,0:T(8,128)(2,1)S(1)} %slice.522), channel_id=1, source_target_pairs={{0,8},{8,16},{16,24},{1,9},{9,17},{17,25},{2,10},{10,18},{18,26},{... | collective-permute-start | bytes 147464 | tf_op jit(solution)/shard_map/ppermute | solution.py:12
  8.9 4.9 %collective-permute-start.1 = (bf16[6,1,16,96]{3,2,1,0:T(8,128)(2,1)S(1)}, bf16[6,1,16,96]{3,2,1,0:T(8,128)(2,1)S(1)}, u32[]{:S(2)}, u32[]{:S(2)}) collective-permute-start(bf16[6,1,16,96]{3,2,1,0:T(8,128)(2,1)S(1)} %get-tuple-element.90), channel_id=1, source_target_pairs={{0,4},{1,5},{2,6},{3,7},{8,12},{9,13},{10,14},{11,15},{16,20},{17,... | collective-permute-start | bytes 55304 | tf_op jit(solution)/shard_map/ppermute | solution.py:20
  12.3 5.7 %collective-permute-start.2 = (bf16[6,1,16,96]{3,2,1,0:T(8,128)(2,1)S(1)}, bf16[6,1,16,96]{3,2,1,0:T(8,128)(2,1)S(1)}, u32[]{:S(2)}, u32[]{:S(2)}) collective-permute-start(bf16[6,1,16,96]{3,2,1,0:T(8,128)(2,1)S(1)} %get-tuple-element.91), channel_id=1, source_target_pairs={{4,0},{5,1},{6,2},{7,3},{12,8},{13,9},{14,10},{15,11},{20,16},{21,... | collective-permute-start | bytes 55304 | tf_op jit(solution)/shard_map/ppermute | solution.py:23
  18.1 2.8 %collective-permute-start.3 = (bf16[6,10,1,96]{3,2,1,0:T(2,128)(2,1)S(1)}, bf16[6,10,1,96]{3,2,1,0:T(2,128)(2,1)S(1)}, u32[]{:S(2)}, u32[]{:S(2)}) collective-permute-start(bf16[6,10,1,96]{3,2,1,0:T(2,128)(2,1)S(1)} %get-tuple-element.80), channel_id=1, source_target_pairs={{0,1},{1,2},{2,3},{4,5},{5,6},{6,7},{8,9},{9,10},{10,11},{12,13},{... | collective-permute-start | bytes 34568 | tf_op jit(solution)/shard_map/ppermute | solution.py:20
  19.4 4.9 %collective-permute-start.4 = (bf16[6,10,1,96]{3,2,1,0:T(2,128)(2,1)S(1)}, bf16[6,10,1,96]{3,2,1,0:T(2,128)(2,1)S(1)}, u32[]{:S(2)}, u32[]{:S(2)}) collective-permute-start(bf16[6,10,1,96]{3,2,1,0:T(2,128)(2,1)S(1)} %get-tuple-element.81), channel_id=1, source_target_pairs={{1,0},{2,1},{3,2},{5,4},{6,5},{7,6},{9,8},{10,9},{11,10},{13,12},{... | collective-permute-start | bytes 34568 | tf_op jit(solution)/shard_map/ppermute | solution.py:23
  29.4 2.4 %copy-start.3 = (f32[192]{0:T(256)S(1)}, f32[192]{0:T(256)}, u32[]{:S(2)}) copy-start(f32[192]{0:T(256)} %param.9) | copy-start | bytes 2308
  29.4 6.9 %copy-start.1 = (bf16[3,3,3,192,192]{4,3,2,1,0:T(8,128)(2,1)S(1)}, bf16[3,3,3,192,192]{4,3,2,1,0:T(8,128)(2,1)}, u32[]{:S(2)}) copy-start(bf16[3,3,3,192,192]{4,3,2,1,0:T(8,128)(2,1)} %param.11) | copy-start | bytes 5971972
  32.0 6.8 %collective-permute-start.5 = (bf16[2,8,16,192]{3,2,1,0:T(8,128)(2,1)S(1)}, bf16[2,8,16,192]{3,2,1,0:T(8,128)(2,1)S(1)}, u32[]{:S(2)}, u32[]{:S(2)}) collective-permute-start(bf16[2,8,16,192]{3,2,1,0:T(8,128)(2,1)S(1)} %slice.549), channel_id=1, source_target_pairs={{0,8},{8,16},{16,24},{1,9},{9,17},{17,25},{2,10},{10,18},{18,26},{... | collective-permute-start | bytes 294920 | tf_op jit(solution)/shard_map/ppermute | solution.py:12
  38.8 3.4 %collective-permute-start.6 = (bf16[6,1,16,192]{3,2,1,0:T(8,128)(2,1)S(1)}, bf16[6,1,16,192]{3,2,1,0:T(8,128)(2,1)S(1)}, u32[]{:S(2)}, u32[]{:S(2)}) collective-permute-start(bf16[6,1,16,192]{3,2,1,0:T(8,128)(2,1)S(1)} %get-tuple-element.56), channel_id=1, source_target_pairs={{0,4},{1,5},{2,6},{3,7},{8,12},{9,13},{10,14},{11,15},{16,20},{17,... | collective-permute-start | bytes 110600 | tf_op jit(solution)/shard_map/ppermute | solution.py:20
  40.5 6.1 %collective-permute-start.7 = (bf16[6,1,16,192]{3,2,1,0:T(8,128)(2,1)S(1)}, bf16[6,1,16,192]{3,2,1,0:T(8,128)(2,1)S(1)}, u32[]{:S(2)}, u32[]{:S(2)}) collective-permute-start(bf16[6,1,16,192]{3,2,1,0:T(8,128)(2,1)S(1)} %get-tuple-element.57), channel_id=1, source_target_pairs={{4,0},{5,1},{6,2},{7,3},{12,8},{13,9},{14,10},{15,11},{20,16},{21,... | collective-permute-start | bytes 110600 | tf_op jit(solution)/shard_map/ppermute | solution.py:23
  46.9 3.7 %collective-permute-start.8 = (bf16[6,10,1,192]{3,2,1,0:T(2,128)(2,1)S(1)}, bf16[6,10,1,192]{3,2,1,0:T(2,128)(2,1)S(1)}, u32[]{:S(2)}, u32[]{:S(2)}) collective-permute-start(bf16[6,10,1,192]{3,2,1,0:T(2,128)(2,1)S(1)} %get-tuple-element.46), channel_id=1, source_target_pairs={{0,1},{1,2},{2,3},{4,5},{5,6},{6,7},{8,9},{9,10},{10,11},{12,13},{... | collective-permute-start | bytes 69128 | tf_op jit(solution)/shard_map/ppermute | solution.py:20
  49.1 4.9 %collective-permute-start.9 = (bf16[6,10,1,192]{3,2,1,0:T(2,128)(2,1)S(1)}, bf16[6,10,1,192]{3,2,1,0:T(2,128)(2,1)S(1)}, u32[]{:S(2)}, u32[]{:S(2)}) collective-permute-start(bf16[6,10,1,192]{3,2,1,0:T(2,128)(2,1)S(1)} %get-tuple-element.47), channel_id=1, source_target_pairs={{1,0},{2,1},{3,2},{5,4},{6,5},{7,6},{9,8},{10,9},{11,10},{13,12},{... | collective-permute-start | bytes 69128 | tf_op jit(solution)/shard_map/ppermute | solution.py:23
  60.7 1.8 %copy-start.2 = (bf16[3,3,192,192]{3,2,1,0:T(8,128)(2,1)S(1)}, bf16[3,3,192,192]{3,2,1,0:T(8,128)(2,1)}, u32[]{:S(2)}) copy-start(bf16[3,3,192,192]{3,2,1,0:T(8,128)(2,1)} %param.13) | copy-start | bytes 1990660
  61.2 5.5 %collective-permute-start.10 = (bf16[4,8,1,192]{3,2,1,0:T(2,128)(2,1)S(1)}, bf16[4,8,1,192]{3,2,1,0:T(2,128)(2,1)S(1)}, u32[]{:S(2)}, u32[]{:S(2)}) collective-permute-start(bf16[4,8,1,192]{3,2,1,0:T(2,128)(2,1)S(1)} %slice.576), channel_id=1, source_target_pairs={{1,0},{2,1},{3,2},{5,4},{6,5},{7,6},{9,8},{10,9},{11,10},{13,12},{... | collective-permute-start | bytes 36872 | tf_op jit(solution)/shard_map/ppermute | solution.py:12
  67.7 6.0 %collective-permute-start.11 = (bf16[4,1,17,192]{3,2,1,0:T(8,128)(2,1)S(1)}, bf16[4,1,17,192]{3,2,1,0:T(8,128)(2,1)S(1)}, u32[]{:S(2)}, u32[]{:S(2)}) collective-permute-start(bf16[4,1,17,192]{3,2,1,0:T(8,128)(2,1)S(1)} %fusion.16), channel_id=1, source_target_pairs={{4,0},{5,1},{6,2},{7,3},{12,8},{13,9},{14,10},{15,11},{20,16},{21,... | collective-permute-start | bytes 78344 | tf_op jit(solution)/shard_map/ppermute | solution.py:12
where the time goes:
time: 80.4 us; the launch traced here: 78.9 us
  waiting for transfers between devices  26.5 us (33%)
  starting transfers between devices  25.6 us (32%)
  local copies, waits for them, and re-layouts  11.1 us (14%)
  matrix products  8.16 us (10%)
  other arithmetic  6.84 us (9%)
    ppermute x4, waiting for transfers between devices, padded(): lax.ppermute(lax.slice_in_dim(block, 0, width, axis=dim), axis, backward)  15.2 us
    ppermute x4, starting transfers between devices, shifted(): return lax.ppermute(value, axis, pairs)  11.8 us
    ppermute x4, waiting for transfers between devices, shifted(): return lax.ppermute(value, axis, pairs)  10.7 us
    ppermute x4, starting transfers between devices, padded(): lax.ppermute(lax.slice_in_dim(block, block.shape[dim] - width, None, axis...  8.49 us
    dot_general x18, matrix products, convolve(): jnp.dot(stacked.reshape(-1, 3 * c_in), filter_weight[depth_tap, row_tap]....  7.06 us
    ppermute x4, starting transfers between devices, padded(): lax.ppermute(lax.slice_in_dim(block, 0, width, axis=dim), axis, backward)  5.35 us
    slice x9, local copies, waits for them, and re-layouts, halve_spatial(): border_filled[:, row_tap:row_tap + 2 * out_rows:2, col_tap:col_tap + 2 *...  4.66 us
    concatenate x16, other arithmetic, convolve(): jnp.concatenate([window_slab[:, :, col_tap:col_tap + cols] for col_tap in...  3.96 us
  transfers between devices with their start and end apart: 12, of which 10 were waited for; matrix products, arithmetic and copies ran while one was open for 4% of the time, Pallas kernels for 0%

commit v1 on v0

v1 whole, which is shorter than its diff:
```python
import functools
import jax
import jax.numpy as jnp
from jax import lax
from jax.experimental import pallas as pl
from jax.experimental.pallas import tpu as pltpu
from jax.sharding import PartitionSpec as P

epsilon = 1e-06
AXES = ("tm", "height", "width")
LANES = 128
LOW, HIGH = 2, 3
EDGE = 4


def swap_pairs(axis, parity):
    sizes = [lax.axis_size(name) for name in AXES]
    place = AXES.index(axis)
    count = sizes[place]
    pairs = []
    for t in range(sizes[0]):
        for h in range(sizes[1]):
            for w in range(sizes[2]):
                source = [t, h, w]
                target = [t, h, w]
                other = source[place] + (1 if source[place] % 2 == parity else -1)
                if 0 <= other < count:
                    target[place] = other
                elif axis == "width":
                    target[place] = other % count
                else:
                    target[2] = w ^ 1
                pairs.append(
                    tuple((p[0] * sizes[1] + p[1]) * sizes[2] + p[2] for p in (source, target))
                )
    return pairs


def exchange(axis, to_next, to_prev):
    count = lax.axis_size(axis)
    index = lax.axis_index(axis)
    even = index % 2 == 0
    zero = jnp.zeros_like(to_next)
    with_pair = lax.ppermute(jnp.where(even, to_next, to_prev), AXES, swap_pairs(axis, 0))
    if count > 2:
        across = lax.ppermute(jnp.where(even, to_prev, to_next), AXES, swap_pairs(axis, 1))
    else:
        across = zero
    from_prev = jnp.where(even, jnp.where(index > 0, across, zero), with_pair)
    from_next = jnp.where(even, with_pair, jnp.where(index < count - 1, across, zero))
    return from_prev, from_next


def kernel(
    dims, mid_ref, left_ref, right_ref, gain1, gain2, shortcut, conv1, conv2, down,
    out_ref, first, raw, stack1, sec_a, sec_b, stack2, mer_a, mer_b, stack3, result,
    w1, w2m, w2r, wdm, wdr, wsc, g1, g2, sems,
):
    frames, rows, cols, c1, c2 = dims
    R = rows + LOW + HIGH
    in_cols, hid_cols, mer_cols = cols + LOW + HIGH, cols + 3, cols + 1
    M1, M2 = stack1.shape[1], stack2.shape[1]
    rest = c2 - LANES
    bf, f32 = jnp.bfloat16, jnp.float32

    copies1, copies2, copies3 = [], [], []
    copies0 = [
        pltpu.make_async_copy(gain1, g1, sems.at[15]),
        pltpu.make_async_copy(gain2, g2, sems.at[16]),
        pltpu.make_async_copy(shortcut, wsc.at[pl.ds(0, c1)], sems.at[17]),
    ]
    for dc in range(3):
        copies1.append(pltpu.make_async_copy(conv1.at[:, :, dc], w1.at[dc, :, :, pl.ds(0, c1)], sems.at[dc]))
        copies2.append(
            pltpu.make_async_copy(conv2.at[:, :, dc, pl.ds(0, LANES)], w2m.at[dc], sems.at[3 + dc])
        )
        copies2.append(
            pltpu.make_async_copy(
                conv2.at[:, :, dc, pl.ds(LANES, rest)], w2r.at[dc, :, pl.ds(0, 3)], sems.at[6 + dc]
            )
        )
        copies3.append(
            pltpu.make_async_copy(down.at[:, dc, pl.ds(0, LANES)], wdm.at[dc], sems.at[9 + dc])
        )
        copies3.append(
            pltpu.make_async_copy(
                down.at[:, dc, pl.ds(LANES, rest)], wdr.at[dc, pl.ds(0, 3)], sems.at[12 + dc]
            )
        )
    for copy in copies0 + copies1 + copies2 + copies3:
        copy.start()
    w1[:, :, :, c1:, :] = jnp.zeros((3, 3, 3, LANES - c1, c2), bf)
    w2r[:, :, 3] = jnp.zeros((3, 3, rest, c2), bf)
    wdr[:, 3] = jnp.zeros((3, rest, c2), bf)
    wsc[c1:] = jnp.zeros((LANES - c1, c2), bf)
    sec_b[...] = jnp.zeros_like(sec_b)
    mer_a[...] = jnp.zeros_like(mer_a)
    mer_b[...] = jnp.zeros_like(mer_b)

    slots = EDGE * LANES
    source = lax.broadcasted_iota(jnp.int32, (EDGE * c1, slots), 0)
    target = lax.broadcasted_iota(jnp.int32, (EDGE * c1, slots), 1)
    slot, lane = target // LANES, target % LANES
    spread = jnp.where((source == slot * c1 + lane) & (lane < c1), 1.0, 0.0).astype(bf)
    for copy in copies0:
        copy.wait()
    gain1 = jnp.concatenate([g1[...], jnp.zeros((1, LANES - c1), f32)], axis=-1)
    pieces = [(left_ref, 0, EDGE - LOW, EDGE, 0)]
    for group in range(cols // EDGE):
        pieces.append((mid_ref, group * EDGE * c1, 0, EDGE, LOW + group * EDGE))
    pieces.append((right_ref, 0, 0, HIGH, LOW + cols))
    P16 = mid_ref.shape[1]
    for ref, lane, lo, hi, c in pieces:
        x = ref[:, :, lane : lane + EDGE * c1].reshape(2 * frames * P16, EDGE * c1)
        xu = jnp.dot(x, spread, preferred_element_type=f32)
        for k in range(lo, hi):
            v = xu[:, k * LANES : (k + 1) * LANES]
            ms = jnp.sum(v * v, axis=-1, keepdims=True) * (1.0 / c1)
            u = v * lax.rsqrt(ms + epsilon) * gain1
            u = u / (1.0 + jnp.exp(-u))
            for f in range(2 * frames):
                first[c, f * R : f * R + P16, :] = u[f * P16 : (f + 1) * P16]
                if f >= frames and LOW <= c < LOW + mer_cols:
                    g = f - frames
                    raw[c - LOW, g * R : g * R + P16, :] = v[f * P16 : (f + 1) * P16]
            c += 1

    def build1(c, carry):
        for k in range(9):
            off = (k // 3) * R + k % 3
            stack1[c, :, k * LANES : (k + 1) * LANES] = first[c, off : off + M1, :].astype(bf)
        return carry

    lax.fori_loop(0, in_cols, build1, 0)

    t, h, w = [lax.axis_index(name) for name in AXES]
    first_t, top, leftmost = [jnp.where(i == 0, 1, 0) for i in (t, h, w)]
    bottom = jnp.where(h == lax.axis_size("height") - 1, 1, 0)
    rightmost = jnp.where(w == lax.axis_size("width") - 1, 1, 0)
    p = lax.broadcasted_iota(jnp.int32, (M1, 1), 0)
    dead = (p < 2 * R) & (first_t == 1)
    for f in range(frames + 2):
        dead |= (p == f * R) & (top == 1)
        dead |= ((p == f * R + rows + 1) | (p == f * R + rows + 2)) & (bottom == 1)
    live1 = jnp.where(dead, 0.0, 1.0).astype(f32)
    q = lax.broadcasted_iota(jnp.int32, (M2, 1), 0)
    dead = q < 0
    for f in range(frames):
        dead |= (q == f * R + rows) & (bottom == 1)
    live2 = jnp.where(dead, 0.0, 1.0).astype(f32)
    keep_left = jnp.where(leftmost == 1, 0.0, 1.0).astype(f32)
    keep_right = jnp.where(rightmost == 1, 0.0, 1.0).astype(f32)

    for copy in copies1:
        copy.wait()
    gain2 = g2[...]
    step1 = 5
    for start in range(0, hid_cols, step1):
        n = min(step1, hid_cols - start)
        acc = None
        for dc in range(3):
            part = jnp.dot(
                stack1[start + dc : start + dc + n].reshape(n * M1, 9 * LANES),
                w1[dc].reshape(9 * LANES, c2),
                preferred_element_type=f32,
            )
            acc = part if acc is None else acc + part
        for i in range(n):
            c = start + i
            hid = acc[i * M1 : (i + 1) * M1]
            ms = jnp.sum(hid * hid, axis=-1, keepdims=True) * (1.0 / c2)
            u = hid * lax.rsqrt(ms + epsilon) * gain2
            u = u / (1.0 + jnp.exp(-u)) * live1
            if c == 0:
                u = u * keep_left
            if c > cols:
                u = u * keep_right
            sec_a[c, :, :] = u[:, :LANES]
            sec_b[c, 0:M1, 0:rest] = u[:, LANES:]
            sec_b[c, 0 : M1 - 1, rest : 2 * rest] = u[1:, LANES:]

    def build2(c, carry):
        for k in range(9):
            off = (k // 3) * R + k % 3
            stack2[c, :, k * LANES : (k + 1) * LANES] = sec_a[c, off : off + M2, :].astype(bf)
        for dt in range(3):
            for half in range(2):
                k = 9 + 2 * dt + half
                off = dt * R + 2 * half
                stack2[c, :, k * LANES : (k + 1) * LANES] = sec_b[c, off : off + M2, :].astype(bf)
        return carry

    lax.fori_loop(0, hid_cols, build2, 0)
    for copy in copies2:
        copy.wait()
    step2 = 9
    for start in range(0, mer_cols, step2):
        n = min(step2, mer_cols - start)
        acc = jnp.dot(
            raw[start : start + n, LOW : LOW + M2, :].reshape(n * M2, LANES).astype(bf),
            wsc[...],
            preferred_element_type=f32,
        )
        for dc in range(3):
            acc += jnp.dot(
                stack2[start + dc : start + dc + n, :, : 9 * LANES].reshape(n * M2, 9 * LANES),
                w2m[dc].reshape(9 * LANES, c2),
                preferred_element_type=f32,
            )
            acc += jnp.dot(
                stack2[start + dc : start + dc + n, :, 9 * LANES :].reshape(n * M2, 6 * LANES),
                w2r[dc].reshape(6 * LANES, c2),
                preferred_element_type=f32,
            )
        for i in range(n):
            c = start + i
            mer = acc[i * M2 : (i + 1) * M2] * live2
            if c == cols:
                mer = mer * keep_right
            mer_a[c, 0:M2, :] = mer[:, :LANES]
            mer_b[c, 0:M2, 0:rest] = mer[:, LANES:]
            mer_b[c, 0 : M2 - 1, rest : 2 * rest] = mer[1:, LANES:]

    out_cols = cols // 2
    for j in range(out_cols):
        for dc in range(3):
            for dr in range(3):
                k = dc * 3 + dr
                stack3[j, :, k * LANES : (k + 1) * LANES] = mer_a[2 * j + dc, dr : dr + M2, :].astype(bf)
            for half in range(2):
                k = 9 + 2 * dc + half
                stack3[j, :, k * LANES : (k + 1) * LANES] = mer_b[
                    2 * j + dc, 2 * half : 2 * half + M2, :
                ].astype(bf)
    for copy in copies3:
        copy.wait()
    acc = jnp.dot(
        stack3[:, :, : 9 * LANES].reshape(out_cols * M2, 9 * LANES),
        wdm[...].reshape(9 * LANES, c2),
        preferred_element_type=f32,
    )
    acc += jnp.dot(
        stack3[:, :, 9 * LANES :].reshape(out_cols * M2, 6 * LANES),
        wdr[...].reshape(6 * LANES, c2),
        preferred_element_type=f32,
    )
    acc = acc.reshape(out_cols, M2, c2)
    result[0] = acc[:, :, :LANES]
    result[1, :, :, 0:rest] = acc[:, :, LANES:]
    for f in range(frames):
        for j in range(out_cols):
            a = result[0, j, pl.ds(f * R, rows // 2, stride=2), :]
            b = result[1, j, pl.ds(f * R, rows // 2, stride=2), :][:, :rest]
            out_ref[f, :, j * c2 : (j + 1) * c2] = jnp.concatenate([a, b], axis=-1).astype(bf)


def up(n, k):
    return -(-n // k) * k


def local(video_in, gain_first, gain_second, conv_first, conv_second, shortcut, downscale_weight):
    frames, rows, merged_cols = video_in.shape
    c1, c2 = shortcut.shape
    cols = merged_cols // c1

    prev, _ = exchange("tm", video_in, video_in)
    both = jnp.concatenate([prev, video_in], axis=0)
    above, below = exchange("height", both[:, rows - HIGH :], both[:, :HIGH])
    spare = jnp.zeros((2 * frames, 16 - (rows + LOW + HIGH), merged_cols), jnp.bfloat16)
    mid = jnp.concatenate([above[:, HIGH - LOW :], both, below, spare], axis=1)
    left, right = exchange("width", mid[:, :, merged_cols - EDGE * c1 :], mid[:, :, : EDGE * c1])

    R = rows + LOW + HIGH
    in_cols, hid_cols, mer_cols = cols + LOW + HIGH, cols + 3, cols + 1
    M1 = up((frames + 1) * R + rows + 3, 16)
    M2 = up((frames - 1) * R + rows + 1, 16)
    bf, f32 = jnp.bfloat16, jnp.float32
    vmem = pl.BlockSpec(memory_space=pltpu.VMEM)
    hbm = pl.BlockSpec(memory_space=pltpu.HBM)
    out_cols = cols // 2
    rows_up = mid.shape[1]
    return pl.pallas_call(
        functools.partial(kernel, (frames, rows, cols, c1, c2)),
        out_shape=jax.ShapeDtypeStruct((frames, rows // 2, out_cols * c2), bf),
        in_specs=[vmem] * 3 + [hbm] * 6,
        out_specs=vmem,
        scratch_shapes=[
            pltpu.VMEM((in_cols, up(max(M1 + 2 * R + 2, (2 * frames - 1) * R + rows_up), 8), LANES), f32),
            pltpu.VMEM((mer_cols, up((frames - 1) * R + rows_up, 8), LANES), f32),
            pltpu.VMEM((in_cols, M1, 9 * LANES), bf),
            pltpu.VMEM((hid_cols, M1, LANES), f32),
            pltpu.VMEM((hid_cols, M1, LANES), f32),
            pltpu.VMEM((hid_cols, M2, 15 * LANES), bf),
            pltpu.VMEM((mer_cols, M2 + 8, LANES), f32),
            pltpu.VMEM((mer_cols, M2 + 8, LANES), f32),
            pltpu.VMEM((out_cols, M2, 15 * LANES), bf),
            pltpu.VMEM((2, out_cols, M2, LANES), f32),
            pltpu.VMEM((3, 3, 3, LANES, c2), bf),
            pltpu.VMEM((3, 3, 3, LANES, c2), bf),
            pltpu.VMEM((3, 3, 4, c2 - LANES, c2), bf),
            pltpu.VMEM((3, 3, LANES, c2), bf),
            pltpu.VMEM((3, 4, c2 - LANES, c2), bf),
            pltpu.VMEM((LANES, c2), bf),
            pltpu.VMEM((1, c1), f32),
            pltpu.VMEM((1, c2), f32),
            pltpu.SemaphoreType.DMA((18,)),
        ],
        compiler_params=pltpu.CompilerParams(vmem_limit_bytes=60 * 1024 * 1024),
        cost_estimate=pl.CostEstimate(flops=4 * 10**9, bytes_accessed=5 * 10**6, transcendentals=10**6),
    )(
        mid, left, right, gain_first.reshape(1, c1), gain_second.reshape(1, c2), shortcut,
        conv_first, conv_second, downscale_weight,
    )


def solution(mesh):
    placed = (P("tm", "height", "width"), P(), P(), P(), P(), P(), P())
    return jax.shard_map(
        local, mesh=mesh, in_specs=placed, out_specs=P("tm", "height", "width"), check_vma=False
    )
```

time: 80.4 us -> 33.2 us (0.41); the launches traced: 78.9 us -> 33 us
  starting transfers between devices: 25.6 us -> 7.85 us
  waiting for transfers between devices: 26.5 us -> 9.35 us
  Pallas kernels: 0 us -> 12.6 us
  local copies, waits for them, and re-layouts: 11.1 us -> 0.03 us
  matrix products: 8.16 us -> 0 us
  other arithmetic: 6.84 us -> 3.06 us
    ppermute x12 -> x5, starting transfers between devices: 25.6 us -> 7.85 us  [the longest x3 7.33 us: exchange(): lax.ppermute(jnp.where(even, to_next, to_prev), AXES, swap_pairs(axis, 0))]
    ppermute x12 -> x5, waiting for transfers between devices: 26.5 us -> 9.35 us  [the longest x3 5.96 us: exchange(): lax.ppermute(jnp.where(even, to_next, to_prev), AXES, swap_pairs(axis, 0))]
    pallas_call x0 -> x1, Pallas kernels: none -> 12.6 us  [local(): pl.pallas_call(functools.partial(kernel, (frames, rows, cols, c1, c2)), o...]
    dot_general x22 -> x0, matrix products: 8.16 us -> none  [the longest x18 7.06 us: convolve(): jnp.dot(stacked.reshape(-1, 3 * c_in), filter_weight[depth_tap, row_tap]....]
    slice x21 -> x0, local copies, waits for them, and re-layouts: 7.71 us -> none  [the longest x9 4.66 us: halve_spatial(): border_filled[:, row_tap:row_tap + 2 * out_rows:2, col_tap:col_tap + 2 *...]
    concatenate x28 -> x1, other arithmetic: 5.43 us -> 1.15 us  [local(): mid = jnp.concatenate([above[:, HIGH - LOW:], both, below, spare], axis=1)]
    select_n x0 -> x6, other arithmetic: none -> 1.92 us  [the longest x1 1.04 us: exchange(): jnp.where(even, to_next, to_prev)]
    add x2 -> x0, local copies, waits for them, and re-layouts: 1.39 us -> none  [convolve(): total + jnp.dot(stacked.reshape(-1, 3 * c_in), filter_weight[depth_tap, r...]
  transfers between devices with their start and end apart: 12 -> 5, of which waited for: 10 -> 3; matrix products, arithmetic and copies ran while one was open for 4% -> 0% of each run, Pallas kernels for 0% -> 0%
where the time goes in v1:
time: 33.2 us; the launch traced here: 33 us
  Pallas kernels  12.6 us (38%)
  waiting for transfers between devices  9.35 us (28%)
  starting transfers between devices  7.85 us (24%)
  other arithmetic  3.06 us (9%)
    pallas_call x1, Pallas kernels, local(): pl.pallas_call(functools.partial(kernel, (frames, rows, cols, c1, c2)), o...  12.6 us
    ppermute x3, starting transfers between devices, exchange(): lax.ppermute(jnp.where(even, to_next, to_prev), AXES, swap_pairs(axis, 0))  7.33 us
    ppermute x3, waiting for transfers between devices, exchange(): lax.ppermute(jnp.where(even, to_next, to_prev), AXES, swap_pairs(axis, 0))  5.96 us
    ppermute x2, waiting for transfers between devices, exchange(): lax.ppermute(jnp.where(even, to_prev, to_next), AXES, swap_pairs(axis, 1))  3.39 us
    concatenate x1, other arithmetic, local(): mid = jnp.concatenate([above[:, HIGH - LOW:], both, below, spare], axis=1)  1.15 us
    select_n x1, other arithmetic, exchange(): jnp.where(even, to_next, to_prev)  1.04 us
    select_n x2, other arithmetic, exchange(): jnp.where(even, with_pair, jnp.where(index < count - 1, across, zero))  0.75 us
  transfers between devices with their start and end apart: 5, of which 3 were waited for; matrix products, arithmetic and copies ran while one was open for 0% of the time, Pallas kernels for 0%

profile of v1, /device:TPU:0, one launch (start us, length us, event | category | flops | bytes accessed | tf_op | source)
XLA Modules:
  0.0 33.0 jit_solution(2017746819883118377)
XLA Ops:
  0.0 0.5 %collective-permute-start = (bf16[4,8,1536]{2,1,0:T(8,128)(2,1)}, bf16[4,8,1536]{2,1,0:T(8,128)(2,1)S(1)}, u32[]{:S(2)}, u32[]{:S(2)}) collective-permute-start(bf16[4,8,1536]{2,1,0:T(8,128)(2,1)} %param.7), channel_id=1, source_target_pairs={{0,1},{1,0},{2,3},{3,2},{4,5},{5,4},{6,7},{7,6},{8,16},{9,17},{10,... | collective-permute-start | bytes 294920 | tf_op jit(solution)/shard_map/ppermute | solution.py:46
  0.5 4.1 %collective-permute-start.1 = (bf16[4,8,1536]{2,1,0:T(8,128)(2,1)}, bf16[4,8,1536]{2,1,0:T(8,128)(2,1)S(1)}, u32[]{:S(2)}, u32[]{:S(2)}) collective-permute-start(bf16[4,8,1536]{2,1,0:T(8,128)(2,1)} %param.7), channel_id=1, source_target_pairs={{0,8},{1,9},{2,10},{3,11},{4,12},{5,13},{6,14},{7,15},{8,0},{9,1},... | collective-permute-start | bytes 294920 | tf_op jit(solution)/shard_map/ppermute | solution.py:44
  4.6 0.0 collective-permute-done
  4.6 2.8 %collective-permute-done.1 = bf16[4,8,1536]{2,1,0:T(8,128)(2,1)S(1)} collective-permute-done((bf16[4,8,1536]{2,1,0:T(8,128)(2,1)}, bf16[4,8,1536]{2,1,0:T(8,128)(2,1)S(1)}, u32[]{:S(2)}, u32[]{:S(2)}) %collective-permute-start.1) | collective-permute-done | bytes 98336 | tf_op jit(solution)/shard_map/ppermute | solution.py:44
  7.5 1.0 %fusion.1 = bf16[8,3,1536]{2,1,0:T(4,128)(2,1)S(1)} fusion(bf16[4,8,1536]{2,1,0:T(8,128)(2,1)S(1)} %select_select_fusion.2, bf16[4,8,1536]{2,1,0:T(8,128)(2,1)} %param.7, pred[]{:T(512)S(6)} %eq.13), kind=kLoop, calls=%fused_computation.4 | loop fusion | flops 331776 | bytes 270337 | tf_op jit(solution)/shard_map/jit(_where)/select_n | solution.py:44
  8.5 1.6 %collective-permute-start.2 = (bf16[8,3,1536]{2,1,0:T(4,128)(2,1)S(1)}, bf16[8,3,1536]{2,1,0:T(4,128)(2,1)S(1)}, u32[]{:S(2)}, u32[]{:S(2)}) collective-permute-start(bf16[8,3,1536]{2,1,0:T(4,128)(2,1)S(1)} %fusion.1), channel_id=1, source_target_pairs={{0,4},{1,5},{2,6},{3,7},{4,0},{5,1},{6,2},{7,3},{8,12},{9,13},{10,... | collective-permute-start | bytes 221192 | tf_op jit(solution)/shard_map/ppermute | solution.py:44
  10.1 3.1 %collective-permute-done.2 = bf16[8,3,1536]{2,1,0:T(4,128)(2,1)S(1)} collective-permute-done((bf16[8,3,1536]{2,1,0:T(4,128)(2,1)S(1)}, bf16[8,3,1536]{2,1,0:T(4,128)(2,1)S(1)}, u32[]{:S(2)}, u32[]{:S(2)}) %collective-permute-start.2) | collective-permute-done | bytes 73760 | tf_op jit(solution)/shard_map/ppermute | solution.py:44
  13.2 0.1 broadcast_select_fusion
  13.4 1.1 %pad_maximum_fusion.mid_ref = bf16[8,16,1536]{2,1,0:T(8,128)(2,1)S(1)} fusion(bf16[8,3,1536]{2,1,0:T(4,128)(2,1)S(1)} %select_n.91, bf16[8,3,1536]{2,1,0:T(4,128)(2,1)S(1)} %broadcast_select_fusion.3, bf16[4,8,1536]{2,1,0:T(8,128)(2,1)} %param.7, bf16[4,8,1536]{2,1,0:T(8,128)(2,1)S(1)} %select_select_fusion.2, bf16[8,2,1536]{2,1,0:T(2,128)(2,1)S(1)} %broadcast_select_fusion), kind=kLoop, calls=%fused_computation | loop fusion | flops 1966080 | bytes 786432 | tf_op jit(solution)/shard_map/concatenate | solution.py:270
  14.5 0.0 copy-start
  14.6 0.1 collective-permute-start.3
  14.6 1.6 %collective-permute-start.4 = (bf16[8,16,384]{2,1,0:T(8,128)(2,1)S(1)}, bf16[8,16,384]{2,1,0:T(8,128)(2,1)S(1)}, u32[]{:S(2)}, u32[]{:S(2)}) collective-permute-start(bf16[8,16,384]{2,1,0:T(8,128)(2,1)S(1)} %get-tuple-element.6), channel_id=1, source_target_pairs={{0,1},{1,0},{2,3},{3,2},{4,5},{5,4},{6,7},{7,6},{8,9},{9,8},{10,11... | collective-permute-start | bytes 294920 | tf_op jit(solution)/shard_map/ppermute | solution.py:44
  16.3 3.4 %collective-permute-done.3 = bf16[8,16,384]{2,1,0:T(8,128)(2,1)S(1)} collective-permute-done((bf16[8,16,384]{2,1,0:T(8,128)(2,1)S(1)}, bf16[8,16,384]{2,1,0:T(8,128)(2,1)S(1)}, u32[]{:S(2)}, u32[]{:S(2)}) %collective-permute-start.3) | collective-permute-done | bytes 98336 | tf_op jit(solution)/shard_map/ppermute | solution.py:46
  19.6 0.0 collective-permute-done.4
  19.6 0.7 %select_select_fusion = (bf16[8,16,384]{2,1,0:T(8,128)(2,1)}, bf16[8,16,384]{2,1,0:T(8,128)(2,1)}) fusion(bf16[8,16,384]{2,1,0:T(8,128)(2,1)S(1)} %collective-permute-done.4, bf16[8,16,384]{2,1,0:T(8,128)(2,1)S(1)} %collective-permute-done.3, pred[]{:T(512)S(6)} %lt.21, pred[]{:T(512)S(6)} %eq.15, pred[]{:T(512)S(6)} %gt.8), kind=kLoop, calls=%fused_computation.6 | loop fusion | flops 196608 | bytes 393219 | tf_op jit(solution)/shard_map/jit(_where)/select_n | solution.py:50
  20.3 0.0 copy-done
  20.4 12.6 %shard_map.73 = bf16[4,4,1536]{2,1,0:T(4,128)(2,1)} custom-call(bf16[8,16,1536]{2,1,0:T(8,128)(2,1)} %copy-done, bf16[8,16,384]{2,1,0:T(8,128)(2,1)} %get-tuple-element.8.left_ref, bf16[8,16,384]{2,1,0:T(8,128)(2,1)} %get-tuple-element.7.right_ref, f32[1,96]{1,0:T(1,128)} %bitcast.3, f32[1,192]{1,0:T(1,128)} %bitcast.2, bf16[96,192]{1,0:T(8,128)(2,1)} %shortcut.1, ...), custom_call_target="tpu_custom_call" | custom-call | flops 4000000000 | bytes 5000000 | tf_op jit(solution)/shard_map/pallas_call | solution.py:282
  (4 shorter events, 0.1 us)
Async XLA Ops:
  0.0 4.6 %collective-permute-start = (bf16[4,8,1536]{2,1,0:T(8,128)(2,1)}, bf16[4,8,1536]{2,1,0:T(8,128)(2,1)S(1)}, u32[]{:S(2)}, u32[]{:S(2)}) collective-permute-start(bf16[4,8,1536]{2,1,0:T(8,128)(2,1)} %param.7), channel_id=1, source_target_pairs={{0,1},{1,0},{2,3},{3,2},{4,5},{5,4},{6,7},{7,6},{8,16},{9,17},{10,... | collective-permute-start | bytes 294920 | tf_op jit(solution)/shard_map/ppermute | solution.py:46
  0.5 7.0 %collective-permute-start.1 = (bf16[4,8,1536]{2,1,0:T(8,128)(2,1)}, bf16[4,8,1536]{2,1,0:T(8,128)(2,1)S(1)}, u32[]{:S(2)}, u32[]{:S(2)}) collective-permute-start(bf16[4,8,1536]{2,1,0:T(8,128)(2,1)} %param.7), channel_id=1, source_target_pairs={{0,8},{1,9},{2,10},{3,11},{4,12},{5,13},{6,14},{7,15},{8,0},{9,1},... | collective-permute-start | bytes 294920 | tf_op jit(solution)/shard_map/ppermute | solution.py:44
  8.5 4.7 %collective-permute-start.2 = (bf16[8,3,1536]{2,1,0:T(4,128)(2,1)S(1)}, bf16[8,3,1536]{2,1,0:T(4,128)(2,1)S(1)}, u32[]{:S(2)}, u32[]{:S(2)}) collective-permute-start(bf16[8,3,1536]{2,1,0:T(4,128)(2,1)S(1)} %fusion.1), channel_id=1, source_target_pairs={{0,4},{1,5},{2,6},{3,7},{4,0},{5,1},{6,2},{7,3},{8,12},{9,13},{10,... | collective-permute-start | bytes 221192 | tf_op jit(solution)/shard_map/ppermute | solution.py:44
  14.5 5.8 %copy-start = (bf16[8,16,1536]{2,1,0:T(8,128)(2,1)}, bf16[8,16,1536]{2,1,0:T(8,128)(2,1)S(1)}, u32[]{:S(2)}) copy-start(bf16[8,16,1536]{2,1,0:T(8,128)(2,1)S(1)} %pad_maximum_fusion.mid_ref) | copy-start | bytes 1179652
  14.6 5.1 %collective-permute-start.3 = (bf16[8,16,384]{2,1,0:T(8,128)(2,1)S(1)}, bf16[8,16,384]{2,1,0:T(8,128)(2,1)S(1)}, u32[]{:S(2)}, u32[]{:S(2)}) collective-permute-start(bf16[8,16,384]{2,1,0:T(8,128)(2,1)S(1)} %get-tuple-element.5), channel_id=1, source_target_pairs={{0,3},{1,2},{2,1},{3,0},{4,7},{5,6},{6,5},{7,4},{8,11},{9,10},{10,... | collective-permute-start | bytes 294920 | tf_op jit(solution)/shard_map/ppermute | solution.py:46
  14.6 5.0 %collective-permute-start.4 = (bf16[8,16,384]{2,1,0:T(8,128)(2,1)S(1)}, bf16[8,16,384]{2,1,0:T(8,128)(2,1)S(1)}, u32[]{:S(2)}, u32[]{:S(2)}) collective-permute-start(bf16[8,16,384]{2,1,0:T(8,128)(2,1)S(1)} %get-tuple-element.6), channel_id=1, source_target_pairs={{0,1},{1,0},{2,3},{3,2},{4,5},{5,4},{6,7},{7,6},{8,9},{9,8},{10,11... | collective-permute-start | bytes 294920 | tf_op jit(solution)/shard_map/ppermute | solution.py:44

commit v2 on v0

v2 whole, which is shorter than its diff:
```python
import functools
import jax
import jax.numpy as jnp
from jax import lax
from jax.experimental import pallas as pl
from jax.experimental.pallas import tpu as pltpu
from jax.sharding import PartitionSpec as P

epsilon = 1e-06
AXES = ("tm", "height", "width")
LANES = 128
LOW, HIGH = 2, 3
EDGE = 4
SLAB = 4


def swap_pairs(axis, parity):
    sizes = [lax.axis_size(name) for name in AXES]
    place = AXES.index(axis)
    count = sizes[place]
    pairs = []
    for t in range(sizes[0]):
        for h in range(sizes[1]):
            for w in range(sizes[2]):
                source = [t, h, w]
                target = [t, h, w]
                other = source[place] + (1 if source[place] % 2 == parity else -1)
                if 0 <= other < count:
                    target[place] = other
                elif axis == "width":
                    target[place] = other % count
                else:
                    target[2] = w ^ 1
                pairs.append(
                    tuple((p[0] * sizes[1] + p[1]) * sizes[2] + p[2] for p in (source, target))
                )
    return pairs


def swap(axis, outgoing):
    return [lax.ppermute(value, AXES, swap_pairs(axis, i)) for i, value in enumerate(outgoing)]


def rounds(axis):
    return 1 if lax.axis_size(axis) == 2 else 2


def choose(condition, target, first, second):
    @pl.when(condition)
    def _():
        target[...] = first()

    @pl.when(jnp.logical_not(condition))
    def _():
        target[...] = second()


def outgoing(axis, refs, to_next, to_prev):
    even = lax.axis_index(axis) % 2 == 0
    choose(even, refs[0], to_next, to_prev)
    if len(refs) > 1:
        choose(even, refs[1], to_prev, to_next)


def incoming(axis, refs, from_prev, from_next):
    index, count = lax.axis_index(axis), lax.axis_size(axis)
    even = index % 2 == 0
    for target, at_even, absent in ((from_prev, 1, 0), (from_next, 0, count - 1)):
        if target is None:
            continue
        for mine, which in ((even, at_even), (jnp.logical_not(even), 1 - at_even)):
            if which >= len(refs):
                continue

            @pl.when(mine & (index != absent))
            def _(target=target, which=which):
                target[...] = refs[which][...]

        @pl.when(index == absent)
        def _(target=target):
            target[...] = jnp.zeros(target.shape, target.dtype)


def rows_out(own, *refs):
    got, slabs = refs[: rounds("tm")], refs[rounds("tm") : -1]
    prev = refs[-1]
    incoming("tm", got, prev, None)
    rows = own.shape[1]

    def part(lo):
        return lambda: jnp.concatenate([prev[:, lo : lo + SLAB], own[:, lo : lo + SLAB]], axis=0)

    outgoing("height", slabs, part(rows - SLAB), part(0))


def cols_out(width, own, prev, *refs):
    got, mid, slabs = refs[: rounds("height")], refs[rounds("height")], refs[rounds("height") + 1 :]
    frames, rows = own.shape[0], own.shape[1]
    mid[0:frames, 0:rows, :] = prev[...]
    mid[frames:, 0:rows, :] = own[...]
    incoming("height", got, mid.at[:, rows : rows + SLAB, :], mid.at[:, rows + SLAB :, :])
    last = mid.shape[2] - width
    outgoing("width", slabs, lambda: mid[:, :, last:], lambda: mid[:, :, 0:width])


def arrange(c1, x, gain1, gain2, shortcut, conv1, conv2, down, xv, g1, g2, wsc, w1, w2m, w2r, wdm, wdr, sems):
    c2 = g2.shape[1]
    rest = c2 - LANES
    copies = [
        pltpu.make_async_copy(x, xv, sems.at[0]),
        pltpu.make_async_copy(gain1, g1, sems.at[1]),
        pltpu.make_async_copy(gain2, g2, sems.at[2]),
        pltpu.make_async_copy(shortcut, wsc.at[pl.ds(0, c1)], sems.at[3]),
    ]
    for dc in range(3):
        moves = [
            (conv1.at[:, :, dc], w1.at[dc, :, :, pl.ds(0, c1)]),
            (conv2.at[:, :, dc, pl.ds(0, LANES)], w2m.at[dc]),
            (conv2.at[:, :, dc, pl.ds(LANES, rest)], w2r.at[dc, :, pl.ds(0, 3)]),
            (down.at[:, dc, pl.ds(0, LANES)], wdm.at[dc]),
            (down.at[:, dc, pl.ds(LANES, rest)], wdr.at[dc, pl.ds(0, 3)]),
        ]
        for i, (source, target) in enumerate(moves):
            copies.append(pltpu.make_async_copy(source, target, sems.at[4 + 5 * dc + i]))
    for copy in copies:
        copy.start()
    bf = jnp.bfloat16
    wsc[c1:] = jnp.zeros((LANES - c1, c2), bf)
    w1[:, :, :, c1:, :] = jnp.zeros((3, 3, 3, LANES - c1, c2), bf)
    w2r[:, :, 3] = jnp.zeros((3, 3, rest, c2), bf)
    wdr[:, 3] = jnp.zeros((3, rest, c2), bf)
    for copy in copies:
        copy.wait()


class Steps:
    def __init__(self, frames, rows, cols, c1, c2, w1, w2m, w2r, wsc, g1, g2):
        self.frames, self.rows, self.cols, self.c1, self.c2 = frames, rows, cols, c1, c2
        self.rest = c2 - LANES
        self.R = rows + LOW + HIGH
        self.M1 = up((frames + 1) * self.R + rows + 3, 16)
        self.M2 = up((frames - 1) * self.R + rows + 1, 16)
        self.w1, self.w2m, self.w2r, self.wsc = w1, w2m, w2r, wsc
        gap = jnp.zeros((1, LANES - c1), jnp.float32)
        self.gain1, self.gain2 = jnp.concatenate([g1[...], gap], axis=-1), g2[...]
        t, h, w = [lax.axis_index(name) for name in AXES]
        starts, top, left = [i == 0 for i in (t, h, w)]
        bottom, right = [i == lax.axis_size(name) - 1 for i, name in ((h, "height"), (w, "width"))]
        p = lax.broadcasted_iota(jnp.int32, (self.M1, 1), 0)
        dead = (p < 2 * self.R) & starts
        for f in range(frames + 2):
            q = p - f * self.R
            dead |= ((q == 0) & top) | (((q == rows + 1) | (q == rows + 2)) & bottom)
        self.live1 = jnp.where(dead, 0.0, 1.0).astype(jnp.float32)
        p = lax.broadcasted_iota(jnp.int32, (self.M2, 1), 0)
        dead = p < 0
        for f in range(frames):
            dead |= (p == f * self.R + rows) & bottom
        self.live2 = jnp.where(dead, 0.0, 1.0).astype(jnp.float32)
        self.keep_left = jnp.where(left, 0.0, 1.0).astype(jnp.float32)
        self.keep_right = jnp.where(right, 0.0, 1.0).astype(jnp.float32)

    def spread(self):
        shape = (EDGE * self.c1, EDGE * LANES)
        source = lax.broadcasted_iota(jnp.int32, shape, 0)
        target = lax.broadcasted_iota(jnp.int32, shape, 1)
        slot, lane = target // LANES, target % LANES
        return jnp.where((source == slot * self.c1 + lane) & (lane < self.c1), 1.0, 0.0).astype(jnp.bfloat16)

    def unpack(self, ref, lane, spread, lo, hi, first, raw, place):
        tall = ref.shape[1]
        count = 2 * self.frames
        x = ref[:, :, lane : lane + EDGE * self.c1].reshape(count * tall, EDGE * self.c1)
        wide = jnp.dot(x, spread, preferred_element_type=jnp.float32)
        for k in range(lo, hi):
            v = wide[:, k * LANES : (k + 1) * LANES]
            ms = jnp.sum(v * v, axis=-1, keepdims=True) * (1.0 / self.c1)
            u = v * lax.rsqrt(ms + epsilon) * self.gain1
            u = u / (1.0 + jnp.exp(-u))
            c = place + k - lo
            for f in range(count):
                at = f * self.R
                for at_row, n, to in (
                    (0, self.rows, LOW),
                    (self.rows + SLAB - LOW, LOW, 0),
                    (self.rows + SLAB, HIGH, LOW + self.rows),
                ):
                    chunk = slice(f * tall + at_row, f * tall + at_row + n)
                    first[c, at + to : at + to + n, :] = u[chunk]
                    if f >= self.frames and (to == LOW or n == HIGH):
                        to += (f - self.frames) * self.R
                        raw[c, to : to + n, :] = v[chunk]

    def stack_first(self, c, first, stack):
        for k in range(9):
            off = (k // 3) * self.R + k % 3
            stack[c, :, k * LANES : (k + 1) * LANES] = first[c, off : off + self.M1, :].astype(jnp.bfloat16)

    def conv_first(self, get, wanted):
        acc = None
        for dc in range(3):
            part = jnp.dot(
                jnp.concatenate([get(c + dc) for c in wanted], axis=0),
                self.w1[dc].reshape(9 * LANES, self.c2),
                preferred_element_type=jnp.float32,
            )
            acc = part if acc is None else acc + part
        return acc

    def act_second(self, hid, keep):
        ms = jnp.sum(hid * hid, axis=-1, keepdims=True) * (1.0 / self.c2)
        u = hid * lax.rsqrt(ms + epsilon) * self.gain2
        u = u / (1.0 + jnp.exp(-u)) * self.live1
        return u if keep is None else u * keep

    def halves(self, c, value, low, high):
        count = value.shape[0]
        low[c, 0:count, :] = value[:, :LANES]
        high[c, 0:count, 0 : self.rest] = value[:, LANES:]
        high[c, 0 : count - 1, self.rest : 2 * self.rest] = value[1:, LANES:]

    def stack_second(self, c, low, high, stack):
        for k in range(9):
            off = (k // 3) * self.R + k % 3
            stack[c, :, k * LANES : (k + 1) * LANES] = low[c, off : off + self.M2, :].astype(jnp.bfloat16)
        for k in range(9, 15):
            off = (k - 9) // 2 * self.R + (k - 9) % 2 * 2
            stack[c, :, k * LANES : (k + 1) * LANES] = high[c, off : off + self.M2, :].astype(jnp.bfloat16)

    def conv_second(self, get, get_raw, wanted):
        acc = jnp.dot(
            jnp.concatenate([get_raw(m + LOW) for m in wanted], axis=0).astype(jnp.bfloat16),
            self.wsc[...],
            preferred_element_type=jnp.float32,
        )
        for dc in range(3):
            lhs = jnp.concatenate([get(m + dc) for m in wanted], axis=0)
            acc += jnp.dot(
                lhs[:, : 9 * LANES],
                self.w2m[dc].reshape(9 * LANES, self.c2),
                preferred_element_type=jnp.float32,
            )
            acc += jnp.dot(
                lhs[:, 9 * LANES :],
                self.w2r[dc].reshape(6 * LANES, self.c2),
                preferred_element_type=jnp.float32,
            )
        return acc

    def merged(self, c, value, keep, low, high):
        value = value * self.live2
        self.halves(c, value if keep is None else value * keep, low, high)


def inner(dims, mid, w1, w2m, w2r, wsc, g1, g2, stack1, stack2, raw, mer_a, mer_b, first, sec_a, sec_b):
    s = Steps(*dims, w1, w2m, w2r, wsc, g1, g2)
    sec_b[...] = jnp.zeros_like(sec_b)
    mer_a[...] = jnp.zeros_like(mer_a)
    mer_b[...] = jnp.zeros_like(mer_b)
    spread = s.spread()
    tail = 2 * s.frames * s.R
    first[:, tail:, :] = jnp.zeros((first.shape[0], first.shape[1] - tail, LANES), jnp.float32)
    for group in range(s.cols // EDGE):
        s.unpack(mid, group * EDGE * s.c1, spread, 0, EDGE, first, raw, group * EDGE)
    for c in range(s.cols):
        s.stack_first(c, first, stack1)
    hidden = list(range(LOW, s.cols))
    step = 7
    for start in range(0, len(hidden), step):
        wanted = hidden[start : start + step]
        acc = s.conv_first(lambda c: stack1[c - LOW], wanted)
        for i, c in enumerate(wanted):
            s.halves(c - LOW, s.act_second(acc[i * s.M1 : (i + 1) * s.M1], None), sec_a, sec_b)
    for c in range(len(hidden)):
        s.stack_second(c, sec_a, sec_b, stack2)
    wanted = list(range(LOW, s.cols - 2))
    acc = s.conv_second(
        lambda c: stack2[c - LOW], lambda c: raw[c - LOW, LOW : LOW + s.M2, :], wanted
    )
    for i in range(len(wanted)):
        s.merged(i, acc[i * s.M2 : (i + 1) * s.M2], None, mer_a, mer_b)


def outer(
    dims, got_a, got_b, w1, w2m, w2r, wsc, g1, g2, wdm, wdr, in_stack1, in_stack2, in_raw, in_mer_a, in_mer_b,
    out, left, right, first, raw, stack1, sec_a, sec_b, stack2, mer_a, mer_b, stack3, result,
):
    incoming("width", (got_a, got_b), left, right)
    s = Steps(*dims, w1, w2m, w2r, wsc, g1, g2)
    bf, f32 = jnp.bfloat16, jnp.float32
    cols, rest, R, M2 = s.cols, s.rest, s.R, s.M2
    sec_b[...] = jnp.zeros_like(sec_b)
    mer_a[...] = jnp.zeros_like(mer_a)
    mer_b[...] = jnp.zeros_like(mer_b)
    spread = s.spread()
    tail = 2 * s.frames * s.R
    first[:, tail:, :] = jnp.zeros((first.shape[0], first.shape[1] - tail, LANES), jnp.float32)
    s.unpack(left, 0, spread, EDGE - LOW, EDGE, first, raw, 0)
    s.unpack(right, 0, spread, 0, HIGH, first, raw, LOW)
    for c in range(LOW + HIGH):
        s.stack_first(c, first, stack1)

    def new_or(own, given, lo, hi):
        return lambda c: given(c - lo) if lo <= c < hi else own(c if c < lo else c - hi + lo)

    wanted = [0, 1, cols, cols + 1, cols + 2]
    acc = s.conv_first(new_or(lambda i: stack1[i], lambda i: in_stack1[i], LOW, LOW + cols), wanted)
    keeps = [s.keep_left, None, None, s.keep_right, s.keep_right]
    for i, keep in enumerate(keeps):
        s.halves(i, s.act_second(acc[i * s.M1 : (i + 1) * s.M1], keep), sec_a, sec_b)
    for c in range(len(wanted)):
        s.stack_second(c, sec_a, sec_b, stack2)
    wanted = [0, 1, cols - 2, cols - 1, cols]
    acc = s.conv_second(
        new_or(lambda i: stack2[i], lambda i: in_stack2[i], LOW, cols),
        new_or(
            lambda i: raw[i, LOW : LOW + M2, :], lambda i: in_raw[i, LOW : LOW + M2, :], LOW, LOW + cols
        ),
        wanted,
    )
    keeps = [None, None, None, None, s.keep_right]
    for i, keep in enumerate(keeps):
        s.merged(i, acc[i * M2 : (i + 1) * M2], keep, mer_a, mer_b)

    lows = new_or(lambda i: (mer_a, i), lambda i: (in_mer_a, i), LOW, cols - 2)
    highs = new_or(lambda i: (mer_b, i), lambda i: (in_mer_b, i), LOW, cols - 2)
    out_cols = cols // 2
    for j in range(out_cols):
        for dc in range(3):
            ref, c = lows(2 * j + dc)
            for dr in range(3):
                k = dc * 3 + dr
                stack3[j, :, k * LANES : (k + 1) * LANES] = ref[c, dr : dr + M2, :].astype(bf)
            ref, c = highs(2 * j + dc)
            for half in range(2):
                k = 9 + 2 * dc + half
                stack3[j, :, k * LANES : (k + 1) * LANES] = ref[c, 2 * half : 2 * half + M2, :].astype(bf)
    acc = jnp.dot(
        stack3[:, :, : 9 * LANES].reshape(out_cols * M2, 9 * LANES),
        wdm[...].reshape(9 * LANES, s.c2),
        preferred_element_type=f32,
    )
    acc += jnp.dot(
        stack3[:, :, 9 * LANES :].reshape(out_cols * M2, 6 * LANES),
        wdr[...].reshape(6 * LANES, s.c2),
        preferred_element_type=f32,
    )
    acc = acc.reshape(out_cols, M2, s.c2)
    result[0] = acc[:, :, :LANES]
    result[1, :, :, 0:rest] = acc[:, :, LANES:]
    for f in range(s.frames):
        for j in range(out_cols):
            a = result[0, j, pl.ds(f * R, s.rows // 2, stride=2), :]
            b = result[1, j, pl.ds(f * R, s.rows // 2, stride=2), :][:, :rest]
            out[f, :, j * s.c2 : (j + 1) * s.c2] = jnp.concatenate([a, b], axis=-1).astype(bf)


def up(n, k):
    return -(-n // k) * k


def cost(flops):
    return pl.CostEstimate(flops=flops, bytes_accessed=5 * 10**6, transcendentals=10**5)


def local(video_in, gain_first, gain_second, conv_first, conv_second, shortcut, downscale_weight):
    frames, rows, merged_cols = video_in.shape
    c1, c2 = shortcut.shape
    cols = merged_cols // c1
    rest = c2 - LANES
    dims = (frames, rows, cols, c1, c2)
    bf, f32 = jnp.bfloat16, jnp.float32
    vmem = pl.BlockSpec(memory_space=pltpu.VMEM)
    hbm = pl.BlockSpec(memory_space=pltpu.HBM)
    params = pltpu.CompilerParams(vmem_limit_bytes=14 * 1024 * 1024)
    small = pltpu.CompilerParams(vmem_limit_bytes=4 * 1024 * 1024)
    out_cols = cols // 2
    R = rows + LOW + HIGH
    M1 = up((frames + 1) * R + rows + 3, 16)
    M2 = up((frames - 1) * R + rows + 1, 16)
    first_rows = up(M1 + 2 * R + 2, 8)
    raw_rows = up(M2 + LOW, 8)
    held = M2 + 8

    source = [gain_first.reshape(1, c1), gain_second.reshape(1, c2), shortcut]
    source += [conv_first, conv_second, downscale_weight]
    own, g1, g2, wsc, w1, w2m, w2r, wdm, wdr = pl.pallas_call(
        functools.partial(arrange, c1),
        out_shape=[
            pltpu.VMEM(video_in.shape, bf),
            pltpu.VMEM((1, c1), f32),
            pltpu.VMEM((1, c2), f32),
            pltpu.VMEM((LANES, c2), bf),
            pltpu.VMEM((3, 3, 3, LANES, c2), bf),
            pltpu.VMEM((3, 3, 3, LANES, c2), bf),
            pltpu.VMEM((3, 3, 4, rest, c2), bf),
            pltpu.VMEM((3, 3, LANES, c2), bf),
            pltpu.VMEM((3, 4, rest, c2), bf),
        ],
        in_specs=[hbm] * 7,
        out_specs=[vmem] * 9,
        scratch_shapes=[pltpu.SemaphoreType.DMA((19,))],
        compiler_params=small,
        cost_estimate=cost(0),
        name="arrange",
    )(*[pltpu.with_memory_space_constraint(a, pltpu.HBM) for a in [video_in] + source])

    tall = rows + 2 * SLAB
    got = swap("tm", [video_in] * rounds("tm"))
    *slabs, prev = pl.pallas_call(
        rows_out,
        out_shape=[pltpu.VMEM((2 * frames, SLAB, merged_cols), bf)] * rounds("height")
        + [pltpu.VMEM(video_in.shape, bf)],
        in_specs=[vmem] * (1 + len(got)),
        out_specs=[vmem] * (1 + rounds("height")),
        compiler_params=small,
        cost_estimate=cost(0),
        name="rows_out",
    )(own, *got)
    got = swap("height", slabs)
    mid, *slabs = pl.pallas_call(
        functools.partial(cols_out, EDGE * c1),
        out_shape=[pltpu.VMEM((2 * frames, tall, merged_cols), bf)]
        + [pltpu.VMEM((2 * frames, tall, EDGE * c1), bf)] * 2,
        in_specs=[vmem] * (2 + len(got)),
        out_specs=[vmem] * 3,
        compiler_params=small,
        cost_estimate=cost(0),
        name="cols_out",
    )(own, prev, *got)
    got_a, got_b = swap("width", slabs)

    hid_in, mer_in = cols - 2, cols - 4
    passed = pl.pallas_call(
        functools.partial(inner, dims),
        out_shape=[
            pltpu.VMEM((cols, M1, 9 * LANES), bf),
            pltpu.VMEM((hid_in, M2, 15 * LANES), bf),
            pltpu.VMEM((cols, raw_rows, LANES), f32),
            pltpu.VMEM((mer_in, held, LANES), f32),
            pltpu.VMEM((mer_in, held, LANES), f32),
        ],
        in_specs=[vmem] * 7,
        out_specs=[vmem] * 5,
        scratch_shapes=[
            pltpu.VMEM((cols, first_rows, LANES), f32),
            pltpu.VMEM((hid_in, M1, LANES), f32),
            pltpu.VMEM((hid_in, M1, LANES), f32),
        ],
        compiler_params=params,
        cost_estimate=cost(4 * 10**9),
        name="inner",
    )(mid, w1, w2m, w2r, wsc, g1, g2)
    edge = LOW + HIGH
    return pl.pallas_call(
        functools.partial(outer, dims),
        out_shape=jax.ShapeDtypeStruct((frames, rows // 2, out_cols * c2), bf),
        in_specs=[vmem] * 15,
        out_specs=vmem,
        scratch_shapes=[
            pltpu.VMEM((2 * frames, tall, EDGE * c1), bf),
            pltpu.VMEM((2 * frames, tall, EDGE * c1), bf),
            pltpu.VMEM((edge, first_rows, LANES), f32),
            pltpu.VMEM((edge, raw_rows, LANES), f32),
            pltpu.VMEM((edge, M1, 9 * LANES), bf),
            pltpu.VMEM((edge, M1, LANES), f32),
            pltpu.VMEM((edge, M1, LANES), f32),
            pltpu.VMEM((edge, M2, 15 * LANES), bf),
            pltpu.VMEM((edge, held, LANES), f32),
            pltpu.VMEM((edge, held, LANES), f32),
            pltpu.VMEM((out_cols, M2, 15 * LANES), bf),
            pltpu.VMEM((2, out_cols, M2, LANES), f32),
        ],
        compiler_params=params,
        cost_estimate=cost(2 * 10**9),
        name="outer",
    )(got_a, got_b, w1, w2m, w2r, wsc, g1, g2, wdm, wdr, *passed)


def solution(mesh):
    placed = (P("tm", "height", "width"), P(), P(), P(), P(), P(), P())
    return jax.shard_map(
        local, mesh=mesh, in_specs=placed, out_specs=P("tm", "height", "width"), check_vma=False
    )
```

time: 80.4 us -> 25.4 us (0.32); the launches traced: 78.9 us -> 25.2 us
  waiting for transfers between devices: 26.5 us -> 3.34 us
  starting transfers between devices: 25.6 us -> 7.86 us
  Pallas kernels: 0 us -> 14 us
  local copies, waits for them, and re-layouts: 11.1 us -> 0 us
  matrix products: 8.16 us -> 0 us
  other arithmetic: 6.84 us -> 0 us
    ppermute x12 -> x5, waiting for transfers between devices: 26.5 us -> 3.34 us  [swap(): lax.ppermute(value, AXES, swap_pairs(axis, i))]
    ppermute x12 -> x5, starting transfers between devices: 25.6 us -> 7.86 us  [swap(): lax.ppermute(value, AXES, swap_pairs(axis, i))]
    pallas_call x0 -> x5, Pallas kernels: none -> 14 us  [the longest x1 5.86 us: local(): pl.pallas_call(functools.partial(inner, dims), out_shape=[pltpu.VMEM((col...]
    dot_general x22 -> x0, matrix products: 8.16 us -> none  [the longest x18 7.06 us: convolve(): jnp.dot(stacked.reshape(-1, 3 * c_in), filter_weight[depth_tap, row_tap]....]
    slice x21 -> x0, local copies, waits for them, and re-layouts: 7.71 us -> none  [the longest x9 4.66 us: halve_spatial(): border_filled[:, row_tap:row_tap + 2 * out_rows:2, col_tap:col_tap + 2 *...]
    concatenate x28 -> x0, other arithmetic: 5.43 us -> none  [the longest x16 3.96 us: convolve(): jnp.concatenate([window_slab[:, :, col_tap:col_tap + cols] for col_tap in...]
    add x2 -> x0, local copies, waits for them, and re-layouts: 1.39 us -> none  [convolve(): total + jnp.dot(stacked.reshape(-1, 3 * c_in), filter_weight[depth_tap, r...]
    reshape x1 -> x0, local copies, waits for them, and re-layouts: 1.05 us -> none  [local(): field = video_in.reshape(frames, rows, cols, c_in)]
  transfers between devices with their start and end apart: 12 -> 5, of which waited for: 10 -> 2; matrix products, arithmetic and copies ran while one was open for 4% -> 0% of each run, Pallas kernels for 0% -> 34%
where the time goes in v2:
time: 25.4 us; the launch traced here: 25.2 us
  Pallas kernels  14 us (55%)
  starting transfers between devices  7.86 us (31%)
  waiting for transfers between devices  3.34 us (13%)
    ppermute x5, starting transfers between devices, swap(): lax.ppermute(value, AXES, swap_pairs(axis, i))  7.86 us
    pallas_call x1, Pallas kernels, local(): pl.pallas_call(functools.partial(inner, dims), out_shape=[pltpu.VMEM((col...  5.86 us
    pallas_call x1, Pallas kernels, local(): pl.pallas_call(functools.partial(outer, dims), out_shape=jax.ShapeDtypeSt...  5.36 us
    ppermute x5, waiting for transfers between devices, swap(): lax.ppermute(value, AXES, swap_pairs(axis, i))  3.34 us
    pallas_call x1, Pallas kernels, local(): pl.pallas_call(functools.partial(arrange, c1), out_shape=[pltpu.VMEM(vide...  2.61 us
  transfers between devices with their start and end apart: 5, of which 2 were waited for; matrix products, arithmetic and copies ran while one was open for 0% of the time, Pallas kernels for 34%

profile of v2, /device:TPU:0, one launch (start us, length us, event | category | flops | bytes accessed | tf_op | source)
XLA Modules:
  0.0 25.2 jit_solution(10050488964218965055)
XLA Ops:
  0.0 0.5 %collective-permute-start.1 = (bf16[4,8,1536]{2,1,0:T(8,128)(2,1)}, bf16[4,8,1536]{2,1,0:T(8,128)(2,1)S(1)}, u32[]{:S(2)}, u32[]{:S(2)}) collective-permute-start(bf16[4,8,1536]{2,1,0:T(8,128)(2,1)} %x.1), channel_id=1, source_target_pairs={{0,1},{1,0},{2,3},{3,2},{4,5},{5,4},{6,7},{7,6},{8,16},{9,17},{10,... | collective-permute-start | bytes 294920 | tf_op jit(solution)/shard_map/ppermute | solution.py:41
  0.5 4.1 %collective-permute-start = (bf16[4,8,1536]{2,1,0:T(8,128)(2,1)}, bf16[4,8,1536]{2,1,0:T(8,128)(2,1)S(1)}, u32[]{:S(2)}, u32[]{:S(2)}) collective-permute-start(bf16[4,8,1536]{2,1,0:T(8,128)(2,1)} %x.1), channel_id=1, source_target_pairs={{0,8},{1,9},{2,10},{3,11},{4,12},{5,13},{6,14},{7,15},{8,0},{9,1},... | collective-permute-start | bytes 294920 | tf_op jit(solution)/shard_map/ppermute | solution.py:41
  4.6 2.6 %arrange.1 = (bf16[4,8,1536]{2,1,0:T(8,128)(2,1)S(1)}, f32[1,96]{1,0:T(1,128)S(1)}, f32[1,192]{1,0:T(1,128)S(1)}, bf16[128,192]{1,0:T(8,128)(2,1)S(1)}, bf16[3,3...) custom-call(bf16[4,8,1536]{2,1,0:T(8,128)(2,1)} %x.1, ...), custom_call_target="tpu_custom_call" | custom-call | bytes 5000000 | tf_op jit(solution)/shard_map/arrange/pallas_call | solution.py:387
  7.2 0.0 collective-permute-done.1.refs_1_
  7.2 0.2 collective-permute-done.refs_0_
  7.5 1.6 %collective-permute-start.2 = (bf16[8,4,1536]{2,1,0:T(4,128)(2,1)S(1)}, bf16[8,4,1536]{2,1,0:T(4,128)(2,1)S(1)}, u32[]{:S(2)}, u32[]{:S(2)}) collective-permute-start(bf16[8,4,1536]{2,1,0:T(4,128)(2,1)S(1)} %get-tuple-element.26), channel_id=1, source_target_pairs={{0,4},{1,5},{2,6},{3,7},{4,0},{5,1},{6,2},{7,3},{8,12},{9,13},{10,... | collective-permute-start | bytes 294920 | tf_op jit(solution)/shard_map/ppermute | solution.py:41
  9.0 3.1 %collective-permute-done.2.refs_0_ = bf16[8,4,1536]{2,1,0:T(4,128)(2,1)S(1)} collective-permute-done((bf16[8,4,1536]{2,1,0:T(4,128)(2,1)S(1)}, bf16[8,4,1536]{2,1,0:T(4,128)(2,1)S(1)}, u32[]{:S(2)}, u32[]{:S(2)}) %collective-permute-start.2) | collective-permute-done | bytes 98336 | tf_op jit(solution)/shard_map/ppermute | solution.py:41
  12.2 0.1 cols_out.1
  12.3 0.1 collective-permute-start.3
  12.3 1.6 %collective-permute-start.4 = (bf16[8,16,384]{2,1,0:T(8,128)(2,1)S(1)}, bf16[8,16,384]{2,1,0:T(8,128)(2,1)S(1)}, u32[]{:S(2)}, u32[]{:S(2)}) collective-permute-start(bf16[8,16,384]{2,1,0:T(8,128)(2,1)S(1)} %get-tuple-element.28), channel_id=1, source_target_pairs={{0,3},{1,2},{2,1},{3,0},{4,7},{5,6},{6,5},{7,4},{8,11},{9,10},{10,... | collective-permute-start | bytes 294920 | tf_op jit(solution)/shard_map/ppermute | solution.py:41
  14.0 5.9 %inner.1 = (bf16[16,80,1152]{2,1,0:T(8,128)(2,1)S(1)}, bf16[14,48,1920]{2,1,0:T(8,128)(2,1)S(1)}, f32[16,56,128]{2,1,0:T(8,128)S(1)}, f32[12,56,128]{2,1,0:T(8,128)S(1)}, f32[12,56,128]{2,1,0:T(8,128)S(1)}) custom-call(bf16[8,16,1536]{2,1,0:T(8,128)(2,1)S(1)} %get-tuple-element.37.mid, bf16[3,3,3,128,192]{4,3,2,1,0:T(8,128)(2,1)S(1)} %get-tuple-element.29.w1, ...), custom_call_target="tpu_custom_call" | custom-call | flops 4000000000 | bytes 5000000 | tf_op jit(solution)/shard_map/inner/pallas_call | solution.py:434
  19.8 0.0 collective-permute-done.3.got_a
  19.9 0.0 collective-permute-done.4.got_b
  19.9 5.4 %outer.1 = bf16[4,4,1536]{2,1,0:T(4,128)(2,1)} custom-call(bf16[8,16,384]{2,1,0:T(8,128)(2,1)S(1)} %collective-permute-done.3.got_a, bf16[8,16,384]{2,1,0:T(8,128)(2,1)S(1)} %collective-permute-done.4.got_b, bf16[3,3,3,128,192]{4,3,2,1,0:T(8,128)(2,1)S(1)} %get-tuple-element.29.w1, bf16[3,3,3,128,192]{4,3,2,1,0:T(8,128)(2,1)S(1)} %get-tuple-element.30.w2m, ...), custom_call_target="tpu_custom_call" | custom-call | flops 2000000000 | bytes 5000000 | tf_op jit(solution)/shard_map/outer/pallas_call | solution.py:455
  (1 shorter events, 0.0 us)
Async XLA Ops:
  0.0 7.2 %collective-permute-start.1 = (bf16[4,8,1536]{2,1,0:T(8,128)(2,1)}, bf16[4,8,1536]{2,1,0:T(8,128)(2,1)S(1)}, u32[]{:S(2)}, u32[]{:S(2)}) collective-permute-start(bf16[4,8,1536]{2,1,0:T(8,128)(2,1)} %x.1), channel_id=1, source_target_pairs={{0,1},{1,0},{2,3},{3,2},{4,5},{5,4},{6,7},{7,6},{8,16},{9,17},{10,... | collective-permute-start | bytes 294920 | tf_op jit(solution)/shard_map/ppermute | solution.py:41
  0.5 7.0 %collective-permute-start = (bf16[4,8,1536]{2,1,0:T(8,128)(2,1)}, bf16[4,8,1536]{2,1,0:T(8,128)(2,1)S(1)}, u32[]{:S(2)}, u32[]{:S(2)}) collective-permute-start(bf16[4,8,1536]{2,1,0:T(8,128)(2,1)} %x.1), channel_id=1, source_target_pairs={{0,8},{1,9},{2,10},{3,11},{4,12},{5,13},{6,14},{7,15},{8,0},{9,1},... | collective-permute-start | bytes 294920 | tf_op jit(solution)/shard_map/ppermute | solution.py:41
  7.5 4.7 %collective-permute-start.2 = (bf16[8,4,1536]{2,1,0:T(4,128)(2,1)S(1)}, bf16[8,4,1536]{2,1,0:T(4,128)(2,1)S(1)}, u32[]{:S(2)}, u32[]{:S(2)}) collective-permute-start(bf16[8,4,1536]{2,1,0:T(4,128)(2,1)S(1)} %get-tuple-element.26), channel_id=1, source_target_pairs={{0,4},{1,5},{2,6},{3,7},{4,0},{5,1},{6,2},{7,3},{8,12},{9,13},{10,... | collective-permute-start | bytes 294920 | tf_op jit(solution)/shard_map/ppermute | solution.py:41
  12.3 7.6 %collective-permute-start.3 = (bf16[8,16,384]{2,1,0:T(8,128)(2,1)S(1)}, bf16[8,16,384]{2,1,0:T(8,128)(2,1)S(1)}, u32[]{:S(2)}, u32[]{:S(2)}) collective-permute-start(bf16[8,16,384]{2,1,0:T(8,128)(2,1)S(1)} %get-tuple-element.27), channel_id=1, source_target_pairs={{0,1},{1,0},{2,3},{3,2},{4,5},{5,4},{6,7},{7,6},{8,9},{9,8},{10,11... | collective-permute-start | bytes 294920 | tf_op jit(solution)/shard_map/ppermute | solution.py:41
  12.3 7.5 %collective-permute-start.4 = (bf16[8,16,384]{2,1,0:T(8,128)(2,1)S(1)}, bf16[8,16,384]{2,1,0:T(8,128)(2,1)S(1)}, u32[]{:S(2)}, u32[]{:S(2)}) collective-permute-start(bf16[8,16,384]{2,1,0:T(8,128)(2,1)S(1)} %get-tuple-element.28), channel_id=1, source_target_pairs={{0,3},{1,2},{2,1},{3,0},{4,7},{5,6},{6,5},{7,4},{8,11},{9,10},{10,... | collective-permute-start | bytes 294920 | tf_op jit(solution)/shard_map/ppermute | solution.py:41

commit v3 on v2

v3 whole, which is shorter than its diff:
```python
import functools
import jax
import jax.numpy as jnp
from jax import lax
from jax.experimental import pallas as pl
from jax.experimental.pallas import tpu as pltpu
from jax.sharding import PartitionSpec as P

epsilon = 1e-06
AXES = ("tm", "height", "width")
LANES = 128
LOW, HIGH = 2, 3
EDGE = 4


def swap_pairs(axis, parity):
    sizes = [lax.axis_size(name) for name in AXES]
    place = AXES.index(axis)
    count = sizes[place]
    pairs = []
    for t in range(sizes[0]):
        for h in range(sizes[1]):
            for w in range(sizes[2]):
                source = [t, h, w]
                target = [t, h, w]
                other = source[place] + (1 if source[place] % 2 == parity else -1)
                if 0 <= other < count:
                    target[place] = other
                elif axis == "width":
                    target[place] = other % count
                else:
                    target[2] = w ^ 1
                pairs.append(
                    tuple((p[0] * sizes[1] + p[1]) * sizes[2] + p[2] for p in (source, target))
                )
    return pairs


def swap(axis, outgoing):
    return [lax.ppermute(value, AXES, swap_pairs(axis, i)) for i, value in enumerate(outgoing)]


def rounds(axis):
    return 1 if lax.axis_size(axis) == 2 else 2


def outgoing(axis, count, to_next, to_prev):
    even = lax.axis_index(axis) % 2 == 0
    return [jnp.where(even, *pair) for pair in ((to_next, to_prev), (to_prev, to_next))[:count]]


def incoming(axis, values):
    index, count = lax.axis_index(axis), lax.axis_size(axis)
    even = index % 2 == 0
    at_even, at_odd = values[0], values[-1]
    zero = jnp.zeros_like(at_even)
    if len(values) == 1:
        return jnp.where(even, zero, at_even), jnp.where(even, at_even, zero)
    return (
        jnp.where(index == 0, zero, jnp.where(even, at_odd, at_even)),
        jnp.where(index == count - 1, zero, jnp.where(even, at_even, at_odd)),
    )


def rows_out(own, *refs):
    got, slabs, prev, wide = refs[: rounds("tm")], refs[rounds("tm") : -2], refs[-2], refs[-1]
    prev[...] = incoming("tm", [ref[...] for ref in got])[0]
    frames, rows = own.shape[0], own.shape[1]
    for i, slab in enumerate(slabs):
        for f in range(2 * frames):
            block = (prev if f < frames else own)[f % frames].astype(jnp.float32)
            part = outgoing("height", len(slabs), block[rows - HIGH :], block[:HIGH])[i]
            wide[f * HIGH : (f + 1) * HIGH, :] = part
        slab[...] = wide[...].astype(jnp.bfloat16)


def cols_out(width, own, prev, *refs):
    got, rim, slabs, wide = refs[: rounds("height")], refs[rounds("height")], refs[-3:-1], refs[-1]
    frames, rows = own.shape[0], own.shape[1]
    above, below = incoming("height", [ref[...].astype(jnp.float32) for ref in got])
    for f in range(2 * frames):
        wide[f, 0:1, :] = jnp.zeros((1, wide.shape[2]), jnp.float32)
        wide[f, 1 : 1 + HIGH, :] = above[f * HIGH : (f + 1) * HIGH]
        wide[f, 1 + HIGH : 1 + 2 * HIGH, :] = below[f * HIGH : (f + 1) * HIGH]
        wide[f, 1 + 2 * HIGH :, :] = jnp.zeros((1, wide.shape[2]), jnp.float32)
    rim[...] = wide[...].astype(jnp.bfloat16)
    last = own.shape[2] - width
    for lo, hi, source in ((0, frames, prev), (frames, 2 * frames, own)):
        for slab, part in zip(slabs, outgoing("width", 2, source[:, :, last:], source[:, :, :width])):
            slab[lo:hi, 0:rows, :] = part
    for slab, part in zip(slabs, outgoing("width", 2, rim[:, :, last:], rim[:, :, :width])):
        slab[:, rows:, :] = part


def arrange(c1, x, gain1, gain2, shortcut, conv1, conv2, down, xv, g1, g2, wsc, w1, w2m, w2r, wdm, wdr, sems):
    c2 = g2.shape[1]
    rest = c2 - LANES
    copies = [
        pltpu.make_async_copy(x, xv, sems.at[0]),
        pltpu.make_async_copy(gain1, g1, sems.at[1]),
        pltpu.make_async_copy(gain2, g2, sems.at[2]),
        pltpu.make_async_copy(shortcut, wsc.at[pl.ds(0, c1)], sems.at[3]),
    ]
    for dc in range(3):
        moves = [
            (conv1.at[:, :, dc], w1.at[dc, :, :, pl.ds(0, c1)]),
            (conv2.at[:, :, dc, pl.ds(0, LANES)], w2m.at[dc]),
            (conv2.at[:, :, dc, pl.ds(LANES, rest)], w2r.at[dc, :, pl.ds(0, 3)]),
            (down.at[:, dc, pl.ds(0, LANES)], wdm.at[dc]),
            (down.at[:, dc, pl.ds(LANES, rest)], wdr.at[dc, pl.ds(0, 3)]),
        ]
        for i, (source, target) in enumerate(moves):
            copies.append(pltpu.make_async_copy(source, target, sems.at[4 + 5 * dc + i]))
    for copy in copies:
        copy.start()
    bf = jnp.bfloat16
    wsc[c1:] = jnp.zeros((LANES - c1, c2), bf)
    w1[:, :, :, c1:, :] = jnp.zeros((3, 3, 3, LANES - c1, c2), bf)
    w2r[:, :, 3] = jnp.zeros((3, 3, rest, c2), bf)
    wdr[:, 3] = jnp.zeros((3, rest, c2), bf)
    for copy in copies:
        copy.wait()


class Steps:
    def __init__(self, frames, rows, cols, c1, c2, w1, w2m, w2r, wsc, g1, g2):
        self.frames, self.rows, self.cols, self.c1, self.c2 = frames, rows, cols, c1, c2
        self.rest = c2 - LANES
        self.R = rows + LOW + HIGH
        self.M1 = up((frames + 1) * self.R + rows + 3, 16)
        self.M2 = up((frames - 1) * self.R + rows + 1, 16)
        self.pitch = rows + 2
        self.w1, self.w2m, self.w2r, self.wsc = w1, w2m, w2r, wsc
        gap = jnp.zeros((1, LANES - c1), jnp.float32)
        self.gain1 = jnp.concatenate([g1[...], gap], axis=-1)
        self.gain2 = None if g2 is None else g2[...]
        t, h, w = [lax.axis_index(name) for name in AXES]
        starts, top, left = [i == 0 for i in (t, h, w)]
        bottom, right = [i == lax.axis_size(name) - 1 for i, name in ((h, "height"), (w, "width"))]
        p = lax.broadcasted_iota(jnp.int32, (self.M1, 1), 0)
        dead = (p < 2 * self.R) & starts
        for f in range(frames + 2):
            q = p - f * self.R
            dead |= ((q == 0) & top) | (((q == rows + 1) | (q == rows + 2)) & bottom)
        self.live1 = jnp.where(dead, 0.0, 1.0).astype(jnp.float32)
        p = lax.broadcasted_iota(jnp.int32, (self.M2, 1), 0)
        dead = p < 0
        for f in range(frames):
            dead |= (p == f * self.R + rows) & bottom
        self.live2 = jnp.where(dead, 0.0, 1.0).astype(jnp.float32)
        self.keep_left = jnp.where(left, 0.0, 1.0).astype(jnp.float32)
        self.keep_right = jnp.where(right, 0.0, 1.0).astype(jnp.float32)

    def spread(self):
        shape = (EDGE * self.c1, EDGE * LANES)
        source = lax.broadcasted_iota(jnp.int32, shape, 0)
        target = lax.broadcasted_iota(jnp.int32, shape, 1)
        slot, lane = target // LANES, target % LANES
        return jnp.where((source == slot * self.c1 + lane) & (lane < self.c1), 1.0, 0.0).astype(jnp.bfloat16)

    def unpack(self, x, spread, lo, hi, first, raw, place, pieces):
        count, tall = x.shape[0], x.shape[1]
        wide = jnp.dot(
            x.reshape(count * tall, EDGE * self.c1), spread, preferred_element_type=jnp.float32
        )
        for k in range(lo, hi):
            v = wide[:, k * LANES : (k + 1) * LANES]
            ms = jnp.sum(v * v, axis=-1, keepdims=True) * (1.0 / self.c1)
            u = v * (0.5 * lax.rsqrt(ms + epsilon)) * self.gain1
            u = u + u * jnp.tanh(u)
            c = place + k - lo
            for f in range(count):
                at = f * self.R
                for source, n, to in pieces:
                    chunk = slice(f * tall + source, f * tall + source + n)
                    first[c, at + to : at + to + n, :] = u[chunk]
                    if f >= self.frames and to >= LOW:
                        to += (f - self.frames) * self.R
                        raw[c, to : to + n, :] = v[chunk]

    def own_pieces(self):
        return [(0, self.rows, LOW)]

    def rim_pieces(self, start):
        return [(start + 1 + HIGH - LOW, LOW, 0), (start + 1 + HIGH, HIGH, LOW + self.rows)]

    def stack_first(self, c, first, stack):
        for k in range(9):
            off = (k // 3) * self.R + k % 3
            stack[c, :, k * LANES : (k + 1) * LANES] = first[c, off : off + self.M1, :].astype(jnp.bfloat16)

    def conv_first(self, get, wanted):
        lhs = [jnp.concatenate([get(c + dc) for dc in range(3)], axis=-1) for c in wanted]
        return jnp.dot(
            jnp.concatenate(lhs, axis=0),
            self.w1[...].reshape(27 * LANES, self.c2),
            preferred_element_type=jnp.float32,
        )

    def act_second(self, hid, keep):
        ms = jnp.sum(hid * hid, axis=-1, keepdims=True) * (1.0 / self.c2)
        scale = 0.5 * lax.rsqrt(ms + epsilon) * self.live1
        u = hid * (scale if keep is None else scale * keep) * self.gain2
        return u + u * jnp.tanh(u)

    def halves(self, c, value, low, high):
        count = value.shape[0]
        low[c, 0:count, :] = value[:, :LANES]
        high[c, 0:count, 0 : self.rest] = value[:, LANES:]
        high[c, 0 : count - 1, self.rest : 2 * self.rest] = value[1:, LANES:]

    def stack_second(self, c, low, high, stack):
        for k in range(9):
            off = (k // 3) * self.R + k % 3
            stack[c, :, k * LANES : (k + 1) * LANES] = low[c, off : off + self.M2, :].astype(jnp.bfloat16)
        for k in range(9, 15):
            off = (k - 9) // 2 * self.R + (k - 9) % 2 * 2
            stack[c, :, k * LANES : (k + 1) * LANES] = high[c, off : off + self.M2, :].astype(jnp.bfloat16)

    def conv_second(self, get, get_raw, wanted):
        mains = [[get(m + dc)[:, : 9 * LANES] for dc in range(3)] for m in wanted]
        rests = [[get(m + dc)[:, 9 * LANES :] for dc in range(3)] for m in wanted]
        lhs = [
            jnp.concatenate(main + rest + [get_raw(m + LOW).astype(jnp.bfloat16)], axis=-1)
            for m, main, rest in zip(wanted, mains, rests)
        ]
        rhs = [self.w2m[...].reshape(27 * LANES, self.c2), self.w2r[...].reshape(18 * LANES, self.c2)]
        return jnp.dot(
            jnp.concatenate(lhs, axis=0),
            jnp.concatenate(rhs + [self.wsc[...]], axis=0),
            preferred_element_type=jnp.float32,
        )

    def merged(self, c, value, keep, low, high):
        value = value * (self.live2 if keep is None else self.live2 * keep)
        n = self.rows + 1
        for f in range(self.frames):
            at = f * self.pitch
            chunk = value[f * self.R : f * self.R + n]
            low[c, at : at + n, :] = chunk[:, :LANES]
            high[c, at : at + n, 0 : self.rest] = chunk[:, LANES:]
            high[c, at : at + n - 1, self.rest : 2 * self.rest] = chunk[1:, LANES:]

    def down(self, lows, highs, wanted, stack, wdm, wdr, result):
        bf = jnp.bfloat16
        count = stack.shape[1]
        for j in wanted:
            for dc in range(3):
                ref, c = lows(2 * j + dc)
                for dr in range(3):
                    k = dc * 3 + dr
                    stack[j, :, k * LANES : (k + 1) * LANES] = ref[c, pl.ds(dr, count, stride=2), :].astype(bf)
                ref, c = highs(2 * j + dc)
                for half in range(2):
                    k = 9 + 2 * dc + half
                    part = ref[c, pl.ds(2 * half, count, stride=2), :]
                    stack[j, :, k * LANES : (k + 1) * LANES] = part.astype(bf)
        acc = jnp.dot(
            jnp.concatenate([stack[j] for j in wanted], axis=0),
            jnp.concatenate([wdm[...].reshape(9 * LANES, self.c2), wdr[...].reshape(6 * LANES, self.c2)], axis=0),
            preferred_element_type=jnp.float32,
        )
        for i, j in enumerate(wanted):
            result(j, acc[i * count : (i + 1) * count])


def early(dims, own, prev, g1, first, raw):
    s = Steps(*dims, None, None, None, None, g1, None)
    tail = 2 * s.frames * s.R
    first[:, tail:, :] = jnp.zeros((first.shape[0], first.shape[1] - tail, LANES), jnp.float32)
    spread = s.spread()
    for group in range(s.cols // EDGE):
        lanes = slice(group * EDGE * s.c1, (group + 1) * EDGE * s.c1)
        x = jnp.concatenate([prev[:, :, lanes], own[:, :, lanes]], axis=0)
        s.unpack(x, spread, 0, EDGE, first, raw, group * EDGE, s.own_pieces())


def inner(
    dims, rim, w1, w2m, w2r, wsc, g1, g2, _first, _raw, first, raw, stack1, stack2, mer_a, mer_b, sec_a, sec_b
):
    s = Steps(*dims, w1, w2m, w2r, wsc, g1, g2)
    sec_b[...] = jnp.zeros_like(sec_b)
    mer_a[...] = jnp.zeros_like(mer_a)
    mer_b[...] = jnp.zeros_like(mer_b)
    spread = s.spread()
    for group in range(s.cols // EDGE):
        x = rim[:, :, group * EDGE * s.c1 : (group + 1) * EDGE * s.c1]
        s.unpack(x, spread, 0, EDGE, first, raw, group * EDGE, s.rim_pieces(0))
    for c in range(s.cols):
        s.stack_first(c, first, stack1)
    hidden = list(range(LOW, s.cols))
    step = 7
    for start in range(0, len(hidden), step):
        wanted = hidden[start : start + step]
        acc = s.conv_first(lambda c: stack1[c - LOW], wanted)
        for i, c in enumerate(wanted):
            s.halves(c - LOW, s.act_second(acc[i * s.M1 : (i + 1) * s.M1], None), sec_a, sec_b)
            s.stack_second(c - LOW, sec_a, sec_b, stack2)
    merged = list(range(LOW, s.cols - 2))
    step = 6
    for start in range(0, len(merged), step):
        wanted = merged[start : start + step]
        acc = s.conv_second(
            lambda c: stack2[c - LOW], lambda c: raw[c - LOW, LOW : LOW + s.M2, :], wanted
        )
        for i, c in enumerate(wanted):
            s.merged(c - LOW, acc[i * s.M2 : (i + 1) * s.M2], None, mer_a, mer_b)


def outer(
    dims, got_a, got_b, w1, w2m, w2r, wsc, g1, g2, wdm, wdr, in_raw, in_stack1, in_stack2, in_mer_a, in_mer_b,
    out, first, raw, stack1, sec_a, sec_b, stack2, mer_a, mer_b, stack3,
):
    s = Steps(*dims, w1, w2m, w2r, wsc, g1, g2)
    cols, M1, M2 = s.cols, s.M1, s.M2
    sec_b[...] = jnp.zeros_like(sec_b)
    mer_a[...] = jnp.zeros_like(mer_a)
    mer_b[...] = jnp.zeros_like(mer_b)
    tail = 2 * s.frames * s.R
    first[:, tail:, :] = jnp.zeros((first.shape[0], first.shape[1] - tail, LANES), jnp.float32)
    spread = s.spread()
    left, right = incoming("width", [got_a[...], got_b[...]])
    pieces = s.own_pieces() + s.rim_pieces(s.rows)
    s.unpack(left, spread, EDGE - LOW, EDGE, first, raw, 0, pieces)
    s.unpack(right, spread, 0, HIGH, first, raw, LOW, pieces)
    for c in range(LOW + HIGH):
        s.stack_first(c, first, stack1)

    def new_or(own, given, lo, hi):
        return lambda c: given(c - lo) if lo <= c < hi else own(c if c < lo else c - hi + lo)

    def store(j, value):
        n = s.rows // 2
        for f in range(s.frames):
            at = f * s.pitch // 2
            out[f, :, j * s.c2 : (j + 1) * s.c2] = value[at : at + n].astype(jnp.bfloat16)

    lows = new_or(lambda i: (mer_a, i), lambda i: (in_mer_a, i), LOW, cols - 2)
    highs = new_or(lambda i: (mer_b, i), lambda i: (in_mer_b, i), LOW, cols - 2)
    out_cols = cols // 2
    get1 = new_or(lambda i: stack1[i], lambda i: in_stack1[i], LOW, LOW + cols)
    get2 = new_or(lambda i: stack2[i], lambda i: in_stack2[i], LOW, cols)
    get_raw = new_or(
        lambda i: raw[i, LOW : LOW + M2, :], lambda i: in_raw[i, LOW : LOW + M2, :], LOW, LOW + cols
    )
    sides = [
        ([0, 1], [s.keep_left, None], [0, 1], [None, None], 0),
        ([cols, cols + 1, cols + 2], [None] + [s.keep_right] * 2, [cols - 2, cols - 1, cols], [None, None, s.keep_right], 2),
    ]
    for wanted, keeps, _, _, at in sides:
        acc = s.conv_first(get1, wanted)
        for i, keep in enumerate(keeps):
            s.halves(at + i, s.act_second(acc[i * M1 : (i + 1) * M1], keep), sec_a, sec_b)
            s.stack_second(at + i, sec_a, sec_b, stack2)
    s.down(lows, highs, list(range(1, out_cols - 2)), stack3, wdm, wdr, store)
    for _, _, wanted, keeps, at in sides:
        acc = s.conv_second(get2, get_raw, wanted)
        for i, keep in enumerate(keeps):
            s.merged(at + i, acc[i * M2 : (i + 1) * M2], keep, mer_a, mer_b)
    s.down(lows, highs, [0, out_cols - 2, out_cols - 1], stack3, wdm, wdr, store)


def up(n, k):
    return -(-n // k) * k


def cost(flops):
    return pl.CostEstimate(flops=flops, bytes_accessed=5 * 10**6, transcendentals=10**5)


def local(video_in, gain_first, gain_second, conv_first, conv_second, shortcut, downscale_weight):
    frames, rows, merged_cols = video_in.shape
    c1, c2 = shortcut.shape
    cols = merged_cols // c1
    rest = c2 - LANES
    dims = (frames, rows, cols, c1, c2)
    bf, f32 = jnp.bfloat16, jnp.float32
    vmem = pl.BlockSpec(memory_space=pltpu.VMEM)
    hbm = pl.BlockSpec(memory_space=pltpu.HBM)
    params = pltpu.CompilerParams(vmem_limit_bytes=14 * 1024 * 1024)
    small = pltpu.CompilerParams(vmem_limit_bytes=4 * 1024 * 1024)
    out_cols = cols // 2
    R = rows + LOW + HIGH
    M1 = up((frames + 1) * R + rows + 3, 16)
    M2 = up((frames - 1) * R + rows + 1, 16)
    first_rows = up(M1 + 2 * R + 2, 8)
    raw_rows = up(M2 + LOW, 8)
    count = up((frames - 1) * (rows + 2) // 2 + rows // 2, 8)
    held = up(2 * count + 1, 8)

    source = [gain_first.reshape(1, c1), gain_second.reshape(1, c2), shortcut]
    source += [conv_first, conv_second, downscale_weight]
    own, g1, g2, wsc, w1, w2m, w2r, wdm, wdr = pl.pallas_call(
        functools.partial(arrange, c1),
        out_shape=[
            pltpu.VMEM(video_in.shape, bf),
            pltpu.VMEM((1, c1), f32),
            pltpu.VMEM((1, c2), f32),
            pltpu.VMEM((LANES, c2), bf),
            pltpu.VMEM((3, 3, 3, LANES, c2), bf),
            pltpu.VMEM((3, 3, 3, LANES, c2), bf),
            pltpu.VMEM((3, 3, 4, rest, c2), bf),
            pltpu.VMEM((3, 3, LANES, c2), bf),
            pltpu.VMEM((3, 4, rest, c2), bf),
        ],
        in_specs=[hbm] * 7,
        out_specs=[vmem] * 9,
        scratch_shapes=[pltpu.SemaphoreType.DMA((19,))],
        compiler_params=small,
        cost_estimate=cost(0),
        name="arrange",
    )(*[pltpu.with_memory_space_constraint(a, pltpu.HBM) for a in [video_in] + source])

    tall = 2 * rows
    got = swap("tm", [video_in] * rounds("tm"))
    *slabs, prev = pl.pallas_call(
        rows_out,
        out_shape=[pltpu.VMEM((2 * frames * HIGH, merged_cols), bf)] * rounds("height")
        + [pltpu.VMEM(video_in.shape, bf)],
        in_specs=[vmem] * (1 + len(got)),
        out_specs=[vmem] * (1 + rounds("height")),
        scratch_shapes=[pltpu.VMEM((2 * frames * HIGH, merged_cols), f32)],
        compiler_params=small,
        cost_estimate=cost(0),
        name="rows_out",
    )(own, *got)
    got = swap("height", slabs)
    first, raw = pl.pallas_call(
        functools.partial(early, dims),
        out_shape=[
            pltpu.VMEM((cols, first_rows, LANES), f32),
            pltpu.VMEM((cols, raw_rows, LANES), f32),
        ],
        in_specs=[vmem] * 3,
        out_specs=[vmem] * 2,
        compiler_params=small,
        cost_estimate=cost(10**9),
        name="early",
    )(own, prev, g1)
    rim, *slabs = pl.pallas_call(
        functools.partial(cols_out, EDGE * c1),
        out_shape=[pltpu.VMEM((2 * frames, 2 + 2 * HIGH, merged_cols), bf)]
        + [pltpu.VMEM((2 * frames, tall, EDGE * c1), bf)] * 2,
        in_specs=[vmem] * (2 + len(got)),
        out_specs=[vmem] * 3,
        scratch_shapes=[pltpu.VMEM((2 * frames, 2 + 2 * HIGH, merged_cols), f32)],
        compiler_params=small,
        cost_estimate=cost(0),
        name="cols_out",
    )(own, prev, *got)
    got_a, got_b = swap("width", slabs)

    hid_in, mer_in = cols - 2, cols - 4
    _, *passed = pl.pallas_call(
        functools.partial(inner, dims),
        out_shape=[
            pltpu.VMEM((cols, first_rows, LANES), f32),
            pltpu.VMEM((cols, raw_rows, LANES), f32),
            pltpu.VMEM((cols, M1, 9 * LANES), bf),
            pltpu.VMEM((hid_in, M2, 15 * LANES), bf),
            pltpu.VMEM((mer_in, held, LANES), f32),
            pltpu.VMEM((mer_in, held, LANES), f32),
        ],
        in_specs=[vmem] * 9,
        out_specs=[vmem] * 6,
        scratch_shapes=[
            pltpu.VMEM((hid_in, M1, LANES), f32),
            pltpu.VMEM((hid_in, M1, LANES), f32),
        ],
        input_output_aliases={7: 0, 8: 1},
        compiler_params=params,
        cost_estimate=cost(4 * 10**9),
        name="inner",
    )(rim, w1, w2m, w2r, wsc, g1, g2, first, raw)
    edge = LOW + HIGH
    return pl.pallas_call(
        functools.partial(outer, dims),
        out_shape=jax.ShapeDtypeStruct((frames, rows // 2, out_cols * c2), bf),
        in_specs=[vmem] * 15,
        out_specs=vmem,
        scratch_shapes=[
            pltpu.VMEM((edge, first_rows, LANES), f32),
            pltpu.VMEM((edge, raw_rows, LANES), f32),
            pltpu.VMEM((edge, M1, 9 * LANES), bf),
            pltpu.VMEM((edge, M1, LANES), f32),
            pltpu.VMEM((edge, M1, LANES), f32),
            pltpu.VMEM((edge, M2, 15 * LANES), bf),
            pltpu.VMEM((edge, held, LANES), f32),
            pltpu.VMEM((edge, held, LANES), f32),
            pltpu.VMEM((out_cols, count, 15 * LANES), bf),
        ],
        compiler_params=params,
        cost_estimate=cost(2 * 10**9),
        name="outer",
    )(got_a, got_b, w1, w2m, w2r, wsc, g1, g2, wdm, wdr, *passed)


def solution(mesh):
    placed = (P("tm", "height", "width"), P(), P(), P(), P(), P(), P())
    return jax.shard_map(
        local, mesh=mesh, in_specs=placed, out_specs=P("tm", "height", "width"), check_vma=False
    )
```

time: 25.4 us -> 23 us (0.906)
  Pallas kernels: 14 us -> 12.4 us
  waiting for transfers between devices: 3.34 us -> 2.5 us
    pallas_call x1, Pallas kernels: 5.36 us -> 3.71 us  [local(): pl.pallas_call(functools.partial(outer, dims), out_shape=jax.ShapeDtypeSt...]
    ppermute x5, waiting for transfers between devices: 3.34 us -> 2.5 us  [swap(): lax.ppermute(value, AXES, swap_pairs(axis, i))]
    pallas_call x1 -> x2, Pallas kernels: 0.03 us -> 0.66 us  [the longest x1 0.57 us: local(): pl.pallas_call(functools.partial(early, dims), out_shape=[pltpu.VMEM((col...]
    pallas_call x1, Pallas kernels: 5.86 us -> 5.31 us  [local(): pl.pallas_call(functools.partial(inner, dims), out_shape=[pltpu.VMEM((col...]
  transfers between devices with their start and end apart: 5 -> 5, of which waited for: 2 -> 2; matrix products, arithmetic and copies ran while one was open for 0% -> 0% of each run, Pallas kernels for 34% -> 37%
where the time goes in v3:
time: 23 us; the launch traced here: 22.8 us
  Pallas kernels  12.4 us (54%)
  starting transfers between devices  7.86 us (34%)
  waiting for transfers between devices  2.5 us (11%)
    ppermute x5, starting transfers between devices, swap(): lax.ppermute(value, AXES, swap_pairs(axis, i))  7.86 us
    pallas_call x1, Pallas kernels, local(): pl.pallas_call(functools.partial(inner, dims), out_shape=[pltpu.VMEM((col...  5.31 us
    pallas_call x1, Pallas kernels, local(): pl.pallas_call(functools.partial(outer, dims), out_shape=jax.ShapeDtypeSt...  3.71 us
    pallas_call x1, Pallas kernels, local(): pl.pallas_call(functools.partial(arrange, c1), out_shape=[pltpu.VMEM(vide...  2.61 us
    ppermute x5, waiting for transfers between devices, swap(): lax.ppermute(value, AXES, swap_pairs(axis, i))  2.5 us
    pallas_call x1, Pallas kernels, local(): pl.pallas_call(functools.partial(early, dims), out_shape=[pltpu.VMEM((col...  0.57 us
  transfers between devices with their start and end apart: 5, of which 2 were waited for; matrix products, arithmetic and copies ran while one was open for 0% of the time, Pallas kernels for 37%

profile of v3, /device:TPU:0, one launch (start us, length us, event | category | flops | bytes accessed | tf_op | source)
XLA Modules:
  0.0 22.8 jit_solution(891080479085223064)
XLA Ops:
  0.0 0.5 %collective-permute-start.1 = (bf16[4,8,1536]{2,1,0:T(8,128)(2,1)}, bf16[4,8,1536]{2,1,0:T(8,128)(2,1)S(1)}, u32[]{:S(2)}, u32[]{:S(2)}) collective-permute-start(bf16[4,8,1536]{2,1,0:T(8,128)(2,1)} %x.1), channel_id=1, source_target_pairs={{0,1},{1,0},{2,3},{3,2},{4,5},{5,4},{6,7},{7,6},{8,16},{9,17},{10,... | collective-permute-start | bytes 294920 | tf_op jit(solution)/shard_map/ppermute | solution.py:40
  0.5 4.1 %collective-permute-start = (bf16[4,8,1536]{2,1,0:T(8,128)(2,1)}, bf16[4,8,1536]{2,1,0:T(8,128)(2,1)S(1)}, u32[]{:S(2)}, u32[]{:S(2)}) collective-permute-start(bf16[4,8,1536]{2,1,0:T(8,128)(2,1)} %x.1), channel_id=1, source_target_pairs={{0,8},{1,9},{2,10},{3,11},{4,12},{5,13},{6,14},{7,15},{8,0},{9,1},... | collective-permute-start | bytes 294920 | tf_op jit(solution)/shard_map/ppermute | solution.py:40
  4.6 2.6 %arrange.1 = (bf16[4,8,1536]{2,1,0:T(8,128)(2,1)S(1)}, f32[1,96]{1,0:T(1,128)S(1)}, f32[1,192]{1,0:T(1,128)S(1)}, bf16[128,192]{1,0:T(8,128)(2,1)S(1)}, bf16[3,3...) custom-call(bf16[4,8,1536]{2,1,0:T(8,128)(2,1)} %x.1, ...), custom_call_target="tpu_custom_call" | custom-call | bytes 5000000 | tf_op jit(solution)/shard_map/arrange/pallas_call | solution.py:393
  7.2 0.0 collective-permute-done.1.refs_1_
  7.2 0.2 collective-permute-done.refs_0_
  7.4 0.1 rows_out.1
  7.5 1.6 %collective-permute-start.2 = (bf16[24,1536]{1,0:T(8,128)(2,1)S(1)}, bf16[24,1536]{1,0:T(8,128)(2,1)S(1)}, u32[]{:S(2)}, u32[]{:S(2)}) collective-permute-start(bf16[24,1536]{1,0:T(8,128)(2,1)S(1)} %get-tuple-element.28), channel_id=1, source_target_pairs={{0,4},{1,5},{2,6},{3,7},{4,0},{5,1},{6,2},{7,3},{8,12},{9,13},{10,... | collective-permute-start | bytes 221192 | tf_op jit(solution)/shard_map/ppermute | solution.py:40
  9.1 0.6 %early.1 = (f32[16,112,128]{2,1,0:T(8,128)S(1)}, f32[16,56,128]{2,1,0:T(8,128)S(1)}) custom-call(bf16[4,8,1536]{2,1,0:T(8,128)(2,1)S(1)} %get-tuple-element.26.own, bf16[4,8,1536]{2,1,0:T(8,128)(2,1)S(1)} %get-tuple-element.27.prev, f32[1,96]{1,0:T(1,128)S(1)} %get-tuple-element.35.g1), custom_call_target="tpu_custom_call" | custom-call | flops 1000000000 | bytes 5000000 | tf_op jit(solution)/shard_map/early/pallas_call | solution.py:428
  9.7 2.3 %collective-permute-done.2.refs_0_ = bf16[24,1536]{1,0:T(8,128)(2,1)S(1)} collective-permute-done((bf16[24,1536]{1,0:T(8,128)(2,1)S(1)}, bf16[24,1536]{1,0:T(8,128)(2,1)S(1)}, u32[]{:S(2)}, u32[]{:S(2)}) %collective-permute-start.2) | collective-permute-done | bytes 73760 | tf_op jit(solution)/shard_map/ppermute | solution.py:40
  11.9 0.1 cols_out.1
  12.1 0.1 collective-permute-start.3
  12.2 1.6 %collective-permute-start.4 = (bf16[8,16,384]{2,1,0:T(8,128)(2,1)S(1)}, bf16[8,16,384]{2,1,0:T(8,128)(2,1)S(1)}, u32[]{:S(2)}, u32[]{:S(2)}) collective-permute-start(bf16[8,16,384]{2,1,0:T(8,128)(2,1)S(1)} %get-tuple-element.30), channel_id=1, source_target_pairs={{0,3},{1,2},{2,1},{3,0},{4,7},{5,6},{6,5},{7,4},{8,11},{9,10},{10,... | collective-permute-start | bytes 294920 | tf_op jit(solution)/shard_map/ppermute | solution.py:40
  13.8 5.3 %inner.1 = (f32[16,112,128]{2,1,0:T(8,128)S(1)}, f32[16,56,128]{2,1,0:T(8,128)S(1)}, bf16[16,80,1152]{2,1,0:T(8,128)(2,1)S(1)}, bf16[14,48,1920]{2,1,0:T(8,128)(...) custom-call(bf16[8,8,1536]{2,1,0:T(8,128)(2,1)S(1)} %get-tuple-eleme, ...), custom_call_target="tpu_custom_call", output_to_operand_aliasing={{0}: (7, {}), {1}: (8, {})} | custom-call | flops 4000000000 | bytes 5000000 | tf_op jit(solution)/shard_map/inner/pallas_call | solution.py:454
  19.1 0.0 collective-permute-done.3.got_a
  19.1 0.0 collective-permute-done.4.got_b
  19.1 3.7 %outer.1 = bf16[4,4,1536]{2,1,0:T(4,128)(2,1)} custom-call(bf16[8,16,384]{2,1,0:T(8,128)(2,1)S(1)} %collective-permute-done.3.got_a, bf16[8,16,384]{2,1,0:T(8,128)(2,1)S(1)} %collective-permute-done.4.got_b, bf16[3,3,3,128,192]{4,3,2,1,0:T(8,128)(2,1)S(1)} %get-tuple-element.31.w1, bf16[3,3,3,128,192]{4,3,2,1,0:T(8,128)(2,1)S(1)} %get-tuple-element.32.w2m, ...), custom_call_target="tpu_custom_call" | custom-call | flops 2000000000 | bytes 5000000 | tf_op jit(solution)/shard_map/outer/pallas_call | solution.py:476
Async XLA Ops:
  0.0 7.2 %collective-permute-start.1 = (bf16[4,8,1536]{2,1,0:T(8,128)(2,1)}, bf16[4,8,1536]{2,1,0:T(8,128)(2,1)S(1)}, u32[]{:S(2)}, u32[]{:S(2)}) collective-permute-start(bf16[4,8,1536]{2,1,0:T(8,128)(2,1)} %x.1), channel_id=1, source_target_pairs={{0,1},{1,0},{2,3},{3,2},{4,5},{5,4},{6,7},{7,6},{8,16},{9,17},{10,... | collective-permute-start | bytes 294920 | tf_op jit(solution)/shard_map/ppermute | solution.py:40
  0.5 7.0 %collective-permute-start = (bf16[4,8,1536]{2,1,0:T(8,128)(2,1)}, bf16[4,8,1536]{2,1,0:T(8,128)(2,1)S(1)}, u32[]{:S(2)}, u32[]{:S(2)}) collective-permute-start(bf16[4,8,1536]{2,1,0:T(8,128)(2,1)} %x.1), channel_id=1, source_target_pairs={{0,8},{1,9},{2,10},{3,11},{4,12},{5,13},{6,14},{7,15},{8,0},{9,1},... | collective-permute-start | bytes 294920 | tf_op jit(solution)/shard_map/ppermute | solution.py:40
  7.5 4.4 %collective-permute-start.2 = (bf16[24,1536]{1,0:T(8,128)(2,1)S(1)}, bf16[24,1536]{1,0:T(8,128)(2,1)S(1)}, u32[]{:S(2)}, u32[]{:S(2)}) collective-permute-start(bf16[24,1536]{1,0:T(8,128)(2,1)S(1)} %get-tuple-element.28), channel_id=1, source_target_pairs={{0,4},{1,5},{2,6},{3,7},{4,0},{5,1},{6,2},{7,3},{8,12},{9,13},{10,... | collective-permute-start | bytes 221192 | tf_op jit(solution)/shard_map/ppermute | solution.py:40
  12.1 7.0 %collective-permute-start.3 = (bf16[8,16,384]{2,1,0:T(8,128)(2,1)S(1)}, bf16[8,16,384]{2,1,0:T(8,128)(2,1)S(1)}, u32[]{:S(2)}, u32[]{:S(2)}) collective-permute-start(bf16[8,16,384]{2,1,0:T(8,128)(2,1)S(1)} %get-tuple-element.29), channel_id=1, source_target_pairs={{0,1},{1,0},{2,3},{3,2},{4,5},{5,4},{6,7},{7,6},{8,9},{9,8},{10,11... | collective-permute-start | bytes 294920 | tf_op jit(solution)/shard_map/ppermute | solution.py:40
  12.2 7.0 %collective-permute-start.4 = (bf16[8,16,384]{2,1,0:T(8,128)(2,1)S(1)}, bf16[8,16,384]{2,1,0:T(8,128)(2,1)S(1)}, u32[]{:S(2)}, u32[]{:S(2)}) collective-permute-start(bf16[8,16,384]{2,1,0:T(8,128)(2,1)S(1)} %get-tuple-element.30), channel_id=1, source_target_pairs={{0,3},{1,2},{2,1},{3,0},{4,7},{5,6},{6,5},{7,4},{8,11},{9,10},{10,... | collective-permute-start | bytes 294920 | tf_op jit(solution)/shard_map/ppermute | solution.py:40

commit v4 on v3

--- a/solution.py
+++ b/solution.py
@@ -75,21 +75,25 @@
 
 
 def cols_out(width, own, prev, *refs):
-    got, rim, slabs, wide = refs[: rounds("height")], refs[rounds("height")], refs[-3:-1], refs[-1]
-    frames, rows = own.shape[0], own.shape[1]
-    above, below = incoming("height", [ref[...].astype(jnp.float32) for ref in got])
+    count = rounds("height")
+    got, rim, slabs, (above, below) = refs[:count], refs[count], refs[-4:-2], refs[-2:]
+    frames, rows, lanes = own.shape
+    values = incoming("height", [ref[...].astype(jnp.float32) for ref in got])
+    for k in range(lanes // LANES):
+        tile = slice(k * LANES, (k + 1) * LANES)
+        for ref, value in zip((above, below), values):
+            ref[k] = value[:, tile]
+        parts = [above[k, pl.ds(r, 2 * frames, stride=HIGH), :] for r in range(HIGH - LOW, HIGH)]
+        parts += [below[k, pl.ds(r, 2 * frames, stride=HIGH), :] for r in range(HIGH)]
+        parts.append(jnp.zeros((rim.shape[0] - len(parts) * 2 * frames, LANES), jnp.float32))
+        rim[:, tile] = jnp.concatenate(parts, axis=0).astype(jnp.bfloat16)
+    last = lanes - width
     for f in range(2 * frames):
-        wide[f, 0:1, :] = jnp.zeros((1, wide.shape[2]), jnp.float32)
-        wide[f, 1 : 1 + HIGH, :] = above[f * HIGH : (f + 1) * HIGH]
-        wide[f, 1 + HIGH : 1 + 2 * HIGH, :] = below[f * HIGH : (f + 1) * HIGH]
-        wide[f, 1 + 2 * HIGH :, :] = jnp.zeros((1, wide.shape[2]), jnp.float32)
-    rim[...] = wide[...].astype(jnp.bfloat16)
-    last = own.shape[2] - width
-    for lo, hi, source in ((0, frames, prev), (frames, 2 * frames, own)):
-        for slab, part in zip(slabs, outgoing("width", 2, source[:, :, last:], source[:, :, :width])):
-            slab[lo:hi, 0:rows, :] = part
-    for slab, part in zip(slabs, outgoing("width", 2, rim[:, :, last:], rim[:, :, :width])):
-        slab[:, rows:, :] = part
+        source = (prev if f < frames else own)[f % frames]
+        for slab, part in zip(slabs, outgoing("width", 2, source[:, last:], source[:, :width])):
+            slab[f * rows : (f + 1) * rows, :] = part
+    for slab, part in zip(slabs, outgoing("width", 2, rim[:, last:], rim[:, :width])):
+        slab[2 * frames * rows :, :] = part
 
 
 def arrange(c1, x, gain1, gain2, shortcut, conv1, conv2, down, xv, g1, g2, wsc, w1, w2m, w2r, wdm, wdr, sems):
@@ -130,6 +134,7 @@
         self.M1 = up((frames + 1) * self.R + rows + 3, 16)
         self.M2 = up((frames - 1) * self.R + rows + 1, 16)
         self.pitch = rows + 2
+        self.rim_rows = list(range(LOW)) + list(range(LOW + rows, LOW + rows + HIGH))
         self.w1, self.w2m, self.w2r, self.wsc = w1, w2m, w2r, wsc
         gap = jnp.zeros((1, LANES - c1), jnp.float32)
         self.gain1 = jnp.concatenate([g1[...], gap], axis=-1)
@@ -158,36 +163,38 @@
         slot, lane = target // LANES, target % LANES
         return jnp.where((source == slot * self.c1 + lane) & (lane < self.c1), 1.0, 0.0).astype(jnp.bfloat16)
 
-    def unpack(self, x, spread, lo, hi, first, raw, place, pieces):
-        count, tall = x.shape[0], x.shape[1]
-        wide = jnp.dot(
-            x.reshape(count * tall, EDGE * self.c1), spread, preferred_element_type=jnp.float32
-        )
+    def unpack(self, x, spread, lo, hi):
+        wide = jnp.dot(x, spread, preferred_element_type=jnp.float32)
         for k in range(lo, hi):
             v = wide[:, k * LANES : (k + 1) * LANES]
             ms = jnp.sum(v * v, axis=-1, keepdims=True) * (1.0 / self.c1)
             u = v * (0.5 * lax.rsqrt(ms + epsilon)) * self.gain1
-            u = u + u * jnp.tanh(u)
-            c = place + k - lo
-            for f in range(count):
-                at = f * self.R
-                for source, n, to in pieces:
-                    chunk = slice(f * tall + source, f * tall + source + n)
-                    first[c, at + to : at + to + n, :] = u[chunk]
-                    if f >= self.frames and to >= LOW:
-                        to += (f - self.frames) * self.R
-                        raw[c, to : to + n, :] = v[chunk]
-
-    def own_pieces(self):
-        return [(0, self.rows, LOW)]
-
-    def rim_pieces(self, start):
-        return [(start + 1 + HIGH - LOW, LOW, 0), (start + 1 + HIGH, HIGH, LOW + self.rows)]
-
-    def stack_first(self, c, first, stack):
+            yield v, u + u * jnp.tanh(u)
+
+    def place_own(self, c, v, u, first, raw):
+        for f in range(2 * self.frames):
+            chunk = slice(f * self.rows, (f + 1) * self.rows)
+            at = f * self.R + LOW
+            first[c, at : at + self.rows, :] = u[chunk]
+            if f >= self.frames:
+                at -= self.frames * self.R
+                raw[c, at : at + self.rows, :] = v[chunk]
+
+    def place_rim(self, c, u, first):
+        n = 2 * self.frames
+        for e, row in enumerate(self.rim_rows):
+            value = jnp.zeros((n, LANES), jnp.float32) if u is None else u[e * n : (e + 1) * n]
+            first[c, pl.ds(row, n, stride=self.R), :] = value
+
+    def place_raw(self, c, v, raw):
+        at = LOW * 2 * self.frames + self.frames
+        raw[c, pl.ds(LOW + self.rows, self.frames, stride=self.R), :] = v[at : at + self.frames]
+
+    def stack_first(self, c, first, stack, at=None):
+        at = c if at is None else at
         for k in range(9):
             off = (k // 3) * self.R + k % 3
-            stack[c, :, k * LANES : (k + 1) * LANES] = first[c, off : off + self.M1, :].astype(jnp.bfloat16)
+            stack[at, :, k * LANES : (k + 1) * LANES] = first[c, off : off + self.M1, :].astype(jnp.bfloat16)
 
     def conv_first(self, get, wanted):
         lhs = [jnp.concatenate([get(c + dc) for dc in range(3)], axis=-1) for c in wanted]
@@ -196,6 +203,24 @@
             self.w1[...].reshape(27 * LANES, self.c2),
             preferred_element_type=jnp.float32,
         )
+
+    def conv_rim(self, get, wanted):
+        n = 2 * self.frames
+        sums = {}
+        for dr in range(3):
+            lhs = [jnp.concatenate([get(c + dc, dr) for dc in range(3)], axis=-1) for c in wanted]
+            part = jnp.dot(
+                jnp.concatenate(lhs, axis=0),
+                self.w1[:, :, dr].reshape(9 * LANES, self.c2),
+                preferred_element_type=jnp.float32,
+            )
+            tall = part.shape[0] // len(wanted)
+            for block in range(3):
+                row = self.rim_rows[dr + block] - dr
+                for i in range(len(wanted)):
+                    value = part[i * tall + block * n : i * tall + (block + 1) * n]
+                    sums[i, row] = sums[i, row] + value if (i, row) in sums else value
+        return sums
 
     def act_second(self, hid, keep):
         ms = jnp.sum(hid * hid, axis=-1, keepdims=True) * (1.0 / self.c2)
@@ -264,38 +289,71 @@
             result(j, acc[i * count : (i + 1) * count])
 
 
-def early(dims, own, prev, g1, first, raw):
-    s = Steps(*dims, None, None, None, None, g1, None)
+def early(dims, own, prev, g1, w1, first, raw, acc_a, acc_b, stack1):
+    s = Steps(*dims, w1, None, None, None, g1, None)
     tail = 2 * s.frames * s.R
     first[:, tail:, :] = jnp.zeros((first.shape[0], first.shape[1] - tail, LANES), jnp.float32)
     spread = s.spread()
     for group in range(s.cols // EDGE):
         lanes = slice(group * EDGE * s.c1, (group + 1) * EDGE * s.c1)
         x = jnp.concatenate([prev[:, :, lanes], own[:, :, lanes]], axis=0)
-        s.unpack(x, spread, 0, EDGE, first, raw, group * EDGE, s.own_pieces())
+        x = x.reshape(2 * s.frames * s.rows, EDGE * s.c1)
+        for k, (v, u) in enumerate(s.unpack(x, spread, 0, EDGE)):
+            c = group * EDGE + k
+            s.place_own(c, v, u, first, raw)
+            s.place_rim(c, None, first)
+            s.stack_first(c, first, stack1)
+    hidden = list(range(LOW, s.cols))
+    step = 7
+    for start in range(0, len(hidden), step):
+        wanted = hidden[start : start + step]
+        acc = s.conv_first(lambda c: stack1[c - LOW], wanted)
+        for i, c in enumerate(wanted):
+            acc_a[c - LOW, 0 : s.M1, :] = acc[i * s.M1 : (i + 1) * s.M1, :LANES]
+            acc_b[c - LOW, 0 : s.M1, 0 : s.rest] = acc[i * s.M1 : (i + 1) * s.M1, LANES:]
 
 
 def inner(
-    dims, rim, w1, w2m, w2r, wsc, g1, g2, _first, _raw, first, raw, stack1, stack2, mer_a, mer_b, sec_a, sec_b
+    dims, rim, w1, w2m, w2r, wsc, g1, g2, _first, _raw, _acc_a, _acc_b,
+    first, raw, acc_a, acc_b, stack1, stack2, mer_a, mer_b, sec_a, sec_b, rims, stack_rim,
 ):
     s = Steps(*dims, w1, w2m, w2r, wsc, g1, g2)
     sec_b[...] = jnp.zeros_like(sec_b)
     mer_a[...] = jnp.zeros_like(mer_a)
     mer_b[...] = jnp.zeros_like(mer_b)
     spread = s.spread()
+    n = 2 * s.frames
+    tall = rim.shape[0]
+    rims[:, tall:, :] = jnp.zeros((s.cols, rims.shape[1] - tall, LANES), jnp.float32)
+    edge = [0, 1, s.cols - 2, s.cols - 1]
     for group in range(s.cols // EDGE):
-        x = rim[:, :, group * EDGE * s.c1 : (group + 1) * EDGE * s.c1]
-        s.unpack(x, spread, 0, EDGE, first, raw, group * EDGE, s.rim_pieces(0))
-    for c in range(s.cols):
-        s.stack_first(c, first, stack1)
+        x = rim[:, group * EDGE * s.c1 : (group + 1) * EDGE * s.c1]
+        for k, (v, u) in enumerate(s.unpack(x, spread, 0, EDGE)):
+            c = group * EDGE + k
+            rims[c, 0:tall, :] = u
+            s.place_raw(c, v, raw)
+            for dr in range(3):
+                for dt in range(3):
+                    off = dr * n + dt
+                    part = rims[c, off : off + stack_rim.shape[2], :]
+                    stack_rim[c, dr, :, dt * LANES : (dt + 1) * LANES] = part.astype(jnp.bfloat16)
+            if c in edge:
+                s.place_rim(c, u, first)
     hidden = list(range(LOW, s.cols))
     step = 7
     for start in range(0, len(hidden), step):
         wanted = hidden[start : start + step]
-        acc = s.conv_first(lambda c: stack1[c - LOW], wanted)
-        for i, c in enumerate(wanted):
-            s.halves(c - LOW, s.act_second(acc[i * s.M1 : (i + 1) * s.M1], None), sec_a, sec_b)
+        gap = jnp.zeros((n, LANES - s.rest), jnp.float32)
+        for (i, row), value in s.conv_rim(lambda c, dr: stack_rim[c - LOW, dr], wanted).items():
+            c = wanted[i] - LOW
+            acc_a[c, pl.ds(row, n, stride=s.R), :] += value[:, :LANES]
+            acc_b[c, pl.ds(row, n, stride=s.R), :] += jnp.concatenate([value[:, LANES:], gap], axis=-1)
+        for c in wanted:
+            hid = jnp.concatenate([acc_a[c - LOW, 0 : s.M1, :], acc_b[c - LOW, 0 : s.M1, : s.rest]], axis=-1)
+            s.halves(c - LOW, s.act_second(hid, None), sec_a, sec_b)
             s.stack_second(c - LOW, sec_a, sec_b, stack2)
+    for i, c in enumerate(edge):
+        s.stack_first(c, first, stack1, i)
     merged = list(range(LOW, s.cols - 2))
     step = 6
     for start in range(0, len(merged), step):
@@ -320,11 +378,13 @@
     first[:, tail:, :] = jnp.zeros((first.shape[0], first.shape[1] - tail, LANES), jnp.float32)
     spread = s.spread()
     left, right = incoming("width", [got_a[...], got_b[...]])
-    pieces = s.own_pieces() + s.rim_pieces(s.rows)
-    s.unpack(left, spread, EDGE - LOW, EDGE, first, raw, 0, pieces)
-    s.unpack(right, spread, 0, HIGH, first, raw, LOW, pieces)
-    for c in range(LOW + HIGH):
-        s.stack_first(c, first, stack1)
+    for x, lo, hi, at in ((left, EDGE - LOW, EDGE, 0), (right, 0, HIGH, LOW)):
+        for k, (v, u) in enumerate(s.unpack(x, spread, lo, hi)):
+            own_rows = 2 * s.frames * s.rows
+            s.place_own(at + k, v[:own_rows], u[:own_rows], first, raw)
+            s.place_rim(at + k, u[own_rows:], first)
+            s.place_raw(at + k, v[own_rows:], raw)
+            s.stack_first(at + k, first, stack1)
 
     def new_or(own, given, lo, hi):
         return lambda c: given(c - lo) if lo <= c < hi else own(c if c < lo else c - hi + lo)
@@ -338,7 +398,7 @@
     lows = new_or(lambda i: (mer_a, i), lambda i: (in_mer_a, i), LOW, cols - 2)
     highs = new_or(lambda i: (mer_b, i), lambda i: (in_mer_b, i), LOW, cols - 2)
     out_cols = cols // 2
-    get1 = new_or(lambda i: stack1[i], lambda i: in_stack1[i], LOW, LOW + cols)
+    get1 = new_or(lambda i: stack1[i], lambda i: in_stack1[i if i < 2 else i - cols + 4], LOW, LOW + cols)
     get2 = new_or(lambda i: stack2[i], lambda i: in_stack2[i], LOW, cols)
     get_raw = new_or(
         lambda i: raw[i, LOW : LOW + M2, :], lambda i: in_raw[i, LOW : LOW + M2, :], LOW, LOW + cols
@@ -384,6 +444,7 @@
     M1 = up((frames + 1) * R + rows + 3, 16)
     M2 = up((frames - 1) * R + rows + 1, 16)
     first_rows = up(M1 + 2 * R + 2, 8)
+    acc_rows = up(2 * frames * R, 8)
     raw_rows = up(M2 + LOW, 8)
     count = up((frames - 1) * (rows + 2) // 2 + rows // 2, 8)
     held = up(2 * count + 1, 8)
@@ -411,7 +472,8 @@
         name="arrange",
     )(*[pltpu.with_memory_space_constraint(a, pltpu.HBM) for a in [video_in] + source])
 
-    tall = 2 * rows
+    rim_tall = up((LOW + HIGH) * 2 * frames, 16)
+    tall = 2 * frames * rows + rim_tall
     got = swap("tm", [video_in] * rounds("tm"))
     *slabs, prev = pl.pallas_call(
         rows_out,
@@ -425,53 +487,57 @@
         name="rows_out",
     )(own, *got)
     got = swap("height", slabs)
-    first, raw = pl.pallas_call(
+    hid_in, mer_in = cols - 2, cols - 4
+    worked = [
+        pltpu.VMEM((cols, first_rows, LANES), f32),
+        pltpu.VMEM((cols, raw_rows, LANES), f32),
+        pltpu.VMEM((hid_in, acc_rows, LANES), f32),
+        pltpu.VMEM((hid_in, acc_rows, LANES), f32),
+    ]
+    work = pl.pallas_call(
         functools.partial(early, dims),
-        out_shape=[
-            pltpu.VMEM((cols, first_rows, LANES), f32),
-            pltpu.VMEM((cols, raw_rows, LANES), f32),
-        ],
-        in_specs=[vmem] * 3,
-        out_specs=[vmem] * 2,
-        compiler_params=small,
+        out_shape=worked,
+        in_specs=[vmem] * 4,
+        out_specs=[vmem] * 4,
+        scratch_shapes=[pltpu.VMEM((cols, M1, 9 * LANES), bf)],
+        compiler_params=params,
         cost_estimate=cost(10**9),
         name="early",
-    )(own, prev, g1)
+    )(own, prev, g1, w1)
     rim, *slabs = pl.pallas_call(
         functools.partial(cols_out, EDGE * c1),
-        out_shape=[pltpu.VMEM((2 * frames, 2 + 2 * HIGH, merged_cols), bf)]
-        + [pltpu.VMEM((2 * frames, tall, EDGE * c1), bf)] * 2,
+        out_shape=[pltpu.VMEM((rim_tall, merged_cols), bf)] + [pltpu.VMEM((tall, EDGE * c1), bf)] * 2,
         in_specs=[vmem] * (2 + len(got)),
         out_specs=[vmem] * 3,
-        scratch_shapes=[pltpu.VMEM((2 * frames, 2 + 2 * HIGH, merged_cols), f32)],
+        scratch_shapes=[pltpu.VMEM((merged_cols // LANES, 2 * frames * HIGH, LANES), f32)] * 2,
         compiler_params=small,
         cost_estimate=cost(0),
         name="cols_out",
     )(own, prev, *got)
     got_a, got_b = swap("width", slabs)
 
-    hid_in, mer_in = cols - 2, cols - 4
-    _, *passed = pl.pallas_call(
+    _, raw, _, _, *passed = pl.pallas_call(
         functools.partial(inner, dims),
-        out_shape=[
-            pltpu.VMEM((cols, first_rows, LANES), f32),
-            pltpu.VMEM((cols, raw_rows, LANES), f32),
-            pltpu.VMEM((cols, M1, 9 * LANES), bf),
+        out_shape=worked
+        + [
+            pltpu.VMEM((4, M1, 9 * LANES), bf),
             pltpu.VMEM((hid_in, M2, 15 * LANES), bf),
             pltpu.VMEM((mer_in, held, LANES), f32),
             pltpu.VMEM((mer_in, held, LANES), f32),
         ],
-        in_specs=[vmem] * 9,
-        out_specs=[vmem] * 6,
+        in_specs=[vmem] * 11,
+        out_specs=[vmem] * 8,
         scratch_shapes=[
             pltpu.VMEM((hid_in, M1, LANES), f32),
             pltpu.VMEM((hid_in, M1, LANES), f32),
+            pltpu.VMEM((cols, rim_tall + 8, LANES), f32),
+            pltpu.VMEM((cols, 3, 32, 3 * LANES), bf),
         ],
-        input_output_aliases={7: 0, 8: 1},
+        input_output_aliases={7: 0, 8: 1, 9: 2, 10: 3},
         compiler_params=params,
         cost_estimate=cost(4 * 10**9),
         name="inner",
-    )(rim, w1, w2m, w2r, wsc, g1, g2, first, raw)
+    )(rim, w1, w2m, w2r, wsc, g1, g2, *work)
     edge = LOW + HIGH
     return pl.pallas_call(
         functools.partial(outer, dims),
@@ -492,7 +558,7 @@
         compiler_params=params,
         cost_estimate=cost(2 * 10**9),
         name="outer",
-    )(got_a, got_b, w1, w2m, w2r, wsc, g1, g2, wdm, wdr, *passed)
+    )(got_a, got_b, w1, w2m, w2r, wsc, g1, g2, wdm, wdr, raw, *passed)
 
 
 def solution(mesh):

time: 23 us -> 21.9 us (0.952)
  waiting for transfers between devices: 2.5 us -> 0.22 us
  Pallas kernels: 12.4 us -> 13.6 us
    ppermute x5, waiting for transfers between devices: 2.5 us -> 0.22 us  [swap(): lax.ppermute(value, AXES, swap_pairs(axis, i))]
    pallas_call x2, Pallas kernels: 5.88 us -> 7.05 us  [the longest x1 4.13 us: local(): pl.pallas_call(functools.partial(inner, dims), out_shape=worked + [pltpu....]
  transfers between devices with their start and end apart: 5 -> 5, of which waited for: 2 -> 1; matrix products, arithmetic and copies ran while one was open for 0% -> 0% of each run, Pallas kernels for 37% -> 44%
where the time goes in v4:
time: 21.9 us; the launch traced here: 21.8 us
  Pallas kernels  13.6 us (62%)
  starting transfers between devices  7.87 us (36%)
  waiting for transfers between devices  0.22 us (1%)
    ppermute x5, starting transfers between devices, swap(): lax.ppermute(value, AXES, swap_pairs(axis, i))  7.87 us
    pallas_call x1, Pallas kernels, local(): pl.pallas_call(functools.partial(inner, dims), out_shape=worked + [pltpu....  4.13 us
    pallas_call x1, Pallas kernels, local(): pl.pallas_call(functools.partial(outer, dims), out_shape=jax.ShapeDtypeSt...  3.81 us
    pallas_call x1, Pallas kernels, local(): pl.pallas_call(functools.partial(early, dims), out_shape=worked, in_specs...  2.92 us
    pallas_call x1, Pallas kernels, local(): pl.pallas_call(functools.partial(arrange, c1), out_shape=[pltpu.VMEM(vide...  2.61 us
  transfers between devices with their start and end apart: 5, of which 1 were waited for; matrix products, arithmetic and copies ran while one was open for 0% of the time, Pallas kernels for 44%

profile of v4, /device:TPU:0, one launch (start us, length us, event | category | flops | bytes accessed | tf_op | source)
XLA Modules:
  0.0 21.8 jit_solution(11380686688696634335)
XLA Ops:
  0.0 0.5 %collective-permute-start.1 = (bf16[4,8,1536]{2,1,0:T(8,128)(2,1)}, bf16[4,8,1536]{2,1,0:T(8,128)(2,1)S(1)}, u32[]{:S(2)}, u32[]{:S(2)}) collective-permute-start(bf16[4,8,1536]{2,1,0:T(8,128)(2,1)} %x.1), channel_id=1, source_target_pairs={{0,1},{1,0},{2,3},{3,2},{4,5},{5,4},{6,7},{7,6},{8,16},{9,17},{10,... | collective-permute-start | bytes 294920 | tf_op jit(solution)/shard_map/ppermute | solution.py:40
  0.5 4.1 %collective-permute-start = (bf16[4,8,1536]{2,1,0:T(8,128)(2,1)}, bf16[4,8,1536]{2,1,0:T(8,128)(2,1)S(1)}, u32[]{:S(2)}, u32[]{:S(2)}) collective-permute-start(bf16[4,8,1536]{2,1,0:T(8,128)(2,1)} %x.1), channel_id=1, source_target_pairs={{0,8},{1,9},{2,10},{3,11},{4,12},{5,13},{6,14},{7,15},{8,0},{9,1},... | collective-permute-start | bytes 294920 | tf_op jit(solution)/shard_map/ppermute | solution.py:40
  4.6 2.6 %arrange.1 = (bf16[4,8,1536]{2,1,0:T(8,128)(2,1)S(1)}, f32[1,96]{1,0:T(1,128)S(1)}, f32[1,192]{1,0:T(1,128)S(1)}, bf16[128,192]{1,0:T(8,128)(2,1)S(1)}, bf16[3,3...) custom-call(bf16[4,8,1536]{2,1,0:T(8,128)(2,1)} %x.1, ...), custom_call_target="tpu_custom_call" | custom-call | bytes 5000000 | tf_op jit(solution)/shard_map/arrange/pallas_call | solution.py:454
  7.2 0.0 collective-permute-done.1.refs_1_
  7.2 0.2 collective-permute-done.refs_0_
  7.4 0.1 rows_out.1
  7.5 1.6 %collective-permute-start.2 = (bf16[24,1536]{1,0:T(8,128)(2,1)S(1)}, bf16[24,1536]{1,0:T(8,128)(2,1)S(1)}, u32[]{:S(2)}, u32[]{:S(2)}) collective-permute-start(bf16[24,1536]{1,0:T(8,128)(2,1)S(1)} %get-tuple-element.30), channel_id=1, source_target_pairs={{0,4},{1,5},{2,6},{3,7},{4,0},{5,1},{6,2},{7,3},{8,12},{9,13},{10,... | collective-permute-start | bytes 221192 | tf_op jit(solution)/shard_map/ppermute | solution.py:40
  9.1 2.9 %early.1 = (f32[16,112,128]{2,1,0:T(8,128)S(1)}, f32[16,56,128]{2,1,0:T(8,128)S(1)}, f32[14,104,128]{2,1,0:T(8,128)S(1)}, f32[14,104,128]{2,1,0:T(8,128)S(1)}) custom-call(bf16[4,8,1536]{2,1,0:T(8,128)(2,1)S(1)} %get-tuple-element.28.own, bf16[4,8,1536]{2,1,0:T(8,128)(2,1)S(1)} %get-tuple-element.29.prev, f32[1,96]{1,0:T(1,128)S(1)} %get-tuple-element.37.g1, ...), custom_call_target="tpu_custom_call" | custom-call | flops 1000000000 | bytes 5000000 | tf_op jit(solution)/shard_map/early/pallas_call | solution.py:497
  12.0 0.0 collective-permute-done.2.refs_0_
  12.0 0.1 cols_out.1
  12.1 0.1 collective-permute-start.3
  12.2 1.6 %collective-permute-start.4 = (bf16[112,384]{1,0:T(8,128)(2,1)S(1)}, bf16[112,384]{1,0:T(8,128)(2,1)S(1)}, u32[]{:S(2)}, u32[]{:S(2)}) collective-permute-start(bf16[112,384]{1,0:T(8,128)(2,1)S(1)} %get-tuple-element.32), channel_id=1, source_target_pairs={{0,3},{1,2},{2,1},{3,0},{4,7},{5,6},{6,5},{7,4},{8,11},{9,10},{10,... | collective-permute-start | bytes 258056 | tf_op jit(solution)/shard_map/ppermute | solution.py:40
  13.8 4.1 %inner.1 = (f32[16,112,128]{2,1,0:T(8,128)S(1)}, f32[16,56,128]{2,1,0:T(8,128)S(1)}, f32[14,104,128]{2,1,0:T(8,128)S(1)}, f32[14,104,128]{2,1,0:T(8,128)S(1)}, b...) custom-call(bf16[48,1536]{1,0:T(8,128)(2,1)S(1)} %get-tuple-element., ...), custom_call_target="tpu_custom_call", output_to_operand_aliasing={{0}: (7, {}), {1}: (8, {}), {2}: (9, {}), {3}: (10, {})} | custom-call | flops 4000000000 | bytes 5000000 | tf_op jit(solution)/shard_map/inner/pallas_call | solution.py:519
  18.0 0.0 collective-permute-done.3.got_a
  18.0 0.0 collective-permute-done.4.got_b
  18.0 3.8 %outer.1 = bf16[4,4,1536]{2,1,0:T(4,128)(2,1)} custom-call(bf16[112,384]{1,0:T(8,128)(2,1)S(1)} %collective-permute-done.3.got_a, bf16[112,384]{1,0:T(8,128)(2,1)S(1)} %collective-permute-done.4.got_b, bf16[3,3,3,128,192]{4,3,2,1,0:T(8,128)(2,1)S(1)} %get-tuple-element.33.w1, bf16[3,3,3,128,192]{4,3,2,1,0:T(8,128)(2,1)S(1)} %get-tuple-element.34.w2m, ...), custom_call_target="tpu_custom_call" | custom-call | flops 2000000000 | bytes 5000000 | tf_op jit(solution)/shard_map/outer/pallas_call | solution.py:542
Async XLA Ops:
  0.0 7.2 %collective-permute-start.1 = (bf16[4,8,1536]{2,1,0:T(8,128)(2,1)}, bf16[4,8,1536]{2,1,0:T(8,128)(2,1)S(1)}, u32[]{:S(2)}, u32[]{:S(2)}) collective-permute-start(bf16[4,8,1536]{2,1,0:T(8,128)(2,1)} %x.1), channel_id=1, source_target_pairs={{0,1},{1,0},{2,3},{3,2},{4,5},{5,4},{6,7},{7,6},{8,16},{9,17},{10,... | collective-permute-start | bytes 294920 | tf_op jit(solution)/shard_map/ppermute | solution.py:40
  0.5 7.0 %collective-permute-start = (bf16[4,8,1536]{2,1,0:T(8,128)(2,1)}, bf16[4,8,1536]{2,1,0:T(8,128)(2,1)S(1)}, u32[]{:S(2)}, u32[]{:S(2)}) collective-permute-start(bf16[4,8,1536]{2,1,0:T(8,128)(2,1)} %x.1), channel_id=1, source_target_pairs={{0,8},{1,9},{2,10},{3,11},{4,12},{5,13},{6,14},{7,15},{8,0},{9,1},... | collective-permute-start | bytes 294920 | tf_op jit(solution)/shard_map/ppermute | solution.py:40
  7.5 4.5 %collective-permute-start.2 = (bf16[24,1536]{1,0:T(8,128)(2,1)S(1)}, bf16[24,1536]{1,0:T(8,128)(2,1)S(1)}, u32[]{:S(2)}, u32[]{:S(2)}) collective-permute-start(bf16[24,1536]{1,0:T(8,128)(2,1)S(1)} %get-tuple-element.30), channel_id=1, source_target_pairs={{0,4},{1,5},{2,6},{3,7},{4,0},{5,1},{6,2},{7,3},{8,12},{9,13},{10,... | collective-permute-start | bytes 221192 | tf_op jit(solution)/shard_map/ppermute | solution.py:40
  12.1 5.9 %collective-permute-start.3 = (bf16[112,384]{1,0:T(8,128)(2,1)S(1)}, bf16[112,384]{1,0:T(8,128)(2,1)S(1)}, u32[]{:S(2)}, u32[]{:S(2)}) collective-permute-start(bf16[112,384]{1,0:T(8,128)(2,1)S(1)} %get-tuple-element.31), channel_id=1, source_target_pairs={{0,1},{1,0},{2,3},{3,2},{4,5},{5,4},{6,7},{7,6},{8,9},{9,8},{10,11... | collective-permute-start | bytes 258056 | tf_op jit(solution)/shard_map/ppermute | solution.py:40
  12.2 5.8 %collective-permute-start.4 = (bf16[112,384]{1,0:T(8,128)(2,1)S(1)}, bf16[112,384]{1,0:T(8,128)(2,1)S(1)}, u32[]{:S(2)}, u32[]{:S(2)}) collective-permute-start(bf16[112,384]{1,0:T(8,128)(2,1)S(1)} %get-tuple-element.32), channel_id=1, source_target_pairs={{0,3},{1,2},{2,1},{3,0},{4,7},{5,6},{6,5},{7,4},{8,11},{9,10},{10,... | collective-permute-start | bytes 258056 | tf_op jit(solution)/shard_map/ppermute | solution.py:40

commit v5 on v4

--- a/solution.py
+++ b/solution.py
@@ -64,7 +64,7 @@
 
 def rows_out(own, *refs):
     got, slabs, prev, wide = refs[: rounds("tm")], refs[rounds("tm") : -2], refs[-2], refs[-1]
-    prev[...] = incoming("tm", [ref[...] for ref in got])[0]
+    prev[...] = incoming("tm", [ref[...] for ref in got[::-1]])[0]
     frames, rows = own.shape[0], own.shape[1]
     for i, slab in enumerate(slabs):
         for f in range(2 * frames):
@@ -407,14 +407,14 @@
         ([0, 1], [s.keep_left, None], [0, 1], [None, None], 0),
         ([cols, cols + 1, cols + 2], [None] + [s.keep_right] * 2, [cols - 2, cols - 1, cols], [None, None, s.keep_right], 2),
     ]
-    for wanted, keeps, _, _, at in sides:
-        acc = s.conv_first(get1, wanted)
+    s.down(lows, highs, list(range(1, out_cols - 2)), stack3, wdm, wdr, store)
+    accs = [s.conv_first(get1, side[0]) for side in sides]
+    for acc, (wanted, keeps, _, _, at) in zip(accs, sides):
         for i, keep in enumerate(keeps):
             s.halves(at + i, s.act_second(acc[i * M1 : (i + 1) * M1], keep), sec_a, sec_b)
             s.stack_second(at + i, sec_a, sec_b, stack2)
-    s.down(lows, highs, list(range(1, out_cols - 2)), stack3, wdm, wdr, store)
-    for _, _, wanted, keeps, at in sides:
-        acc = s.conv_second(get2, get_raw, wanted)
+    accs = [s.conv_second(get2, get_raw, side[2]) for side in sides]
+    for acc, (_, _, wanted, keeps, at) in zip(accs, sides):
         for i, keep in enumerate(keeps):
             s.merged(at + i, acc[i * M2 : (i + 1) * M2], keep, mer_a, mer_b)
     s.down(lows, highs, [0, out_cols - 2, out_cols - 1], stack3, wdm, wdr, store)
@@ -485,7 +485,7 @@
         compiler_params=small,
         cost_estimate=cost(0),
         name="rows_out",
-    )(own, *got)
+    )(own, *got[::-1])
     got = swap("height", slabs)
     hid_in, mer_in = cols - 2, cols - 4
     worked = [

time: 21.9 us -> 21 us (0.959)
  the two profiles are of different devices: /device:TPU:0 before, /device:TPU:17 now
where the time goes in v5:
time: 21 us; the launch traced here: 20.9 us
  Pallas kernels  13.5 us (64%)
  starting transfers between devices  6.09 us (29%)
  waiting for transfers between devices  1.19 us (6%)
    ppermute x5, starting transfers between devices, swap(): lax.ppermute(value, AXES, swap_pairs(axis, i))  6.09 us
    pallas_call x1, Pallas kernels, local(): pl.pallas_call(functools.partial(inner, dims), out_shape=worked + [pltpu....  4.12 us
    pallas_call x1, Pallas kernels, local(): pl.pallas_call(functools.partial(outer, dims), out_shape=jax.ShapeDtypeSt...  3.7 us
    pallas_call x1, Pallas kernels, local(): pl.pallas_call(functools.partial(early, dims), out_shape=worked, in_specs...  2.92 us
    pallas_call x1, Pallas kernels, local(): pl.pallas_call(functools.partial(arrange, c1), out_shape=[pltpu.VMEM(vide...  2.61 us
    ppermute x5, waiting for transfers between devices, swap(): lax.ppermute(value, AXES, swap_pairs(axis, i))  1.19 us
  transfers between devices with their start and end apart: 5, of which 1 were waited for; matrix products, arithmetic and copies ran while one was open for 0% of the time, Pallas kernels for 46%

profile of v5, /device:TPU:17, one launch (start us, length us, event | category | flops | bytes accessed | tf_op | source)
XLA Modules:
  0.0 20.9 jit_solution(4951141862410733517)
XLA Ops:
  0.0 1.3 %collective-permute-start.1 = (bf16[4,8,1536]{2,1,0:T(8,128)(2,1)}, bf16[4,8,1536]{2,1,0:T(8,128)(2,1)S(1)}, u32[]{:S(2)}, u32[]{:S(2)}) collective-permute-start(bf16[4,8,1536]{2,1,0:T(8,128)(2,1)} %x.1), channel_id=1, source_target_pairs={{0,8},{1,9},{2,10},{3,11},{4,12},{5,13},{6,14},{7,15},{8,0},{9,1},... | collective-permute-start | bytes 294920 | tf_op jit(solution)/shard_map/ppermute | solution.py:40
  1.3 0.0 collective-permute-start
  1.3 2.6 %arrange.1 = (bf16[4,8,1536]{2,1,0:T(8,128)(2,1)S(1)}, f32[1,96]{1,0:T(1,128)S(1)}, f32[1,192]{1,0:T(1,128)S(1)}, bf16[128,192]{1,0:T(8,128)(2,1)S(1)}, bf16[3,3...) custom-call(bf16[4,8,1536]{2,1,0:T(8,128)(2,1)} %x.1, ...), custom_call_target="tpu_custom_call" | custom-call | bytes 5000000 | tf_op jit(solution)/shard_map/arrange/pallas_call | solution.py:454
  3.9 0.0 collective-permute-done.1.refs_1_
  3.9 1.2 %collective-permute-done.refs_0_ = bf16[4,8,1536]{2,1,0:T(8,128)(2,1)S(1)} collective-permute-done((bf16[4,8,1536]{2,1,0:T(8,128)(2,1)}, bf16[4,8,1536]{2,1,0:T(8,128)(2,1)S(1)}, u32[]{:S(2)}, u32[]{:S(2)}) %collective-permute-start) | collective-permute-done | bytes 98336 | tf_op jit(solution)/shard_map/ppermute | solution.py:40
  5.1 0.1 rows_out.1
  5.2 1.3 %collective-permute-start.2 = (bf16[24,1536]{1,0:T(8,128)(2,1)S(1)}, bf16[24,1536]{1,0:T(8,128)(2,1)S(1)}, u32[]{:S(2)}, u32[]{:S(2)}) collective-permute-start(bf16[24,1536]{1,0:T(8,128)(2,1)S(1)} %get-tuple-element.30), channel_id=1, source_target_pairs={{0,4},{1,5},{2,6},{3,7},{4,0},{5,1},{6,2},{7,3},{8,12},{9,13},{10,... | collective-permute-start | bytes 221192 | tf_op jit(solution)/shard_map/ppermute | solution.py:40
  6.5 2.9 %early.1 = (f32[16,112,128]{2,1,0:T(8,128)S(1)}, f32[16,56,128]{2,1,0:T(8,128)S(1)}, f32[14,104,128]{2,1,0:T(8,128)S(1)}, f32[14,104,128]{2,1,0:T(8,128)S(1)}) custom-call(bf16[4,8,1536]{2,1,0:T(8,128)(2,1)S(1)} %get-tuple-element.28.own, bf16[4,8,1536]{2,1,0:T(8,128)(2,1)S(1)} %get-tuple-element.29.prev, f32[1,96]{1,0:T(1,128)S(1)} %get-tuple-element.37.g1, ...), custom_call_target="tpu_custom_call" | custom-call | flops 1000000000 | bytes 5000000 | tf_op jit(solution)/shard_map/early/pallas_call | solution.py:497
  9.4 0.0 collective-permute-done.2.refs_0_
  9.4 0.1 cols_out.1
  9.5 2.3 %collective-permute-start.3 = (bf16[112,384]{1,0:T(8,128)(2,1)S(1)}, bf16[112,384]{1,0:T(8,128)(2,1)S(1)}, u32[]{:S(2)}, u32[]{:S(2)}) collective-permute-start(bf16[112,384]{1,0:T(8,128)(2,1)S(1)} %get-tuple-element.31), channel_id=1, source_target_pairs={{0,1},{1,0},{2,3},{3,2},{4,5},{5,4},{6,7},{7,6},{8,9},{9,8},{10,11... | collective-permute-start | bytes 258056 | tf_op jit(solution)/shard_map/ppermute | solution.py:40
  11.8 1.2 %collective-permute-start.4 = (bf16[112,384]{1,0:T(8,128)(2,1)S(1)}, bf16[112,384]{1,0:T(8,128)(2,1)S(1)}, u32[]{:S(2)}, u32[]{:S(2)}) collective-permute-start(bf16[112,384]{1,0:T(8,128)(2,1)S(1)} %get-tuple-element.32), channel_id=1, source_target_pairs={{0,3},{1,2},{2,1},{3,0},{4,7},{5,6},{6,5},{7,4},{8,11},{9,10},{10,... | collective-permute-start | bytes 258056 | tf_op jit(solution)/shard_map/ppermute | solution.py:40
  13.0 4.1 %inner.1 = (f32[16,112,128]{2,1,0:T(8,128)S(1)}, f32[16,56,128]{2,1,0:T(8,128)S(1)}, f32[14,104,128]{2,1,0:T(8,128)S(1)}, f32[14,104,128]{2,1,0:T(8,128)S(1)}, b...) custom-call(bf16[48,1536]{1,0:T(8,128)(2,1)S(1)} %get-tuple-element., ...), custom_call_target="tpu_custom_call", output_to_operand_aliasing={{0}: (7, {}), {1}: (8, {}), {2}: (9, {}), {3}: (10, {})} | custom-call | flops 4000000000 | bytes 5000000 | tf_op jit(solution)/shard_map/inner/pallas_call | solution.py:519
  17.1 0.0 collective-permute-done.3.got_a
  17.1 0.0 collective-permute-done.4.got_b
  17.2 3.7 %outer.1 = bf16[4,4,1536]{2,1,0:T(4,128)(2,1)} custom-call(bf16[112,384]{1,0:T(8,128)(2,1)S(1)} %collective-permute-done.3.got_a, bf16[112,384]{1,0:T(8,128)(2,1)S(1)} %collective-permute-done.4.got_b, bf16[3,3,3,128,192]{4,3,2,1,0:T(8,128)(2,1)S(1)} %get-tuple-element.33.w1, bf16[3,3,3,128,192]{4,3,2,1,0:T(8,128)(2,1)S(1)} %get-tuple-element.34.w2m, ...), custom_call_target="tpu_custom_call" | custom-call | flops 2000000000 | bytes 5000000 | tf_op jit(solution)/shard_map/outer/pallas_call | solution.py:542
Async XLA Ops:
  0.0 3.9 %collective-permute-start.1 = (bf16[4,8,1536]{2,1,0:T(8,128)(2,1)}, bf16[4,8,1536]{2,1,0:T(8,128)(2,1)S(1)}, u32[]{:S(2)}, u32[]{:S(2)}) collective-permute-start(bf16[4,8,1536]{2,1,0:T(8,128)(2,1)} %x.1), channel_id=1, source_target_pairs={{0,8},{1,9},{2,10},{3,11},{4,12},{5,13},{6,14},{7,15},{8,0},{9,1},... | collective-permute-start | bytes 294920 | tf_op jit(solution)/shard_map/ppermute | solution.py:40
  1.3 3.8 %collective-permute-start = (bf16[4,8,1536]{2,1,0:T(8,128)(2,1)}, bf16[4,8,1536]{2,1,0:T(8,128)(2,1)S(1)}, u32[]{:S(2)}, u32[]{:S(2)}) collective-permute-start(bf16[4,8,1536]{2,1,0:T(8,128)(2,1)} %x.1), channel_id=1, source_target_pairs={{0,1},{1,0},{2,3},{3,2},{4,5},{5,4},{6,7},{7,6},{8,16},{9,17},{10,... | collective-permute-start | bytes 294920 | tf_op jit(solution)/shard_map/ppermute | solution.py:40
  5.2 4.2 %collective-permute-start.2 = (bf16[24,1536]{1,0:T(8,128)(2,1)S(1)}, bf16[24,1536]{1,0:T(8,128)(2,1)S(1)}, u32[]{:S(2)}, u32[]{:S(2)}) collective-permute-start(bf16[24,1536]{1,0:T(8,128)(2,1)S(1)} %get-tuple-element.30), channel_id=1, source_target_pairs={{0,4},{1,5},{2,6},{3,7},{4,0},{5,1},{6,2},{7,3},{8,12},{9,13},{10,... | collective-permute-start | bytes 221192 | tf_op jit(solution)/shard_map/ppermute | solution.py:40
  9.5 7.7 %collective-permute-start.3 = (bf16[112,384]{1,0:T(8,128)(2,1)S(1)}, bf16[112,384]{1,0:T(8,128)(2,1)S(1)}, u32[]{:S(2)}, u32[]{:S(2)}) collective-permute-start(bf16[112,384]{1,0:T(8,128)(2,1)S(1)} %get-tuple-element.31), channel_id=1, source_target_pairs={{0,1},{1,0},{2,3},{3,2},{4,5},{5,4},{6,7},{7,6},{8,9},{9,8},{10,11... | collective-permute-start | bytes 258056 | tf_op jit(solution)/shard_map/ppermute | solution.py:40
  11.8 5.3 %collective-permute-start.4 = (bf16[112,384]{1,0:T(8,128)(2,1)S(1)}, bf16[112,384]{1,0:T(8,128)(2,1)S(1)}, u32[]{:S(2)}, u32[]{:S(2)}) collective-permute-start(bf16[112,384]{1,0:T(8,128)(2,1)S(1)} %get-tuple-element.32), channel_id=1, source_target_pairs={{0,3},{1,2},{2,1},{3,0},{4,7},{5,6},{6,5},{7,4},{8,11},{9,10},{10,... | collective-permute-start | bytes 258056 | tf_op jit(solution)/shard_map/ppermute | solution.py:40

commit v6 on v5

--- a/solution.py
+++ b/solution.py
@@ -13,7 +13,19 @@
 EDGE = 4
 
 
-def swap_pairs(axis, parity):
+def rounds(axis):
+    if lax.axis_size(axis) == 2:
+        return 1
+    return 3 if axis == "tm" else 2
+
+
+def round_of(axis, low):
+    if axis == "tm":
+        return jnp.where(low % 2 == 1, 1, low % 4) if isinstance(low, jax.Array) else (1 if low % 2 else low % 4)
+    return low % 2
+
+
+def swap_pairs(axis, turn):
     sizes = [lax.axis_size(name) for name in AXES]
     place = AXES.index(axis)
     count = sizes[place]
@@ -23,11 +35,13 @@
             for w in range(sizes[2]):
                 source = [t, h, w]
                 target = [t, h, w]
-                other = source[place] + (1 if source[place] % 2 == parity else -1)
-                if 0 <= other < count:
-                    target[place] = other
+                mine = source[place]
+                if mine + 1 < count and round_of(axis, mine) == turn:
+                    target[place] = mine + 1
+                elif mine > 0 and round_of(axis, mine - 1) == turn:
+                    target[place] = mine - 1
                 elif axis == "width":
-                    target[place] = other % count
+                    target[place] = count - 1 - mine
                 else:
                     target[2] = w ^ 1
                 pairs.append(
@@ -38,10 +52,6 @@
 
 def swap(axis, outgoing):
     return [lax.ppermute(value, AXES, swap_pairs(axis, i)) for i, value in enumerate(outgoing)]
-
-
-def rounds(axis):
-    return 1 if lax.axis_size(axis) == 2 else 2
 
 
 def outgoing(axis, count, to_next, to_prev):
@@ -64,7 +74,14 @@
 
 def rows_out(own, *refs):
     got, slabs, prev, wide = refs[: rounds("tm")], refs[rounds("tm") : -2], refs[-2], refs[-1]
-    prev[...] = incoming("tm", [ref[...] for ref in got[::-1]])[0]
+    index = lax.axis_index("tm")
+    prev[...] = jnp.zeros(prev.shape, prev.dtype)
+    for i, ref in zip([0, 2, 1] if len(got) == 3 else range(len(got)), got):
+
+        @pl.when((index > 0) & (round_of("tm", index - 1) == i))
+        def _(ref=ref):
+            prev[...] = ref[...]
+
     frames, rows = own.shape[0], own.shape[1]
     for i, slab in enumerate(slabs):
         for f in range(2 * frames):
@@ -366,7 +383,7 @@
 
 
 def outer(
-    dims, got_a, got_b, w1, w2m, w2r, wsc, g1, g2, wdm, wdr, in_raw, in_stack1, in_stack2, in_mer_a, in_mer_b,
+    dims, got_b, got_a, w1, w2m, w2r, wsc, g1, g2, wdm, wdr, in_raw, in_stack1, in_stack2, in_mer_a, in_mer_b,
     out, first, raw, stack1, sec_a, sec_b, stack2, mer_a, mer_b, stack3,
 ):
     s = Steps(*dims, w1, w2m, w2r, wsc, g1, g2)
@@ -485,7 +502,7 @@
         compiler_params=small,
         cost_estimate=cost(0),
         name="rows_out",
-    )(own, *got[::-1])
+    )(own, *[got[i] for i in ([0, 2, 1] if len(got) == 3 else range(len(got)))])
     got = swap("height", slabs)
     hid_in, mer_in = cols - 2, cols - 4
     worked = [
@@ -558,7 +575,7 @@
         compiler_params=params,
         cost_estimate=cost(2 * 10**9),
         name="outer",
-    )(got_a, got_b, w1, w2m, w2r, wsc, g1, g2, wdm, wdr, raw, *passed)
+    )(got_b, got_a, w1, w2m, w2r, wsc, g1, g2, wdm, wdr, raw, *passed)
 
 
 def solution(mesh):

time: 21 us -> 20.7 us (0.986)
  the two profiles are of different devices: /device:TPU:17 before, /device:TPU:0 now
where the time goes in v6:
time: 20.7 us; the launch traced here: 20.5 us
  Pallas kernels  13.6 us (66%)
  starting transfers between devices  6.88 us (33%)
    ppermute x6, starting transfers between devices, swap(): lax.ppermute(value, AXES, swap_pairs(axis, i))  6.88 us
    pallas_call x1, Pallas kernels, local(): pl.pallas_call(functools.partial(inner, dims), out_shape=worked + [pltpu....  4.13 us
    pallas_call x1, Pallas kernels, local(): pl.pallas_call(functools.partial(outer, dims), out_shape=jax.ShapeDtypeSt...  3.71 us
    pallas_call x1, Pallas kernels, local(): pl.pallas_call(functools.partial(early, dims), out_shape=worked, in_specs...  2.93 us
    pallas_call x1, Pallas kernels, local(): pl.pallas_call(functools.partial(arrange, c1), out_shape=[pltpu.VMEM(vide...  2.61 us
  transfers between devices with their start and end apart: 6, of which 0 were waited for; matrix products, arithmetic and copies ran while one was open for 0% of the time, Pallas kernels for 47%

profile of v6, /device:TPU:0, one launch (start us, length us, event | category | flops | bytes accessed | tf_op | source)
XLA Modules:
  0.0 20.5 jit_solution(7602657793488245776)
XLA Ops:
  0.0 3.0 %collective-permute-start = (bf16[4,8,1536]{2,1,0:T(8,128)(2,1)}, bf16[4,8,1536]{2,1,0:T(8,128)(2,1)S(1)}, u32[]{:S(2)}, u32[]{:S(2)}) collective-permute-start(bf16[4,8,1536]{2,1,0:T(8,128)(2,1)} %x.1), channel_id=1, source_target_pairs={{0,8},{1,9},{2,10},{3,11},{4,12},{5,13},{6,14},{7,15},{8,0},{9,1},... | collective-permute-start | bytes 294920 | tf_op jit(solution)/shard_map/ppermute | solution.py:54
  3.0 0.0 collective-permute-start.2
  3.0 0.5 %collective-permute-start.1 = (bf16[4,8,1536]{2,1,0:T(8,128)(2,1)}, bf16[4,8,1536]{2,1,0:T(8,128)(2,1)S(1)}, u32[]{:S(2)}, u32[]{:S(2)}) collective-permute-start(bf16[4,8,1536]{2,1,0:T(8,128)(2,1)} %x.1), channel_id=1, source_target_pairs={{0,1},{1,0},{2,3},{3,2},{4,5},{5,4},{6,7},{7,6},{8,9},{9,8},{10,11... | collective-permute-start | bytes 294920 | tf_op jit(solution)/shard_map/ppermute | solution.py:54
  3.5 2.6 %arrange.1 = (bf16[4,8,1536]{2,1,0:T(8,128)(2,1)S(1)}, f32[1,96]{1,0:T(1,128)S(1)}, f32[1,192]{1,0:T(1,128)S(1)}, bf16[128,192]{1,0:T(8,128)(2,1)S(1)}, bf16[3,3...) custom-call(bf16[4,8,1536]{2,1,0:T(8,128)(2,1)} %x.1, ...), custom_call_target="tpu_custom_call" | custom-call | bytes 5000000 | tf_op jit(solution)/shard_map/arrange/pallas_call | solution.py:471
  6.2 0.0 collective-permute-done.refs_0_
  6.2 0.0 collective-permute-done.2.refs_2_
  6.2 0.0 collective-permute-done.1.refs_1_
  6.2 0.1 rows_out.1
  6.3 1.6 %collective-permute-start.3 = (bf16[24,1536]{1,0:T(8,128)(2,1)S(1)}, bf16[24,1536]{1,0:T(8,128)(2,1)S(1)}, u32[]{:S(2)}, u32[]{:S(2)}) collective-permute-start(bf16[24,1536]{1,0:T(8,128)(2,1)S(1)} %get-tuple-element.30), channel_id=1, source_target_pairs={{0,4},{1,5},{2,6},{3,7},{4,0},{5,1},{6,2},{7,3},{8,12},{9,13},{10,... | collective-permute-start | bytes 221192 | tf_op jit(solution)/shard_map/ppermute | solution.py:54
  7.9 2.9 %early.1 = (f32[16,112,128]{2,1,0:T(8,128)S(1)}, f32[16,56,128]{2,1,0:T(8,128)S(1)}, f32[14,104,128]{2,1,0:T(8,128)S(1)}, f32[14,104,128]{2,1,0:T(8,128)S(1)}) custom-call(bf16[4,8,1536]{2,1,0:T(8,128)(2,1)S(1)} %get-tuple-element.28.own, bf16[4,8,1536]{2,1,0:T(8,128)(2,1)S(1)} %get-tuple-element.29.prev, f32[1,96]{1,0:T(1,128)S(1)} %get-tuple-element.37.g1, ...), custom_call_target="tpu_custom_call" | custom-call | flops 1000000000 | bytes 5000000 | tf_op jit(solution)/shard_map/early/pallas_call | solution.py:514
  10.9 0.0 collective-permute-done.3.refs_0_
  10.9 0.1 cols_out.1
  11.0 0.8 %collective-permute-start.4 = (bf16[112,384]{1,0:T(8,128)(2,1)S(1)}, bf16[112,384]{1,0:T(8,128)(2,1)S(1)}, u32[]{:S(2)}, u32[]{:S(2)}) collective-permute-start(bf16[112,384]{1,0:T(8,128)(2,1)S(1)} %get-tuple-element.31), channel_id=1, source_target_pairs={{0,3},{1,2},{2,1},{3,0},{4,7},{5,6},{6,5},{7,4},{8,11},{9,10},{10,... | collective-permute-start | bytes 258056 | tf_op jit(solution)/shard_map/ppermute | solution.py:54
  11.8 0.9 %collective-permute-start.5 = (bf16[112,384]{1,0:T(8,128)(2,1)S(1)}, bf16[112,384]{1,0:T(8,128)(2,1)S(1)}, u32[]{:S(2)}, u32[]{:S(2)}) collective-permute-start(bf16[112,384]{1,0:T(8,128)(2,1)S(1)} %get-tuple-element.32), channel_id=1, source_target_pairs={{0,1},{1,0},{2,3},{3,2},{4,5},{5,4},{6,7},{7,6},{8,9},{9,8},{10,11... | collective-permute-start | bytes 258056 | tf_op jit(solution)/shard_map/ppermute | solution.py:54
  12.7 4.1 %inner.1 = (f32[16,112,128]{2,1,0:T(8,128)S(1)}, f32[16,56,128]{2,1,0:T(8,128)S(1)}, f32[14,104,128]{2,1,0:T(8,128)S(1)}, f32[14,104,128]{2,1,0:T(8,128)S(1)}, b...) custom-call(bf16[48,1536]{1,0:T(8,128)(2,1)S(1)} %get-tuple-element., ...), custom_call_target="tpu_custom_call", output_to_operand_aliasing={{0}: (7, {}), {1}: (8, {}), {2}: (9, {}), {3}: (10, {})} | custom-call | flops 4000000000 | bytes 5000000 | tf_op jit(solution)/shard_map/inner/pallas_call | solution.py:536
  16.8 0.0 collective-permute-done.4.got_b
  16.8 0.0 collective-permute-done.5.got_a
  16.8 3.7 %outer.1 = bf16[4,4,1536]{2,1,0:T(4,128)(2,1)} custom-call(bf16[112,384]{1,0:T(8,128)(2,1)S(1)} %collective-permute-done.4.got_b, bf16[112,384]{1,0:T(8,128)(2,1)S(1)} %collective-permute-done.5.got_a, bf16[3,3,3,128,192]{4,3,2,1,0:T(8,128)(2,1)S(1)} %get-tuple-element.33.w1, bf16[3,3,3,128,192]{4,3,2,1,0:T(8,128)(2,1)S(1)} %get-tuple-element.34.w2m, ...), custom_call_target="tpu_custom_call" | custom-call | flops 2000000000 | bytes 5000000 | tf_op jit(solution)/shard_map/outer/pallas_call | solution.py:559
Async XLA Ops:
  0.0 6.2 %collective-permute-start = (bf16[4,8,1536]{2,1,0:T(8,128)(2,1)}, bf16[4,8,1536]{2,1,0:T(8,128)(2,1)S(1)}, u32[]{:S(2)}, u32[]{:S(2)}) collective-permute-start(bf16[4,8,1536]{2,1,0:T(8,128)(2,1)} %x.1), channel_id=1, source_target_pairs={{0,8},{1,9},{2,10},{3,11},{4,12},{5,13},{6,14},{7,15},{8,0},{9,1},... | collective-permute-start | bytes 294920 | tf_op jit(solution)/shard_map/ppermute | solution.py:54
  3.0 3.1 %collective-permute-start.2 = (bf16[4,8,1536]{2,1,0:T(8,128)(2,1)}, bf16[4,8,1536]{2,1,0:T(8,128)(2,1)S(1)}, u32[]{:S(2)}, u32[]{:S(2)}) collective-permute-start(bf16[4,8,1536]{2,1,0:T(8,128)(2,1)} %x.1), channel_id=1, source_target_pairs={{0,1},{1,0},{2,3},{3,2},{4,5},{5,4},{6,7},{7,6},{8,16},{9,17},{10,... | collective-permute-start | bytes 294920 | tf_op jit(solution)/shard_map/ppermute | solution.py:54
  3.0 3.2 %collective-permute-start.1 = (bf16[4,8,1536]{2,1,0:T(8,128)(2,1)}, bf16[4,8,1536]{2,1,0:T(8,128)(2,1)S(1)}, u32[]{:S(2)}, u32[]{:S(2)}) collective-permute-start(bf16[4,8,1536]{2,1,0:T(8,128)(2,1)} %x.1), channel_id=1, source_target_pairs={{0,1},{1,0},{2,3},{3,2},{4,5},{5,4},{6,7},{7,6},{8,9},{9,8},{10,11... | collective-permute-start | bytes 294920 | tf_op jit(solution)/shard_map/ppermute | solution.py:54
  6.3 4.6 %collective-permute-start.3 = (bf16[24,1536]{1,0:T(8,128)(2,1)S(1)}, bf16[24,1536]{1,0:T(8,128)(2,1)S(1)}, u32[]{:S(2)}, u32[]{:S(2)}) collective-permute-start(bf16[24,1536]{1,0:T(8,128)(2,1)S(1)} %get-tuple-element.30), channel_id=1, source_target_pairs={{0,4},{1,5},{2,6},{3,7},{4,0},{5,1},{6,2},{7,3},{8,12},{9,13},{10,... | collective-permute-start | bytes 221192 | tf_op jit(solution)/shard_map/ppermute | solution.py:54
  11.0 5.8 %collective-permute-start.4 = (bf16[112,384]{1,0:T(8,128)(2,1)S(1)}, bf16[112,384]{1,0:T(8,128)(2,1)S(1)}, u32[]{:S(2)}, u32[]{:S(2)}) collective-permute-start(bf16[112,384]{1,0:T(8,128)(2,1)S(1)} %get-tuple-element.31), channel_id=1, source_target_pairs={{0,3},{1,2},{2,1},{3,0},{4,7},{5,6},{6,5},{7,4},{8,11},{9,10},{10,... | collective-permute-start | bytes 258056 | tf_op jit(solution)/shard_map/ppermute | solution.py:54
  11.8 5.0 %collective-permute-start.5 = (bf16[112,384]{1,0:T(8,128)(2,1)S(1)}, bf16[112,384]{1,0:T(8,128)(2,1)S(1)}, u32[]{:S(2)}, u32[]{:S(2)}) collective-permute-start(bf16[112,384]{1,0:T(8,128)(2,1)S(1)} %get-tuple-element.32), channel_id=1, source_target_pairs={{0,1},{1,0},{2,3},{3,2},{4,5},{5,4},{6,7},{7,6},{8,9},{9,8},{10,11... | collective-permute-start | bytes 258056 | tf_op jit(solution)/shard_map/ppermute | solution.py:54

commit v7 on v6

--- a/solution.py
+++ b/solution.py
@@ -282,6 +282,8 @@
             low[c, at : at + n, :] = chunk[:, :LANES]
             high[c, at : at + n, 0 : self.rest] = chunk[:, LANES:]
             high[c, at : at + n - 1, self.rest : 2 * self.rest] = chunk[1:, LANES:]
+            gap = jnp.zeros((1, self.rest), jnp.float32)
+            high[c, at + n - 1 : at + n, self.rest : 2 * self.rest] = gap
 
     def down(self, lows, highs, wanted, stack, wdm, wdr, result):
         bf = jnp.bfloat16
@@ -321,7 +323,7 @@
             s.place_rim(c, None, first)
             s.stack_first(c, first, stack1)
     hidden = list(range(LOW, s.cols))
-    step = 7
+    step = 14
     for start in range(0, len(hidden), step):
         wanted = hidden[start : start + step]
         acc = s.conv_first(lambda c: stack1[c - LOW], wanted)
@@ -335,9 +337,6 @@
     first, raw, acc_a, acc_b, stack1, stack2, mer_a, mer_b, sec_a, sec_b, rims, stack_rim,
 ):
     s = Steps(*dims, w1, w2m, w2r, wsc, g1, g2)
-    sec_b[...] = jnp.zeros_like(sec_b)
-    mer_a[...] = jnp.zeros_like(mer_a)
-    mer_b[...] = jnp.zeros_like(mer_b)
     spread = s.spread()
     n = 2 * s.frames
     tall = rim.shape[0]
@@ -357,7 +356,7 @@
             if c in edge:
                 s.place_rim(c, u, first)
     hidden = list(range(LOW, s.cols))
-    step = 7
+    step = 5
     for start in range(0, len(hidden), step):
         wanted = hidden[start : start + step]
         gap = jnp.zeros((n, LANES - s.rest), jnp.float32)
@@ -372,7 +371,7 @@
     for i, c in enumerate(edge):
         s.stack_first(c, first, stack1, i)
     merged = list(range(LOW, s.cols - 2))
-    step = 6
+    step = 3
     for start in range(0, len(merged), step):
         wanted = merged[start : start + step]
         acc = s.conv_second(
@@ -388,9 +387,6 @@
 ):
     s = Steps(*dims, w1, w2m, w2r, wsc, g1, g2)
     cols, M1, M2 = s.cols, s.M1, s.M2
-    sec_b[...] = jnp.zeros_like(sec_b)
-    mer_a[...] = jnp.zeros_like(mer_a)
-    mer_b[...] = jnp.zeros_like(mer_b)
     tail = 2 * s.frames * s.R
     first[:, tail:, :] = jnp.zeros((first.shape[0], first.shape[1] - tail, LANES), jnp.float32)
     spread = s.spread()

time: 20.7 us -> 20.5 us (level)
  no operation moved by 1% of the time
where the time goes in v7:
time: 20.5 us; the launch traced here: 20.4 us
  Pallas kernels  13.4 us (65%)
  starting transfers between devices  6.88 us (34%)
    ppermute x6, starting transfers between devices, swap(): lax.ppermute(value, AXES, swap_pairs(axis, i))  6.88 us
    pallas_call x1, Pallas kernels, local(): pl.pallas_call(functools.partial(inner, dims), out_shape=worked + [pltpu....  4.04 us
    pallas_call x1, Pallas kernels, local(): pl.pallas_call(functools.partial(outer, dims), out_shape=jax.ShapeDtypeSt...  3.68 us
    pallas_call x1, Pallas kernels, local(): pl.pallas_call(functools.partial(early, dims), out_shape=worked, in_specs...  2.88 us
    pallas_call x1, Pallas kernels, local(): pl.pallas_call(functools.partial(arrange, c1), out_shape=[pltpu.VMEM(vide...  2.61 us
  transfers between devices with their start and end apart: 6, of which 0 were waited for; matrix products, arithmetic and copies ran while one was open for 0% of the time, Pallas kernels for 47%

profile of v7, /device:TPU:0, one launch (start us, length us, event | category | flops | bytes accessed | tf_op | source)
XLA Modules:
  0.0 20.4 jit_solution(16722283256980767404)
XLA Ops:
  0.0 3.0 %collective-permute-start = (bf16[4,8,1536]{2,1,0:T(8,128)(2,1)}, bf16[4,8,1536]{2,1,0:T(8,128)(2,1)S(1)}, u32[]{:S(2)}, u32[]{:S(2)}) collective-permute-start(bf16[4,8,1536]{2,1,0:T(8,128)(2,1)} %x.1), channel_id=1, source_target_pairs={{0,8},{1,9},{2,10},{3,11},{4,12},{5,13},{6,14},{7,15},{8,0},{9,1},... | collective-permute-start | bytes 294920 | tf_op jit(solution)/shard_map/ppermute | solution.py:54
  3.0 0.0 collective-permute-start.2
  3.0 0.5 %collective-permute-start.1 = (bf16[4,8,1536]{2,1,0:T(8,128)(2,1)}, bf16[4,8,1536]{2,1,0:T(8,128)(2,1)S(1)}, u32[]{:S(2)}, u32[]{:S(2)}) collective-permute-start(bf16[4,8,1536]{2,1,0:T(8,128)(2,1)} %x.1), channel_id=1, source_target_pairs={{0,1},{1,0},{2,3},{3,2},{4,5},{5,4},{6,7},{7,6},{8,9},{9,8},{10,11... | collective-permute-start | bytes 294920 | tf_op jit(solution)/shard_map/ppermute | solution.py:54
  3.5 2.6 %arrange.1 = (bf16[4,8,1536]{2,1,0:T(8,128)(2,1)S(1)}, f32[1,96]{1,0:T(1,128)S(1)}, f32[1,192]{1,0:T(1,128)S(1)}, bf16[128,192]{1,0:T(8,128)(2,1)S(1)}, bf16[3,3...) custom-call(bf16[4,8,1536]{2,1,0:T(8,128)(2,1)} %x.1, ...), custom_call_target="tpu_custom_call" | custom-call | bytes 5000000 | tf_op jit(solution)/shard_map/arrange/pallas_call | solution.py:467
  6.2 0.0 collective-permute-done.refs_0_
  6.2 0.0 collective-permute-done.2.refs_2_
  6.2 0.0 collective-permute-done.1.refs_1_
  6.2 0.1 rows_out.1
  6.3 1.6 %collective-permute-start.3 = (bf16[24,1536]{1,0:T(8,128)(2,1)S(1)}, bf16[24,1536]{1,0:T(8,128)(2,1)S(1)}, u32[]{:S(2)}, u32[]{:S(2)}) collective-permute-start(bf16[24,1536]{1,0:T(8,128)(2,1)S(1)} %get-tuple-element.30), channel_id=1, source_target_pairs={{0,4},{1,5},{2,6},{3,7},{4,0},{5,1},{6,2},{7,3},{8,12},{9,13},{10,... | collective-permute-start | bytes 221192 | tf_op jit(solution)/shard_map/ppermute | solution.py:54
  7.9 2.9 %early.1 = (f32[16,112,128]{2,1,0:T(8,128)S(1)}, f32[16,56,128]{2,1,0:T(8,128)S(1)}, f32[14,104,128]{2,1,0:T(8,128)S(1)}, f32[14,104,128]{2,1,0:T(8,128)S(1)}) custom-call(bf16[4,8,1536]{2,1,0:T(8,128)(2,1)S(1)} %get-tuple-element.28.own, bf16[4,8,1536]{2,1,0:T(8,128)(2,1)S(1)} %get-tuple-element.29.prev, f32[1,96]{1,0:T(1,128)S(1)} %get-tuple-element.37.g1, ...), custom_call_target="tpu_custom_call" | custom-call | flops 1000000000 | bytes 5000000 | tf_op jit(solution)/shard_map/early/pallas_call | solution.py:510
  10.8 0.0 collective-permute-done.3.refs_0_
  10.8 0.1 cols_out.1
  10.9 0.8 %collective-permute-start.4 = (bf16[112,384]{1,0:T(8,128)(2,1)S(1)}, bf16[112,384]{1,0:T(8,128)(2,1)S(1)}, u32[]{:S(2)}, u32[]{:S(2)}) collective-permute-start(bf16[112,384]{1,0:T(8,128)(2,1)S(1)} %get-tuple-element.31), channel_id=1, source_target_pairs={{0,3},{1,2},{2,1},{3,0},{4,7},{5,6},{6,5},{7,4},{8,11},{9,10},{10,... | collective-permute-start | bytes 258056 | tf_op jit(solution)/shard_map/ppermute | solution.py:54
  11.7 0.9 %collective-permute-start.5 = (bf16[112,384]{1,0:T(8,128)(2,1)S(1)}, bf16[112,384]{1,0:T(8,128)(2,1)S(1)}, u32[]{:S(2)}, u32[]{:S(2)}) collective-permute-start(bf16[112,384]{1,0:T(8,128)(2,1)S(1)} %get-tuple-element.32), channel_id=1, source_target_pairs={{0,1},{1,0},{2,3},{3,2},{4,5},{5,4},{6,7},{7,6},{8,9},{9,8},{10,11... | collective-permute-start | bytes 258056 | tf_op jit(solution)/shard_map/ppermute | solution.py:54
  12.6 4.0 %inner.1 = (f32[16,112,128]{2,1,0:T(8,128)S(1)}, f32[16,56,128]{2,1,0:T(8,128)S(1)}, f32[14,104,128]{2,1,0:T(8,128)S(1)}, f32[14,104,128]{2,1,0:T(8,128)S(1)}, b...) custom-call(bf16[48,1536]{1,0:T(8,128)(2,1)S(1)} %get-tuple-element., ...), custom_call_target="tpu_custom_call", output_to_operand_aliasing={{0}: (7, {}), {1}: (8, {}), {2}: (9, {}), {3}: (10, {})} | custom-call | flops 4000000000 | bytes 5000000 | tf_op jit(solution)/shard_map/inner/pallas_call | solution.py:532
  16.7 0.0 collective-permute-done.4.got_b
  16.7 0.0 collective-permute-done.5.got_a
  16.7 3.7 %outer.1 = bf16[4,4,1536]{2,1,0:T(4,128)(2,1)} custom-call(bf16[112,384]{1,0:T(8,128)(2,1)S(1)} %collective-permute-done.4.got_b, bf16[112,384]{1,0:T(8,128)(2,1)S(1)} %collective-permute-done.5.got_a, bf16[3,3,3,128,192]{4,3,2,1,0:T(8,128)(2,1)S(1)} %get-tuple-element.33.w1, bf16[3,3,3,128,192]{4,3,2,1,0:T(8,128)(2,1)S(1)} %get-tuple-element.34.w2m, ...), custom_call_target="tpu_custom_call" | custom-call | flops 2000000000 | bytes 5000000 | tf_op jit(solution)/shard_map/outer/pallas_call | solution.py:555
Async XLA Ops:
  0.0 6.2 %collective-permute-start = (bf16[4,8,1536]{2,1,0:T(8,128)(2,1)}, bf16[4,8,1536]{2,1,0:T(8,128)(2,1)S(1)}, u32[]{:S(2)}, u32[]{:S(2)}) collective-permute-start(bf16[4,8,1536]{2,1,0:T(8,128)(2,1)} %x.1), channel_id=1, source_target_pairs={{0,8},{1,9},{2,10},{3,11},{4,12},{5,13},{6,14},{7,15},{8,0},{9,1},... | collective-permute-start | bytes 294920 | tf_op jit(solution)/shard_map/ppermute | solution.py:54
  3.0 3.1 %collective-permute-start.2 = (bf16[4,8,1536]{2,1,0:T(8,128)(2,1)}, bf16[4,8,1536]{2,1,0:T(8,128)(2,1)S(1)}, u32[]{:S(2)}, u32[]{:S(2)}) collective-permute-start(bf16[4,8,1536]{2,1,0:T(8,128)(2,1)} %x.1), channel_id=1, source_target_pairs={{0,1},{1,0},{2,3},{3,2},{4,5},{5,4},{6,7},{7,6},{8,16},{9,17},{10,... | collective-permute-start | bytes 294920 | tf_op jit(solution)/shard_map/ppermute | solution.py:54
  3.0 3.2 %collective-permute-start.1 = (bf16[4,8,1536]{2,1,0:T(8,128)(2,1)}, bf16[4,8,1536]{2,1,0:T(8,128)(2,1)S(1)}, u32[]{:S(2)}, u32[]{:S(2)}) collective-permute-start(bf16[4,8,1536]{2,1,0:T(8,128)(2,1)} %x.1), channel_id=1, source_target_pairs={{0,1},{1,0},{2,3},{3,2},{4,5},{5,4},{6,7},{7,6},{8,9},{9,8},{10,11... | collective-permute-start | bytes 294920 | tf_op jit(solution)/shard_map/ppermute | solution.py:54
  6.3 4.5 %collective-permute-start.3 = (bf16[24,1536]{1,0:T(8,128)(2,1)S(1)}, bf16[24,1536]{1,0:T(8,128)(2,1)S(1)}, u32[]{:S(2)}, u32[]{:S(2)}) collective-permute-start(bf16[24,1536]{1,0:T(8,128)(2,1)S(1)} %get-tuple-element.30), channel_id=1, source_target_pairs={{0,4},{1,5},{2,6},{3,7},{4,0},{5,1},{6,2},{7,3},{8,12},{9,13},{10,... | collective-permute-start | bytes 221192 | tf_op jit(solution)/shard_map/ppermute | solution.py:54
  10.9 5.8 %collective-permute-start.4 = (bf16[112,384]{1,0:T(8,128)(2,1)S(1)}, bf16[112,384]{1,0:T(8,128)(2,1)S(1)}, u32[]{:S(2)}, u32[]{:S(2)}) collective-permute-start(bf16[112,384]{1,0:T(8,128)(2,1)S(1)} %get-tuple-element.31), channel_id=1, source_target_pairs={{0,3},{1,2},{2,1},{3,0},{4,7},{5,6},{6,5},{7,4},{8,11},{9,10},{10,... | collective-permute-start | bytes 258056 | tf_op jit(solution)/shard_map/ppermute | solution.py:54
  11.7 4.9 %collective-permute-start.5 = (bf16[112,384]{1,0:T(8,128)(2,1)S(1)}, bf16[112,384]{1,0:T(8,128)(2,1)S(1)}, u32[]{:S(2)}, u32[]{:S(2)}) collective-permute-start(bf16[112,384]{1,0:T(8,128)(2,1)S(1)} %get-tuple-element.32), channel_id=1, source_target_pairs={{0,1},{1,0},{2,3},{3,2},{4,5},{5,4},{6,7},{7,6},{8,9},{9,8},{10,11... | collective-permute-start | bytes 258056 | tf_op jit(solution)/shard_map/ppermute | solution.py:54

commit v8 on v7

--- a/solution.py
+++ b/solution.py
@@ -99,7 +99,7 @@
     for k in range(lanes // LANES):
         tile = slice(k * LANES, (k + 1) * LANES)
         for ref, value in zip((above, below), values):
-            ref[k] = value[:, tile]
+            ref[k, 0 : 2 * frames * HIGH, :] = value[:, tile]
         parts = [above[k, pl.ds(r, 2 * frames, stride=HIGH), :] for r in range(HIGH - LOW, HIGH)]
         parts += [below[k, pl.ds(r, 2 * frames, stride=HIGH), :] for r in range(HIGH)]
         parts.append(jnp.zeros((rim.shape[0] - len(parts) * 2 * frames, LANES), jnp.float32))
@@ -456,9 +456,9 @@
     R = rows + LOW + HIGH
     M1 = up((frames + 1) * R + rows + 3, 16)
     M2 = up((frames - 1) * R + rows + 1, 16)
-    first_rows = up(M1 + 2 * R + 2, 8)
-    acc_rows = up(2 * frames * R, 8)
-    raw_rows = up(M2 + LOW, 8)
+    first_rows = up(max(M1 + 2 * R + 2, (2 * frames + 1) * R), 8)
+    acc_rows = up((2 * frames + 1) * R, 8)
+    raw_rows = up(max(M2 + LOW, (frames + 1) * R), 8)
     count = up((frames - 1) * (rows + 2) // 2 + rows // 2, 8)
     held = up(2 * count + 1, 8)
 
@@ -522,7 +522,7 @@
         out_shape=[pltpu.VMEM((rim_tall, merged_cols), bf)] + [pltpu.VMEM((tall, EDGE * c1), bf)] * 2,
         in_specs=[vmem] * (2 + len(got)),
         out_specs=[vmem] * 3,
-        scratch_shapes=[pltpu.VMEM((merged_cols // LANES, 2 * frames * HIGH, LANES), f32)] * 2,
+        scratch_shapes=[pltpu.VMEM((merged_cols // LANES, up((2 * frames + 1) * HIGH, 8), LANES), f32)] * 2,
         compiler_params=small,
         cost_estimate=cost(0),
         name="cols_out",

time: 20.5 us -> 20.6 us (level)
  no operation moved by 1% of the time
where the time goes in v8:
time: 20.6 us; the launch traced here: 20.4 us
  Pallas kernels  13.5 us (66%)
  starting transfers between devices  6.88 us (33%)
    ppermute x6, starting transfers between devices, swap(): lax.ppermute(value, AXES, swap_pairs(axis, i))  6.88 us
    pallas_call x1, Pallas kernels, local(): pl.pallas_call(functools.partial(inner, dims), out_shape=worked + [pltpu....  4.08 us
    pallas_call x1, Pallas kernels, local(): pl.pallas_call(functools.partial(outer, dims), out_shape=jax.ShapeDtypeSt...  3.69 us
    pallas_call x1, Pallas kernels, local(): pl.pallas_call(functools.partial(early, dims), out_shape=worked, in_specs...  2.91 us
    pallas_call x1, Pallas kernels, local(): pl.pallas_call(functools.partial(arrange, c1), out_shape=[pltpu.VMEM(vide...  2.61 us
  transfers between devices with their start and end apart: 6, of which 0 were waited for; matrix products, arithmetic and copies ran while one was open for 0% of the time, Pallas kernels for 47%

profile of v8, /device:TPU:0, one launch (start us, length us, event | category | flops | bytes accessed | tf_op | source)
XLA Modules:
  0.0 20.4 jit_solution(10299868451522853767)
XLA Ops:
  0.0 3.0 %collective-permute-start = (bf16[4,8,1536]{2,1,0:T(8,128)(2,1)}, bf16[4,8,1536]{2,1,0:T(8,128)(2,1)S(1)}, u32[]{:S(2)}, u32[]{:S(2)}) collective-permute-start(bf16[4,8,1536]{2,1,0:T(8,128)(2,1)} %x.1), channel_id=1, source_target_pairs={{0,8},{1,9},{2,10},{3,11},{4,12},{5,13},{6,14},{7,15},{8,0},{9,1},... | collective-permute-start | bytes 294920 | tf_op jit(solution)/shard_map/ppermute | solution.py:54
  3.0 0.0 collective-permute-start.2
  3.0 0.5 %collective-permute-start.1 = (bf16[4,8,1536]{2,1,0:T(8,128)(2,1)}, bf16[4,8,1536]{2,1,0:T(8,128)(2,1)S(1)}, u32[]{:S(2)}, u32[]{:S(2)}) collective-permute-start(bf16[4,8,1536]{2,1,0:T(8,128)(2,1)} %x.1), channel_id=1, source_target_pairs={{0,1},{1,0},{2,3},{3,2},{4,5},{5,4},{6,7},{7,6},{8,9},{9,8},{10,11... | collective-permute-start | bytes 294920 | tf_op jit(solution)/shard_map/ppermute | solution.py:54
  3.5 2.6 %arrange.1 = (bf16[4,8,1536]{2,1,0:T(8,128)(2,1)S(1)}, f32[1,96]{1,0:T(1,128)S(1)}, f32[1,192]{1,0:T(1,128)S(1)}, bf16[128,192]{1,0:T(8,128)(2,1)S(1)}, bf16[3,3...) custom-call(bf16[4,8,1536]{2,1,0:T(8,128)(2,1)} %x.1, ...), custom_call_target="tpu_custom_call" | custom-call | bytes 5000000 | tf_op jit(solution)/shard_map/arrange/pallas_call | solution.py:467
  6.2 0.0 collective-permute-done.refs_0_
  6.2 0.0 collective-permute-done.2.refs_2_
  6.2 0.0 collective-permute-done.1.refs_1_
  6.2 0.1 rows_out.1
  6.3 1.6 %collective-permute-start.3 = (bf16[24,1536]{1,0:T(8,128)(2,1)S(1)}, bf16[24,1536]{1,0:T(8,128)(2,1)S(1)}, u32[]{:S(2)}, u32[]{:S(2)}) collective-permute-start(bf16[24,1536]{1,0:T(8,128)(2,1)S(1)} %get-tuple-element.30), channel_id=1, source_target_pairs={{0,4},{1,5},{2,6},{3,7},{4,0},{5,1},{6,2},{7,3},{8,12},{9,13},{10,... | collective-permute-start | bytes 221192 | tf_op jit(solution)/shard_map/ppermute | solution.py:54
  7.9 2.9 %early.1 = (f32[16,120,128]{2,1,0:T(8,128)S(1)}, f32[16,72,128]{2,1,0:T(8,128)S(1)}, f32[14,120,128]{2,1,0:T(8,128)S(1)}, f32[14,120,128]{2,1,0:T(8,128)S(1)}) custom-call(bf16[4,8,1536]{2,1,0:T(8,128)(2,1)S(1)} %get-tuple-element.28.own, bf16[4,8,1536]{2,1,0:T(8,128)(2,1)S(1)} %get-tuple-element.29.prev, f32[1,96]{1,0:T(1,128)S(1)} %get-tuple-element.37.g1, ...), custom_call_target="tpu_custom_call" | custom-call | flops 1000000000 | bytes 5000000 | tf_op jit(solution)/shard_map/early/pallas_call | solution.py:510
  10.9 0.0 collective-permute-done.3.refs_0_
  10.9 0.1 cols_out.1
  11.0 0.8 %collective-permute-start.4 = (bf16[112,384]{1,0:T(8,128)(2,1)S(1)}, bf16[112,384]{1,0:T(8,128)(2,1)S(1)}, u32[]{:S(2)}, u32[]{:S(2)}) collective-permute-start(bf16[112,384]{1,0:T(8,128)(2,1)S(1)} %get-tuple-element.31), channel_id=1, source_target_pairs={{0,3},{1,2},{2,1},{3,0},{4,7},{5,6},{6,5},{7,4},{8,11},{9,10},{10,... | collective-permute-start | bytes 258056 | tf_op jit(solution)/shard_map/ppermute | solution.py:54
  11.8 0.9 %collective-permute-start.5 = (bf16[112,384]{1,0:T(8,128)(2,1)S(1)}, bf16[112,384]{1,0:T(8,128)(2,1)S(1)}, u32[]{:S(2)}, u32[]{:S(2)}) collective-permute-start(bf16[112,384]{1,0:T(8,128)(2,1)S(1)} %get-tuple-element.32), channel_id=1, source_target_pairs={{0,1},{1,0},{2,3},{3,2},{4,5},{5,4},{6,7},{7,6},{8,9},{9,8},{10,11... | collective-permute-start | bytes 258056 | tf_op jit(solution)/shard_map/ppermute | solution.py:54
  12.7 4.1 %inner.1 = (f32[16,120,128]{2,1,0:T(8,128)S(1)}, f32[16,72,128]{2,1,0:T(8,128)S(1)}, f32[14,120,128]{2,1,0:T(8,128)S(1)}, f32[14,120,128]{2,1,0:T(8,128)S(1)}, b...) custom-call(bf16[48,1536]{1,0:T(8,128)(2,1)S(1)} %get-tuple-element., ...), custom_call_target="tpu_custom_call", output_to_operand_aliasing={{0}: (7, {}), {1}: (8, {}), {2}: (9, {}), {3}: (10, {})} | custom-call | flops 4000000000 | bytes 5000000 | tf_op jit(solution)/shard_map/inner/pallas_call | solution.py:532
  16.7 0.0 collective-permute-done.4.got_b
  16.7 0.0 collective-permute-done.5.got_a
  16.8 3.7 %outer.1 = bf16[4,4,1536]{2,1,0:T(4,128)(2,1)} custom-call(bf16[112,384]{1,0:T(8,128)(2,1)S(1)} %collective-permute-done.4.got_b, bf16[112,384]{1,0:T(8,128)(2,1)S(1)} %collective-permute-done.5.got_a, bf16[3,3,3,128,192]{4,3,2,1,0:T(8,128)(2,1)S(1)} %get-tuple-element.33.w1, bf16[3,3,3,128,192]{4,3,2,1,0:T(8,128)(2,1)S(1)} %get-tuple-element.34.w2m, ...), custom_call_target="tpu_custom_call" | custom-call | flops 2000000000 | bytes 5000000 | tf_op jit(solution)/shard_map/outer/pallas_call | solution.py:555
Async XLA Ops:
  0.0 6.2 %collective-permute-start = (bf16[4,8,1536]{2,1,0:T(8,128)(2,1)}, bf16[4,8,1536]{2,1,0:T(8,128)(2,1)S(1)}, u32[]{:S(2)}, u32[]{:S(2)}) collective-permute-start(bf16[4,8,1536]{2,1,0:T(8,128)(2,1)} %x.1), channel_id=1, source_target_pairs={{0,8},{1,9},{2,10},{3,11},{4,12},{5,13},{6,14},{7,15},{8,0},{9,1},... | collective-permute-start | bytes 294920 | tf_op jit(solution)/shard_map/ppermute | solution.py:54
  3.0 3.1 %collective-permute-start.2 = (bf16[4,8,1536]{2,1,0:T(8,128)(2,1)}, bf16[4,8,1536]{2,1,0:T(8,128)(2,1)S(1)}, u32[]{:S(2)}, u32[]{:S(2)}) collective-permute-start(bf16[4,8,1536]{2,1,0:T(8,128)(2,1)} %x.1), channel_id=1, source_target_pairs={{0,1},{1,0},{2,3},{3,2},{4,5},{5,4},{6,7},{7,6},{8,16},{9,17},{10,... | collective-permute-start | bytes 294920 | tf_op jit(solution)/shard_map/ppermute | solution.py:54
  3.0 3.2 %collective-permute-start.1 = (bf16[4,8,1536]{2,1,0:T(8,128)(2,1)}, bf16[4,8,1536]{2,1,0:T(8,128)(2,1)S(1)}, u32[]{:S(2)}, u32[]{:S(2)}) collective-permute-start(bf16[4,8,1536]{2,1,0:T(8,128)(2,1)} %x.1), channel_id=1, source_target_pairs={{0,1},{1,0},{2,3},{3,2},{4,5},{5,4},{6,7},{7,6},{8,9},{9,8},{10,11... | collective-permute-start | bytes 294920 | tf_op jit(solution)/shard_map/ppermute | solution.py:54
  6.3 4.6 %collective-permute-start.3 = (bf16[24,1536]{1,0:T(8,128)(2,1)S(1)}, bf16[24,1536]{1,0:T(8,128)(2,1)S(1)}, u32[]{:S(2)}, u32[]{:S(2)}) collective-permute-start(bf16[24,1536]{1,0:T(8,128)(2,1)S(1)} %get-tuple-element.30), channel_id=1, source_target_pairs={{0,4},{1,5},{2,6},{3,7},{4,0},{5,1},{6,2},{7,3},{8,12},{9,13},{10,... | collective-permute-start | bytes 221192 | tf_op jit(solution)/shard_map/ppermute | solution.py:54
  11.0 5.8 %collective-permute-start.4 = (bf16[112,384]{1,0:T(8,128)(2,1)S(1)}, bf16[112,384]{1,0:T(8,128)(2,1)S(1)}, u32[]{:S(2)}, u32[]{:S(2)}) collective-permute-start(bf16[112,384]{1,0:T(8,128)(2,1)S(1)} %get-tuple-element.31), channel_id=1, source_target_pairs={{0,3},{1,2},{2,1},{3,0},{4,7},{5,6},{6,5},{7,4},{8,11},{9,10},{10,... | collective-permute-start | bytes 258056 | tf_op jit(solution)/shard_map/ppermute | solution.py:54
  11.8 5.0 %collective-permute-start.5 = (bf16[112,384]{1,0:T(8,128)(2,1)S(1)}, bf16[112,384]{1,0:T(8,128)(2,1)S(1)}, u32[]{:S(2)}, u32[]{:S(2)}) collective-permute-start(bf16[112,384]{1,0:T(8,128)(2,1)S(1)} %get-tuple-element.32), channel_id=1, source_target_pairs={{0,1},{1,0},{2,3},{3,2},{4,5},{5,4},{6,7},{7,6},{8,9},{9,8},{10,11... | collective-permute-start | bytes 258056 | tf_op jit(solution)/shard_map/ppermute | solution.py:54

commit v9 on v8

--- a/solution.py
+++ b/solution.py
@@ -225,7 +225,7 @@
         n = 2 * self.frames
         sums = {}
         for dr in range(3):
-            lhs = [jnp.concatenate([get(c + dc, dr) for dc in range(3)], axis=-1) for c in wanted]
+            lhs = [jnp.concatenate([get(c + dc, dr) for dc in range(3)], axis=-1) for c in wanted[::2]]
             part = jnp.dot(
                 jnp.concatenate(lhs, axis=0),
                 self.w1[:, :, dr].reshape(9 * LANES, self.c2),
@@ -348,15 +348,16 @@
             c = group * EDGE + k
             rims[c, 0:tall, :] = u
             s.place_raw(c, v, raw)
-            for dr in range(3):
-                for dt in range(3):
-                    off = dr * n + dt
-                    part = rims[c, off : off + stack_rim.shape[2], :]
-                    stack_rim[c, dr, :, dt * LANES : (dt + 1) * LANES] = part.astype(jnp.bfloat16)
             if c in edge:
                 s.place_rim(c, u, first)
+    for c in range(s.cols - 1):
+        for dr in range(3):
+            for dt in range(3):
+                rows = slice(dr * n + dt, dr * n + dt + 3 * n)
+                part = jnp.concatenate([rims[c, rows, :], rims[c + 1, rows, :]], axis=0)
+                stack_rim[c, dr, :, dt * LANES : (dt + 1) * LANES] = part.astype(jnp.bfloat16)
     hidden = list(range(LOW, s.cols))
-    step = 5
+    step = 6
     for start in range(0, len(hidden), step):
         wanted = hidden[start : start + step]
         gap = jnp.zeros((n, LANES - s.rest), jnp.float32)
@@ -544,7 +545,7 @@
             pltpu.VMEM((hid_in, M1, LANES), f32),
             pltpu.VMEM((hid_in, M1, LANES), f32),
             pltpu.VMEM((cols, rim_tall + 8, LANES), f32),
-            pltpu.VMEM((cols, 3, 32, 3 * LANES), bf),
+            pltpu.VMEM((cols - 1, 3, 12 * frames, 3 * LANES), bf),
         ],
         input_output_aliases={7: 0, 8: 1, 9: 2, 10: 3},
         compiler_params=params,

time: 20.6 us -> 20.5 us (level)
  no operation moved by 1% of the time
where the time goes in v9:
time: 20.5 us; the launch traced here: 20.3 us
  Pallas kernels  13.4 us (65%)
  starting transfers between devices  6.88 us (34%)
    ppermute x6, starting transfers between devices, swap(): lax.ppermute(value, AXES, swap_pairs(axis, i))  6.88 us
    pallas_call x1, Pallas kernels, local(): pl.pallas_call(functools.partial(inner, dims), out_shape=worked + [pltpu....  3.98 us
    pallas_call x1, Pallas kernels, local(): pl.pallas_call(functools.partial(outer, dims), out_shape=jax.ShapeDtypeSt...  3.69 us
    pallas_call x1, Pallas kernels, local(): pl.pallas_call(functools.partial(early, dims), out_shape=worked, in_specs...  2.91 us
    pallas_call x1, Pallas kernels, local(): pl.pallas_call(functools.partial(arrange, c1), out_shape=[pltpu.VMEM(vide...  2.61 us
  transfers between devices with their start and end apart: 6, of which 0 were waited for; matrix products, arithmetic and copies ran while one was open for 0% of the time, Pallas kernels for 47%

profile of v9, /device:TPU:0, one launch (start us, length us, event | category | flops | bytes accessed | tf_op | source)
XLA Modules:
  0.0 20.3 jit_solution(13586368088235381136)
XLA Ops:
  0.0 3.0 %collective-permute-start = (bf16[4,8,1536]{2,1,0:T(8,128)(2,1)}, bf16[4,8,1536]{2,1,0:T(8,128)(2,1)S(1)}, u32[]{:S(2)}, u32[]{:S(2)}) collective-permute-start(bf16[4,8,1536]{2,1,0:T(8,128)(2,1)} %x.1), channel_id=1, source_target_pairs={{0,8},{1,9},{2,10},{3,11},{4,12},{5,13},{6,14},{7,15},{8,0},{9,1},... | collective-permute-start | bytes 294920 | tf_op jit(solution)/shard_map/ppermute | solution.py:54
  3.0 0.0 collective-permute-start.2
  3.0 0.5 %collective-permute-start.1 = (bf16[4,8,1536]{2,1,0:T(8,128)(2,1)}, bf16[4,8,1536]{2,1,0:T(8,128)(2,1)S(1)}, u32[]{:S(2)}, u32[]{:S(2)}) collective-permute-start(bf16[4,8,1536]{2,1,0:T(8,128)(2,1)} %x.1), channel_id=1, source_target_pairs={{0,1},{1,0},{2,3},{3,2},{4,5},{5,4},{6,7},{7,6},{8,9},{9,8},{10,11... | collective-permute-start | bytes 294920 | tf_op jit(solution)/shard_map/ppermute | solution.py:54
  3.5 2.6 %arrange.1 = (bf16[4,8,1536]{2,1,0:T(8,128)(2,1)S(1)}, f32[1,96]{1,0:T(1,128)S(1)}, f32[1,192]{1,0:T(1,128)S(1)}, bf16[128,192]{1,0:T(8,128)(2,1)S(1)}, bf16[3,3...) custom-call(bf16[4,8,1536]{2,1,0:T(8,128)(2,1)} %x.1, ...), custom_call_target="tpu_custom_call" | custom-call | bytes 5000000 | tf_op jit(solution)/shard_map/arrange/pallas_call | solution.py:468
  6.2 0.0 collective-permute-done.refs_0_
  6.2 0.0 collective-permute-done.2.refs_2_
  6.2 0.0 collective-permute-done.1.refs_1_
  6.2 0.1 rows_out.1
  6.3 1.6 %collective-permute-start.3 = (bf16[24,1536]{1,0:T(8,128)(2,1)S(1)}, bf16[24,1536]{1,0:T(8,128)(2,1)S(1)}, u32[]{:S(2)}, u32[]{:S(2)}) collective-permute-start(bf16[24,1536]{1,0:T(8,128)(2,1)S(1)} %get-tuple-element.30), channel_id=1, source_target_pairs={{0,4},{1,5},{2,6},{3,7},{4,0},{5,1},{6,2},{7,3},{8,12},{9,13},{10,... | collective-permute-start | bytes 221192 | tf_op jit(solution)/shard_map/ppermute | solution.py:54
  7.9 2.9 %early.1 = (f32[16,120,128]{2,1,0:T(8,128)S(1)}, f32[16,72,128]{2,1,0:T(8,128)S(1)}, f32[14,120,128]{2,1,0:T(8,128)S(1)}, f32[14,120,128]{2,1,0:T(8,128)S(1)}) custom-call(bf16[4,8,1536]{2,1,0:T(8,128)(2,1)S(1)} %get-tuple-element.28.own, bf16[4,8,1536]{2,1,0:T(8,128)(2,1)S(1)} %get-tuple-element.29.prev, f32[1,96]{1,0:T(1,128)S(1)} %get-tuple-element.37.g1, ...), custom_call_target="tpu_custom_call" | custom-call | flops 1000000000 | bytes 5000000 | tf_op jit(solution)/shard_map/early/pallas_call | solution.py:511
  10.9 0.0 collective-permute-done.3.refs_0_
  10.9 0.1 cols_out.1
  11.0 0.8 %collective-permute-start.4 = (bf16[112,384]{1,0:T(8,128)(2,1)S(1)}, bf16[112,384]{1,0:T(8,128)(2,1)S(1)}, u32[]{:S(2)}, u32[]{:S(2)}) collective-permute-start(bf16[112,384]{1,0:T(8,128)(2,1)S(1)} %get-tuple-element.31), channel_id=1, source_target_pairs={{0,3},{1,2},{2,1},{3,0},{4,7},{5,6},{6,5},{7,4},{8,11},{9,10},{10,... | collective-permute-start | bytes 258056 | tf_op jit(solution)/shard_map/ppermute | solution.py:54
  11.8 0.9 %collective-permute-start.5 = (bf16[112,384]{1,0:T(8,128)(2,1)S(1)}, bf16[112,384]{1,0:T(8,128)(2,1)S(1)}, u32[]{:S(2)}, u32[]{:S(2)}) collective-permute-start(bf16[112,384]{1,0:T(8,128)(2,1)S(1)} %get-tuple-element.32), channel_id=1, source_target_pairs={{0,1},{1,0},{2,3},{3,2},{4,5},{5,4},{6,7},{7,6},{8,9},{9,8},{10,11... | collective-permute-start | bytes 258056 | tf_op jit(solution)/shard_map/ppermute | solution.py:54
  12.7 4.0 %inner.1 = (f32[16,120,128]{2,1,0:T(8,128)S(1)}, f32[16,72,128]{2,1,0:T(8,128)S(1)}, f32[14,120,128]{2,1,0:T(8,128)S(1)}, f32[14,120,128]{2,1,0:T(8,128)S(1)}, b...) custom-call(bf16[48,1536]{1,0:T(8,128)(2,1)S(1)} %get-tuple-element., ...), custom_call_target="tpu_custom_call", output_to_operand_aliasing={{0}: (7, {}), {1}: (8, {}), {2}: (9, {}), {3}: (10, {})} | custom-call | flops 4000000000 | bytes 5000000 | tf_op jit(solution)/shard_map/inner/pallas_call | solution.py:533
  16.6 0.0 collective-permute-done.4.got_b
  16.7 0.0 collective-permute-done.5.got_a
  16.7 3.7 %outer.1 = bf16[4,4,1536]{2,1,0:T(4,128)(2,1)} custom-call(bf16[112,384]{1,0:T(8,128)(2,1)S(1)} %collective-permute-done.4.got_b, bf16[112,384]{1,0:T(8,128)(2,1)S(1)} %collective-permute-done.5.got_a, bf16[3,3,3,128,192]{4,3,2,1,0:T(8,128)(2,1)S(1)} %get-tuple-element.33.w1, bf16[3,3,3,128,192]{4,3,2,1,0:T(8,128)(2,1)S(1)} %get-tuple-element.34.w2m, ...), custom_call_target="tpu_custom_call" | custom-call | flops 2000000000 | bytes 5000000 | tf_op jit(solution)/shard_map/outer/pallas_call | solution.py:556
Async XLA Ops:
  0.0 6.2 %collective-permute-start = (bf16[4,8,1536]{2,1,0:T(8,128)(2,1)}, bf16[4,8,1536]{2,1,0:T(8,128)(2,1)S(1)}, u32[]{:S(2)}, u32[]{:S(2)}) collective-permute-start(bf16[4,8,1536]{2,1,0:T(8,128)(2,1)} %x.1), channel_id=1, source_target_pairs={{0,8},{1,9},{2,10},{3,11},{4,12},{5,13},{6,14},{7,15},{8,0},{9,1},... | collective-permute-start | bytes 294920 | tf_op jit(solution)/shard_map/ppermute | solution.py:54
  3.0 3.1 %collective-permute-start.2 = (bf16[4,8,1536]{2,1,0:T(8,128)(2,1)}, bf16[4,8,1536]{2,1,0:T(8,128)(2,1)S(1)}, u32[]{:S(2)}, u32[]{:S(2)}) collective-permute-start(bf16[4,8,1536]{2,1,0:T(8,128)(2,1)} %x.1), channel_id=1, source_target_pairs={{0,1},{1,0},{2,3},{3,2},{4,5},{5,4},{6,7},{7,6},{8,16},{9,17},{10,... | collective-permute-start | bytes 294920 | tf_op jit(solution)/shard_map/ppermute | solution.py:54
  3.0 3.2 %collective-permute-start.1 = (bf16[4,8,1536]{2,1,0:T(8,128)(2,1)}, bf16[4,8,1536]{2,1,0:T(8,128)(2,1)S(1)}, u32[]{:S(2)}, u32[]{:S(2)}) collective-permute-start(bf16[4,8,1536]{2,1,0:T(8,128)(2,1)} %x.1), channel_id=1, source_target_pairs={{0,1},{1,0},{2,3},{3,2},{4,5},{5,4},{6,7},{7,6},{8,9},{9,8},{10,11... | collective-permute-start | bytes 294920 | tf_op jit(solution)/shard_map/ppermute | solution.py:54
  6.3 4.6 %collective-permute-start.3 = (bf16[24,1536]{1,0:T(8,128)(2,1)S(1)}, bf16[24,1536]{1,0:T(8,128)(2,1)S(1)}, u32[]{:S(2)}, u32[]{:S(2)}) collective-permute-start(bf16[24,1536]{1,0:T(8,128)(2,1)S(1)} %get-tuple-element.30), channel_id=1, source_target_pairs={{0,4},{1,5},{2,6},{3,7},{4,0},{5,1},{6,2},{7,3},{8,12},{9,13},{10,... | collective-permute-start | bytes 221192 | tf_op jit(solution)/shard_map/ppermute | solution.py:54
  11.0 5.7 %collective-permute-start.4 = (bf16[112,384]{1,0:T(8,128)(2,1)S(1)}, bf16[112,384]{1,0:T(8,128)(2,1)S(1)}, u32[]{:S(2)}, u32[]{:S(2)}) collective-permute-start(bf16[112,384]{1,0:T(8,128)(2,1)S(1)} %get-tuple-element.31), channel_id=1, source_target_pairs={{0,3},{1,2},{2,1},{3,0},{4,7},{5,6},{6,5},{7,4},{8,11},{9,10},{10,... | collective-permute-start | bytes 258056 | tf_op jit(solution)/shard_map/ppermute | solution.py:54
  11.8 4.9 %collective-permute-start.5 = (bf16[112,384]{1,0:T(8,128)(2,1)S(1)}, bf16[112,384]{1,0:T(8,128)(2,1)S(1)}, u32[]{:S(2)}, u32[]{:S(2)}) collective-permute-start(bf16[112,384]{1,0:T(8,128)(2,1)S(1)} %get-tuple-element.32), channel_id=1, source_target_pairs={{0,1},{1,0},{2,3},{3,2},{4,5},{5,4},{6,7},{7,6},{8,9},{9,8},{10,11... | collective-permute-start | bytes 258056 | tf_op jit(solution)/shard_map/ppermute | solution.py:54

commit v10 on v9

--- a/solution.py
+++ b/solution.py
@@ -372,7 +372,7 @@
     for i, c in enumerate(edge):
         s.stack_first(c, first, stack1, i)
     merged = list(range(LOW, s.cols - 2))
-    step = 3
+    step = 4
     for start in range(0, len(merged), step):
         wanted = merged[start : start + step]
         acc = s.conv_second(

time: 20.5 us -> 20.5 us (level)
  no operation moved by 1% of the time
where the time goes in v10:
time: 20.5 us; the launch traced here: 20.3 us
  Pallas kernels  13.4 us (65%)
  starting transfers between devices  6.88 us (34%)
    ppermute x6, starting transfers between devices, swap(): lax.ppermute(value, AXES, swap_pairs(axis, i))  6.88 us
    pallas_call x1, Pallas kernels, local(): pl.pallas_call(functools.partial(inner, dims), out_shape=worked + [pltpu....  3.97 us
    pallas_call x1, Pallas kernels, local(): pl.pallas_call(functools.partial(outer, dims), out_shape=jax.ShapeDtypeSt...  3.69 us
    pallas_call x1, Pallas kernels, local(): pl.pallas_call(functools.partial(early, dims), out_shape=worked, in_specs...  2.91 us
    pallas_call x1, Pallas kernels, local(): pl.pallas_call(functools.partial(arrange, c1), out_shape=[pltpu.VMEM(vide...  2.61 us
  transfers between devices with their start and end apart: 6, of which 0 were waited for; matrix products, arithmetic and copies ran while one was open for 0% of the time, Pallas kernels for 47%

profile of v10, /device:TPU:0, one launch (start us, length us, event | category | flops | bytes accessed | tf_op | source)
XLA Modules:
  0.0 20.3 jit_solution(15760287126719973811)
XLA Ops:
  0.0 3.0 %collective-permute-start = (bf16[4,8,1536]{2,1,0:T(8,128)(2,1)}, bf16[4,8,1536]{2,1,0:T(8,128)(2,1)S(1)}, u32[]{:S(2)}, u32[]{:S(2)}) collective-permute-start(bf16[4,8,1536]{2,1,0:T(8,128)(2,1)} %x.1), channel_id=1, source_target_pairs={{0,8},{1,9},{2,10},{3,11},{4,12},{5,13},{6,14},{7,15},{8,0},{9,1},... | collective-permute-start | bytes 294920 | tf_op jit(solution)/shard_map/ppermute | solution.py:54
  3.0 0.0 collective-permute-start.2
  3.0 0.5 %collective-permute-start.1 = (bf16[4,8,1536]{2,1,0:T(8,128)(2,1)}, bf16[4,8,1536]{2,1,0:T(8,128)(2,1)S(1)}, u32[]{:S(2)}, u32[]{:S(2)}) collective-permute-start(bf16[4,8,1536]{2,1,0:T(8,128)(2,1)} %x.1), channel_id=1, source_target_pairs={{0,1},{1,0},{2,3},{3,2},{4,5},{5,4},{6,7},{7,6},{8,9},{9,8},{10,11... | collective-permute-start | bytes 294920 | tf_op jit(solution)/shard_map/ppermute | solution.py:54
  3.5 2.6 %arrange.1 = (bf16[4,8,1536]{2,1,0:T(8,128)(2,1)S(1)}, f32[1,96]{1,0:T(1,128)S(1)}, f32[1,192]{1,0:T(1,128)S(1)}, bf16[128,192]{1,0:T(8,128)(2,1)S(1)}, bf16[3,3...) custom-call(bf16[4,8,1536]{2,1,0:T(8,128)(2,1)} %x.1, ...), custom_call_target="tpu_custom_call" | custom-call | bytes 5000000 | tf_op jit(solution)/shard_map/arrange/pallas_call | solution.py:468
  6.2 0.0 collective-permute-done.refs_0_
  6.2 0.0 collective-permute-done.2.refs_2_
  6.2 0.0 collective-permute-done.1.refs_1_
  6.2 0.1 rows_out.1
  6.3 1.6 %collective-permute-start.3 = (bf16[24,1536]{1,0:T(8,128)(2,1)S(1)}, bf16[24,1536]{1,0:T(8,128)(2,1)S(1)}, u32[]{:S(2)}, u32[]{:S(2)}) collective-permute-start(bf16[24,1536]{1,0:T(8,128)(2,1)S(1)} %get-tuple-element.30), channel_id=1, source_target_pairs={{0,4},{1,5},{2,6},{3,7},{4,0},{5,1},{6,2},{7,3},{8,12},{9,13},{10,... | collective-permute-start | bytes 221192 | tf_op jit(solution)/shard_map/ppermute | solution.py:54
  7.9 2.9 %early.1 = (f32[16,120,128]{2,1,0:T(8,128)S(1)}, f32[16,72,128]{2,1,0:T(8,128)S(1)}, f32[14,120,128]{2,1,0:T(8,128)S(1)}, f32[14,120,128]{2,1,0:T(8,128)S(1)}) custom-call(bf16[4,8,1536]{2,1,0:T(8,128)(2,1)S(1)} %get-tuple-element.28.own, bf16[4,8,1536]{2,1,0:T(8,128)(2,1)S(1)} %get-tuple-element.29.prev, f32[1,96]{1,0:T(1,128)S(1)} %get-tuple-element.37.g1, ...), custom_call_target="tpu_custom_call" | custom-call | flops 1000000000 | bytes 5000000 | tf_op jit(solution)/shard_map/early/pallas_call | solution.py:511
  10.9 0.0 collective-permute-done.3.refs_0_
  10.9 0.1 cols_out.1
  11.0 0.8 %collective-permute-start.4 = (bf16[112,384]{1,0:T(8,128)(2,1)S(1)}, bf16[112,384]{1,0:T(8,128)(2,1)S(1)}, u32[]{:S(2)}, u32[]{:S(2)}) collective-permute-start(bf16[112,384]{1,0:T(8,128)(2,1)S(1)} %get-tuple-element.31), channel_id=1, source_target_pairs={{0,3},{1,2},{2,1},{3,0},{4,7},{5,6},{6,5},{7,4},{8,11},{9,10},{10,... | collective-permute-start | bytes 258056 | tf_op jit(solution)/shard_map/ppermute | solution.py:54
  11.8 0.9 %collective-permute-start.5 = (bf16[112,384]{1,0:T(8,128)(2,1)S(1)}, bf16[112,384]{1,0:T(8,128)(2,1)S(1)}, u32[]{:S(2)}, u32[]{:S(2)}) collective-permute-start(bf16[112,384]{1,0:T(8,128)(2,1)S(1)} %get-tuple-element.32), channel_id=1, source_target_pairs={{0,1},{1,0},{2,3},{3,2},{4,5},{5,4},{6,7},{7,6},{8,9},{9,8},{10,11... | collective-permute-start | bytes 258056 | tf_op jit(solution)/shard_map/ppermute | solution.py:54
  12.7 4.0 %inner.1 = (f32[16,120,128]{2,1,0:T(8,128)S(1)}, f32[16,72,128]{2,1,0:T(8,128)S(1)}, f32[14,120,128]{2,1,0:T(8,128)S(1)}, f32[14,120,128]{2,1,0:T(8,128)S(1)}, b...) custom-call(bf16[48,1536]{1,0:T(8,128)(2,1)S(1)} %get-tuple-element., ...), custom_call_target="tpu_custom_call", output_to_operand_aliasing={{0}: (7, {}), {1}: (8, {}), {2}: (9, {}), {3}: (10, {})} | custom-call | flops 4000000000 | bytes 5000000 | tf_op jit(solution)/shard_map/inner/pallas_call | solution.py:533
  16.6 0.0 collective-permute-done.4.got_b
  16.6 0.0 collective-permute-done.5.got_a
  16.7 3.7 %outer.1 = bf16[4,4,1536]{2,1,0:T(4,128)(2,1)} custom-call(bf16[112,384]{1,0:T(8,128)(2,1)S(1)} %collective-permute-done.4.got_b, bf16[112,384]{1,0:T(8,128)(2,1)S(1)} %collective-permute-done.5.got_a, bf16[3,3,3,128,192]{4,3,2,1,0:T(8,128)(2,1)S(1)} %get-tuple-element.33.w1, bf16[3,3,3,128,192]{4,3,2,1,0:T(8,128)(2,1)S(1)} %get-tuple-element.34.w2m, ...), custom_call_target="tpu_custom_call" | custom-call | flops 2000000000 | bytes 5000000 | tf_op jit(solution)/shard_map/outer/pallas_call | solution.py:556
Async XLA Ops:
  0.0 6.2 %collective-permute-start = (bf16[4,8,1536]{2,1,0:T(8,128)(2,1)}, bf16[4,8,1536]{2,1,0:T(8,128)(2,1)S(1)}, u32[]{:S(2)}, u32[]{:S(2)}) collective-permute-start(bf16[4,8,1536]{2,1,0:T(8,128)(2,1)} %x.1), channel_id=1, source_target_pairs={{0,8},{1,9},{2,10},{3,11},{4,12},{5,13},{6,14},{7,15},{8,0},{9,1},... | collective-permute-start | bytes 294920 | tf_op jit(solution)/shard_map/ppermute | solution.py:54
  3.0 3.1 %collective-permute-start.2 = (bf16[4,8,1536]{2,1,0:T(8,128)(2,1)}, bf16[4,8,1536]{2,1,0:T(8,128)(2,1)S(1)}, u32[]{:S(2)}, u32[]{:S(2)}) collective-permute-start(bf16[4,8,1536]{2,1,0:T(8,128)(2,1)} %x.1), channel_id=1, source_target_pairs={{0,1},{1,0},{2,3},{3,2},{4,5},{5,4},{6,7},{7,6},{8,16},{9,17},{10,... | collective-permute-start | bytes 294920 | tf_op jit(solution)/shard_map/ppermute | solution.py:54
  3.0 3.2 %collective-permute-start.1 = (bf16[4,8,1536]{2,1,0:T(8,128)(2,1)}, bf16[4,8,1536]{2,1,0:T(8,128)(2,1)S(1)}, u32[]{:S(2)}, u32[]{:S(2)}) collective-permute-start(bf16[4,8,1536]{2,1,0:T(8,128)(2,1)} %x.1), channel_id=1, source_target_pairs={{0,1},{1,0},{2,3},{3,2},{4,5},{5,4},{6,7},{7,6},{8,9},{9,8},{10,11... | collective-permute-start | bytes 294920 | tf_op jit(solution)/shard_map/ppermute | solution.py:54
  6.3 4.6 %collective-permute-start.3 = (bf16[24,1536]{1,0:T(8,128)(2,1)S(1)}, bf16[24,1536]{1,0:T(8,128)(2,1)S(1)}, u32[]{:S(2)}, u32[]{:S(2)}) collective-permute-start(bf16[24,1536]{1,0:T(8,128)(2,1)S(1)} %get-tuple-element.30), channel_id=1, source_target_pairs={{0,4},{1,5},{2,6},{3,7},{4,0},{5,1},{6,2},{7,3},{8,12},{9,13},{10,... | collective-permute-start | bytes 221192 | tf_op jit(solution)/shard_map/ppermute | solution.py:54
  11.0 5.7 %collective-permute-start.4 = (bf16[112,384]{1,0:T(8,128)(2,1)S(1)}, bf16[112,384]{1,0:T(8,128)(2,1)S(1)}, u32[]{:S(2)}, u32[]{:S(2)}) collective-permute-start(bf16[112,384]{1,0:T(8,128)(2,1)S(1)} %get-tuple-element.31), channel_id=1, source_target_pairs={{0,3},{1,2},{2,1},{3,0},{4,7},{5,6},{6,5},{7,4},{8,11},{9,10},{10,... | collective-permute-start | bytes 258056 | tf_op jit(solution)/shard_map/ppermute | solution.py:54
  11.8 4.9 %collective-permute-start.5 = (bf16[112,384]{1,0:T(8,128)(2,1)S(1)}, bf16[112,384]{1,0:T(8,128)(2,1)S(1)}, u32[]{:S(2)}, u32[]{:S(2)}) collective-permute-start(bf16[112,384]{1,0:T(8,128)(2,1)S(1)} %get-tuple-element.32), channel_id=1, source_target_pairs={{0,1},{1,0},{2,3},{3,2},{4,5},{5,4},{6,7},{7,6},{8,9},{9,8},{10,11... | collective-permute-start | bytes 258056 | tf_op jit(solution)/shard_map/ppermute | solution.py:54
